TPU v7x, 32 devices: a whole 2x2x4 slice. The times are simulated.
32 devices in a mesh: seq: 8 (over y, x, core), section: 4 (over z).
Axes of the slice: x: 2, y: 2, z: 4, core: 2. Of those that a mesh axis runs over, the one named last changes fastest.
Arguments:
- tokens: bfloat16 [4096, 1024], P('seq'), may hold values from -6 to 6
- input_gain: float32 [4, 1024], P('section'), may hold values from 0.5 to 2
- main_weight: bfloat16 [4, 1024, 4096], P('section'), may hold values from -0.1875 to 0.1875
- side_weight: bfloat16 [4, 1024, 288], P('section'), may hold values from -0.1875 to 0.1875
- conv_kernel: float32 [4, 4, 2304], P('section'), may hold values from -3 to 3
- step_bias: float32 [4, 32], P('section'), may hold values from -4 to 1
- decay_rate: float32 [4, 32], P('section'), may hold values from 0.0001 to 0.04, as said below
- skip_gain: float32 [4, 32], P('section'), may hold values from 1 to 4
- output_gain: float32 [4, 2048], P('section'), may hold values from 0.5 to 2
- output_weight: bfloat16 [4, 2048, 1024], P('section', 'seq'), may hold values from -0.09375 to 0.09375
Outputs:
- layer_outputs: bfloat16 [4, 4096, 1024], P('section', 'seq')
Inputs may be any that keep to these rules, and one draw needn't show every extreme that they name: `decay_rate`: positive.
All inputs are finite; a program needn't handle non-finite values.
Results may differ from a plain program's by a relative error of at most 0.0074.
Values may be sent and summed in bfloat16 or wider, within the bound.
No kernel may reach another device: no remote copies, remote signals or barrier semaphores. Data moves between devices by JAX's collectives and lax.ppermute only.
A program may use at most 128 MiB of HBM per device.

v0:
```python
import jax
import jax.numpy as jnp
from jax import lax
from jax.sharding import PartitionSpec as P

BLOCK = 256


EPSILON = 1e-05


def from_partner(value, axis, distance):
    mask = 2**distance
    pairs = [(source, source ^ mask) for source in range(lax.axis_size(axis))]
    return lax.ppermute(value, axis, pairs)


def padded_2(value, sides, width):
    for axis, dim in sides:
        peers, length = (lax.axis_size(axis), value.shape[dim])
        up = [(i, (i + 1) % peers) for i in range(peers - 1)]
        down = [(j, i) for i, j in up]
        last = lax.slice_in_dim(value, length - width, length, axis=dim)
        first = lax.slice_in_dim(value, 0, width, axis=dim)
        before = lax.ppermute(last, axis, up)
        after = lax.ppermute(first, axis, down)
        value = jnp.concatenate([before, value, after], axis=dim)
    return value


def passed_along(block, axis, distance):
    devices = range(lax.axis_size(axis))
    route = [(i - distance, i) for i in devices if i - distance in devices]
    return lax.ppermute(block, axis, route)


def norm_rows(values, gain_row):
    widened = values.astype(jnp.float32)
    inverse_rms = lax.rsqrt(jnp.mean(widened * widened, axis=-1, keepdims=True) + EPSILON)
    return (widened * inverse_rms * gain_row).astype(jnp.bfloat16)


def gate_norm(convolved, gate_in, gain_row):
    gated = convolved * jax.nn.silu(gate_in.astype(jnp.float32))
    inverse_rms = lax.rsqrt(jnp.mean(gated * gated, axis=-1, keepdims=True) + EPSILON)
    return (gated * inverse_rms * gain_row).astype(jnp.bfloat16)


def project(normed, main_weight, side_weight, inner_size, state_size):
    projected = jnp.dot(normed, main_weight, preferred_element_type=jnp.float32).astype(
        jnp.bfloat16
    )
    side_columns = jnp.dot(normed, side_weight, preferred_element_type=jnp.float32).astype(
        jnp.bfloat16
    )
    channel = jnp.concatenate(
        [projected[:, inner_size:], side_columns[:, : 2 * state_size]], axis=1
    )
    return (projected[:, :inner_size], channel, side_columns[:, 2 * state_size :])


def causal_filter(channel, before, kernel):
    length = channel.shape[0]
    padded = jnp.concatenate([before, channel], axis=0).astype(jnp.float32)
    running = kernel[0] * padded[0:length]
    for offset in range(1, kernel.shape[0]):
        running = running + kernel[offset] * padded[offset : offset + length]
    return jax.nn.silu(running).astype(jnp.bfloat16)


def block_group(members, head_count):
    inner_rows, input_coef, output_coef, step_size, log_decay = members
    blocks, length, inner_size = inner_rows.shape
    inner_heads = inner_rows.reshape(blocks, length, head_count, inner_size // head_count)
    cumulative = jnp.cumsum(log_decay, axis=1)
    scores = jnp.einsum("ctn,csn->cts", output_coef, input_coef, preferred_element_type=jnp.float32)
    cum_heads = jnp.transpose(cumulative, (0, 2, 1))
    decay_gap = cum_heads[:, :, :, None] - cum_heads[:, :, None, :]
    position = jnp.arange(length)
    causal = position[:, None] >= position[None, :]
    kept_share = jnp.where(causal, jnp.exp(jnp.minimum(decay_gap, 0.0)), 0.0)
    step_heads = jnp.transpose(step_size, (0, 2, 1))
    weights = (scores[:, None, :, :] * kept_share * step_heads[:, :, None, :]).astype(jnp.bfloat16)
    within = jnp.einsum("chts,cshp->cthp", weights, inner_heads, preferred_element_type=jnp.float32)
    block_end = cumulative[:, -1:, :]
    weighted = (
        inner_heads.astype(jnp.float32) * (jnp.exp(block_end - cumulative) * step_size)[..., None]
    )
    states = jnp.einsum(
        "clhp,cln->chpn", weighted, input_coef.astype(jnp.float32), precision=lax.Precision.HIGHEST
    )
    totals = jnp.exp(block_end[:, 0, :])
    return (within, states, totals, cumulative)


def block_terms(inner_rows, input_coef, output_coef, step_size, log_decay, head_count):
    blocks = inner_rows.shape[0]

    def regroup(values):
        return values.reshape((blocks, 1) + values.shape[1:])

    def group_terms(members):
        return block_group(members, head_count)

    pieces = (
        regroup(inner_rows),
        regroup(input_coef),
        regroup(output_coef),
        regroup(step_size),
        regroup(log_decay),
    )
    results = lax.map(group_terms, pieces)
    return tuple((member.reshape((blocks,) + member.shape[2:]) for member in results))


def carried_terms(output_coef, cumulative, entering):
    product = jnp.einsum(
        "ctn,chpn->cthp", output_coef.astype(jnp.float32), entering, precision=lax.Precision.HIGHEST
    )
    return product * jnp.exp(cumulative)[..., None]


def combine_pair(earlier, latter):
    return (earlier[0] * latter[0], latter[0][:, None, None] * earlier[1] + latter[1])


def select_pair(condition, first, second):
    return jax.tree.map(lambda left, right: jnp.where(condition, left, right), first, second)


def run_when(active, action, *operands):

    def silent(*values):
        return jax.tree.map(jnp.zeros_like, action(*values))

    return lax.cond(active, action, silent, *operands)


def direction_start(
    channel, before, raw_step, kernel, step_shift, decay, inner_size, state_size, head_count
):
    convolved = causal_filter(channel, before, kernel)
    step_size = jax.nn.softplus(raw_step.astype(jnp.float32) + step_shift)
    log_decay = -step_size * decay
    blocks = channel.shape[0] // BLOCK
    inner_rows = convolved[:, :inner_size].reshape(blocks, BLOCK, inner_size)
    input_coef = convolved[:, inner_size : inner_size + state_size].reshape(
        blocks, BLOCK, state_size
    )
    output_coef = convolved[:, inner_size + state_size :].reshape(blocks, BLOCK, state_size)
    within, states, totals, cumulative = block_terms(
        inner_rows,
        input_coef,
        output_coef,
        step_size.reshape(blocks, BLOCK, head_count),
        log_decay.reshape(blocks, BLOCK, head_count),
        head_count,
    )
    through = jnp.ones((head_count,), jnp.float32)
    carried = jnp.zeros(states.shape[1:], jnp.float32)
    for block_index in range(blocks):
        carried = totals[block_index][:, None, None] * carried + states[block_index]
        through = through * totals[block_index]
    return ((convolved, output_coef, within, states, totals, cumulative), (through, carried))


def direction_finish(pieces, entering, gate_in, skip_row, gain_row, head_count):
    convolved, output_coef, within, states, totals, cumulative = pieces
    blocks = totals.shape[0]
    starts = []
    current = entering
    for block_index in range(blocks):
        starts.append(current)
        current = totals[block_index][:, None, None] * current + states[block_index]
    starting = jnp.stack(starts)
    length = convolved.shape[0]
    inner_size = gate_in.shape[1]
    head_dim = inner_size // head_count
    inner_heads = (
        convolved[:, :inner_size].astype(jnp.float32).reshape(length, head_count, head_dim)
    )
    output = within + carried_terms(output_coef, cumulative, starting)
    combined = output.reshape(length, head_count, head_dim) + inner_heads * skip_row[None, :, None]
    return gate_norm(combined.reshape(length, inner_size), gate_in, gain_row)


def per_device(
    tokens,
    input_gain,
    main_weight,
    side_weight,
    conv_kernel,
    step_bias,
    decay_rate,
    skip_gain,
    output_gain,
    output_weight,
):
    gain_in = input_gain[0]
    main_proj = main_weight[0]
    side_proj = side_weight[0]
    kernel = conv_kernel[0]
    shift_row = step_bias[0]
    decay_row = decay_rate[0]
    skip_row = skip_gain[0]
    gain_out = output_gain[0]
    out_proj = lax.all_gather(output_weight[0], "seq", axis=0, tiled=True)
    inner_size = out_proj.shape[0]
    head_count = decay_row.shape[-1]
    state_size = (side_proj.shape[1] - head_count) // 2
    head_dim = inner_size // head_count
    margin = kernel.shape[0] - 1
    identity_pair = (
        jnp.ones((head_count,), jnp.float32),
        jnp.zeros((head_count, head_dim, state_size), jnp.float32),
    )
    section_index = lax.axis_index("section")
    reverse_side = section_index % 2 == 1
    layer_here = section_index // 2
    seq_index = lax.axis_index("seq")
    seq_count = lax.axis_size("seq")

    def orient(values):
        return jnp.where(reverse_side, jnp.flip(values, 0), values)

    def prepare(rows_in):
        return project(norm_rows(rows_in, gain_in), main_proj, side_proj, inner_size, state_size)

    rounds = lax.axis_size("section") // 2
    current = tokens
    finished = jnp.zeros_like(tokens)
    for round_index in range(rounds):
        active = layer_here == round_index
        gate_in, channel, raw_step = run_when(active, prepare, current)
        padded = padded_2(channel, (("seq", 0),), margin)
        before = jnp.where(
            reverse_side, jnp.flip(padded[padded.shape[0] - margin :], 0), padded[:margin]
        )

        def begin(channel, raw_step, before):
            return direction_start(
                orient(channel),
                before,
                orient(raw_step),
                kernel,
                shift_row,
                decay_row,
                inner_size,
                state_size,
                head_count,
            )

        pieces, apply_summary = run_when(active, begin, channel, raw_step, before)
        earlier_part = identity_pair
        group_total = apply_summary
        for bit in range(seq_count.bit_length() - 1):
            received = from_partner(group_total, "seq", bit)
            upper = seq_index // 2**bit % 2 == 1
            partner_first = jnp.logical_xor(upper, reverse_side)
            earlier_part = select_pair(
                partner_first, combine_pair(received, earlier_part), earlier_part
            )
            group_total = select_pair(
                partner_first,
                combine_pair(received, group_total),
                combine_pair(group_total, received),
            )
        entering = earlier_part[1]

        def finish(pieces, entering, gate_in):
            normed_out = orient(
                direction_finish(pieces, entering, orient(gate_in), skip_row, gain_out, head_count)
            )
            return jnp.dot(normed_out, out_proj, preferred_element_type=jnp.float32)

        own_term = run_when(active, finish, pieces, entering, gate_in)
        other_term = from_partner(own_term, "section", 0)
        layer_rows = (current.astype(jnp.float32) + (own_term + other_term)).astype(jnp.bfloat16)
        finished = jnp.where(active, layer_rows, finished)
        if round_index + 1 < rounds:
            current = passed_along(layer_rows, "section", 2)
    return finished[None]


def solution(mesh):
    placed = (
        P("seq", None),
        P("section", None),
        P("section", None, None),
        P("section", None, None),
        P("section", None, None),
        P("section", None),
        P("section", None),
        P("section", None),
        P("section", None),
        P("section", "seq", None),
    )
    return jax.shard_map(
        per_device, mesh=mesh, in_specs=placed, out_specs=P("section", "seq", None), check_vma=False
    )
```

profile of v0, /device:TPU:20, one launch (start us, length us, event | category | flops | bytes accessed | tf_op | source)
XLA Modules:
  0.0 629.0 jit_solution(10123401352851684105)
XLA Ops:
  7.3 2.3 copy.77
  9.6 2.5 conditional.6
  12.1 2.8 collective-permute-start
  14.8 1.9 collective-permute-start.1
  17.3 3.6 collective-permute-done.1
  20.9 7.4 %conditional.7 = (bf16[512,2304]{1,0:T(8,128)(2,1)}, bf16[2,256,128]{2,1,0:T(8,128)(2,1)S(1)}, f32[2,256,32,64]{1,3,2,0:T(8,128)}, f32[2,32,64,128]{3,2,1,0:T(8,...) conditional(s32[]{:T(128)} %convert_element_type.125, () %tuple.66, ...), branch_computations={%region_3.4_spmd, %region_4.9_spmd} | conditional | flops 1126344704 | bytes 69833264 | solution.py:136
  25.4 2.5 broadcast.281
  29.5 2.1 collective-permute-done.2
  33.3 2.0 collective-permute-start.3
  35.3 32.6 %collective-permute-done.3 = f32[32]{0:T(128)S(1)} collective-permute-done((f32[32]{0:T(128)S(1)}, f32[32]{0:T(128)S(1)}, u32[]{:S(2)}, u32[]{:S(2)}) %collective-permute-start.3) | collective-permute-done | bytes 160 | tf_op jit(solution)/shard_map/ppermute | solution.py:15
  69.2 25.0 %collective-permute-done.6 = f32[32,64,128]{2,1,0:T(8,128)S(1)} collective-permute-done((f32[32,64,128]{2,1,0:T(8,128)}, f32[32,64,128]{2,1,0:T(8,128)S(1)}, u32[]{:S(2)}, u32[]{:S(2)}) %collective-permute-start.6) | collective-permute-done | bytes 1048608 | tf_op jit(solution)/shard_map/ppermute | solution.py:15
  95.4 1.8 conditional.8
  98.7 45.1 %collective-permute-done.7 = f32[512,1024]{1,0:T(8,128)S(1)} collective-permute-done((f32[512,1024]{1,0:T(8,128)}, f32[512,1024]{1,0:T(8,128)S(1)}, u32[]{:S(2)}, u32[]{:S(2)}) %collective-permute-start.7) | collective-permute-done | bytes 2097184 | tf_op jit(solution)/shard_map/ppermute | solution.py:15
  143.8 2.5 add_convert_fusion.1
  147.6 153.9 %collective-permute-done.8 = bf16[512,1024]{1,0:T(8,128)(2,1)S(1)} collective-permute-done((bf16[512,1024]{1,0:T(8,128)(2,1)S(1)}, bf16[512,1024]{1,0:T(8,128)(2,1)S(1)}, u32[]{:S(2)}, u32[]{:S(2)}) %collective-permute-start.8) | collective-permute-done | bytes 1048608 | tf_op jit(solution)/shard_map/ppermute | solution.py:34
  302.5 12.6 %conditional.9 = (bf16[512,2048]{1,0:T(8,128)(2,1)}, bf16[512,2304]{1,0:T(8,128)(2,1)S(1)}, bf16[512,32]{1,0:T(8,128)(2,1)S(1)}) conditional(s32[]{:T(128)} %convert_element_type.128, () %tuple.73, (bf16[512,1024]{1,0:T(8,128)(2,1)S(1)}, f32[1,1024]{1,0:T(1,128)S(1)}, bf16[1024,4096]{1,0:T(8,128)(2,1)}, bf16[1024,288]{1,0:T(8,128)(2,1)}) %tuple.191), branch_computations={%region_12.13_spmd, %region_13.15_spmd} | conditional | flops 4609688064 | bytes 30328856 | solution.py:136
  302.9 1.9 convolution_convert_fusion.3
  304.9 8.3 %convolution_convert_fusion.2 = bf16[512,4096]{1,0:T(8,128)(2,1)S(1)} fusion(bf16[1024,4096]{1,0:T(8,128)(2,1)} %get-tuple-element.480, bf16[512,1024]{1,0:T(8,128)(2,1)S(1)} %get-tuple-element.478, f32[1024]{0:T(1024)S(1)} %bitcast.382, f32[512]{0:T(512)S(1)} %add_rsqrt_fusion.2), kind=kOutput, calls=%fused_computation.35 | convolution fusion | flops 4299161600 | bytes 13637632 | tf_op jit(solution)/shard_map/cond/branch_1_fun/dot_general | solution.py:50
  315.7 1.9 collective-permute-start.9
  317.6 2.4 collective-permute-start.10
  320.0 8.2 %rev.43 = bf16[3,2304]{1,0:T(4,128)(2,1)} reverse(bf16[3,2304]{1,0:T(4,128)(2,1)} %collective-permute-done.9), dimensions={0} | reverse | bytes 27648 | tf_op jit(solution)/shard_map/jit(_flip)/rev | solution.py:237
  328.3 87.1 %conditional.10 = (bf16[512,2304]{1,0:T(8,128)(2,1)}, bf16[2,256,128]{2,1,0:T(8,128)(2,1)}, f32[2,256,32,64]{1,3,2,0:T(8,128)}, f32[2,32,64,128]{3,2,1,0:T(8,128...) conditional(s32[]{:T(128)} %convert_element_type.128, () %tuple.72, ...), branch_computations={%region_15.16_spmd, %region_16.21_spmd} | conditional | flops 1126344704 | bytes 69214416 | solution.py:136
  330.3 2.7 rev.37
  336.9 23.0 %rev.36 = bf16[512,2304]{1,0:T(8,128)(2,1)} reverse(bf16[512,2304]{1,0:T(8,128)(2,1)S(1)} %get-tuple-element.497), dimensions={0} | reverse | bytes 4718592 | tf_op jit(solution)/shard_map/cond/branch_1_fun/jit(_flip)/rev | solution.py:224
  361.4 3.9 multiply_convert_fusion.11
  367.0 3.2 slice.216
  370.2 40.5 %while.31 = (s32[]{:T(128)}, f32[2,1,256,32,64]{2,4,3,1,0:T(8,128)}, f32[2,1,32,64,128]{4,3,2,1,0:T(8,128)}, f32[2,1,32]{1,0,2:T(2,128)}, f32[2,1,256,32]{2,0,3,...) while((s32[]{:T(128)}, ...), condition=%wide.region_20.20_spmd, body=%wide.region_17.19_spmd.sunk | while | flops 1105289344 | bytes 20288892 | solution.py:112
  384.2 2.1 fusion.122
  386.2 4.2 bitcast_dynamic-update-slice_fusion.4
  404.4 2.1 fusion.122
  406.5 4.2 bitcast_dynamic-update-slice_fusion.4
  416.5 2.2 collective-permute-done.11
  421.0 23.5 %collective-permute-done.12 = f32[32]{0:T(128)S(1)} collective-permute-done((f32[32]{0:T(128)S(1)}, f32[32]{0:T(128)S(1)}, u32[]{:S(2)}, u32[]{:S(2)}) %collective-permute-start.12) | collective-permute-done | bytes 160 | tf_op jit(solution)/shard_map/ppermute | solution.py:15
  445.5 23.9 %collective-permute-done.15 = f32[32,64,128]{2,1,0:T(8,128)} collective-permute-done((f32[32,64,128]{2,1,0:T(8,128)S(1)}, f32[32,64,128]{2,1,0:T(8,128)}, u32[]{:S(2)}, u32[]{:S(2)}) %collective-permute-start.15) | collective-permute-done | bytes 1048608 | tf_op jit(solution)/shard_map/ppermute | solution.py:15
  469.5 77.8 %conditional.11 = (f32[512,1024]{1,0:T(8,128)}) conditional(s32[]{:T(128)} %convert_element_type.128, () %tuple.71, (pred[]{:T(512)}, pred[]{:T(512)}, pred[]{:T(512)}, pred[32]{0:T(512)(128)(4,1)S(1)}, f32[32]{0:T(128)S(1)}, /*index=5*/f32[32]{0:T(128)S(1)}, f32[32]{0:T(128)S(1)}, f32[32,64,128]{2,1,0:T(8,128)}, f32[32,64,128]{2,1,0:T(8,128)S(1)}, ...), branch_computations={%region_21.22_spmd, %region_22.24_spmd} | conditional | flops 3779854848 | bytes 83740072 | solution.py:136
  469.5 3.6 fusion.35
  474.1 5.0 fusion.28
  479.1 3.4 copy.76
  482.5 2.4 copy.97
  484.9 2.9 copy.85
  487.8 22.5 %rev.38 = bf16[512,2048]{0,1:T(8,128)(2,1)} reverse(bf16[512,2048]{0,1:T(8,128)(2,1)S(1)} %copy.85), dimensions={0} | reverse | bytes 4194304 | tf_op jit(solution)/shard_map/cond/branch_1_fun/jit(_flip)/rev | solution.py:224
  510.3 4.3 copy.84
  514.6 3.8 multiply_reduce_fusion.1
  518.9 22.5 %rev.39 = bf16[512,2048]{0,1:T(8,128)(2,1)} reverse(bf16[512,2048]{0,1:T(8,128)(2,1)S(1)} %multiply_convert_fusion.1), dimensions={0} | reverse | bytes 4194304 | tf_op jit(solution)/shard_map/cond/branch_1_fun/jit(_flip)/rev | solution.py:224
  541.4 5.9 fusion.32
  547.3 26.6 %collective-permute-start.16 = (f32[512,1024]{1,0:T(8,128)}, f32[512,1024]{1,0:T(8,128)S(1)}, u32[]{:S(2)}, u32[]{:S(2)}) collective-permute-start(f32[512,1024]{1,0:T(8,128)} %get-tuple-element.1148), channel_id=1, source_target_pairs={{0,1},{1,0},{2,3},{3,2},{4,5},{5,4},{6,7},{7,6},{8,9},{9,8},{10,11... | collective-permute-start | bytes 6291464 | tf_op jit(solution)/shard_map/ppermute | solution.py:15
  573.9 44.6 %collective-permute-done.16 = f32[512,1024]{1,0:T(8,128)S(1)} collective-permute-done((f32[512,1024]{1,0:T(8,128)}, f32[512,1024]{1,0:T(8,128)S(1)}, u32[]{:S(2)}, u32[]{:S(2)}) %collective-permute-start.16) | collective-permute-done | bytes 2097184 | tf_op jit(solution)/shard_map/ppermute | solution.py:15
  618.5 3.5 fusion.83
  (180 shorter events, 68.7 us)
Async XLA Ops:
  6.5 87.6 %all-gather.3.cloned.1.call-start = ((), (), s32[]{:S(2)}) async-start(), calls=%async_computation | async-start | bytes 4718592 | tf_op jit(solution)/shard_map/all_gather | solution.py:207
  9.6 11.4 %copy-start.20 = (f32[1,32]{1,0:T(1,128)S(1)}, f32[1,32]{1,0:T(1,128)}, u32[]{:S(2)}) copy-start(f32[1,32]{1,0:T(1,128)} %param.31) | copy-start | bytes 388
  9.6 11.4 %copy-start.21 = (f32[1,32]{1,0:T(1,128)S(1)}, f32[1,32]{1,0:T(1,128)}, u32[]{:S(2)}) copy-start(f32[1,32]{1,0:T(1,128)} %param.32) | copy-start | bytes 388
  12.1 4.7 collective-permute-start
  14.8 6.1 collective-permute-start.1
  28.4 0.7 copy-start.6
  29.0 2.7 copy-start.29
  29.0 2.7 collective-permute-start.4
  29.0 2.7 collective-permute-start.2
  31.7 0.6 copy-start.23
  32.5 62.9 %copy-start.7 = (bf16[2,256,128]{2,1,0:T(8,128)(2,1)S(1)}, bf16[2,256,128]{2,1,0:T(8,128)(2,1)}, u32[]{:S(2)}) copy-start(bf16[2,256,128]{2,1,0:T(8,128)(2,1)} %copy-done.6) | copy-start | bytes 393220
  32.5 62.9 %copy-start.18 = (f32[1,2048]{1,0:T(1,128)S(1)}, f32[1,2048]{1,0:T(1,128)}, u32[]{:S(2)}) copy-start(f32[1,2048]{1,0:T(1,128)} %param.34) | copy-start | bytes 24580
  32.6 35.3 %collective-permute-start.5 = (f32[32,64,128]{2,1,0:T(8,128)S(1)}, f32[32,64,128]{2,1,0:T(8,128)S(1)}, u32[]{:S(2)}, u32[]{:S(2)}) collective-permute-start(f32[32,64,128]{2,1,0:T(8,128)S(1)} %add_select_fusion.7), channel_id=1, source_target_pairs={{0,8},{4,12},{8,0},{12,4},{16,24},{20,28},{24,16},{28,20},{1,9},{5... | collective-permute-start | bytes 3145736 | tf_op jit(solution)/shard_map/ppermute | solution.py:15
  33.3 34.5 %collective-permute-start.3 = (f32[32]{0:T(128)S(1)}, f32[32]{0:T(128)S(1)}, u32[]{:S(2)}, u32[]{:S(2)}) collective-permute-start(f32[32]{0:T(128)S(1)} %mul.598), channel_id=1, source_target_pairs={{0,8},{4,12},{8,0},{12,4},{16,24},{20,28},{24,16},{28,20},{1,9},{5... | collective-permute-start | bytes 392 | tf_op jit(solution)/shard_map/ppermute | solution.py:15
  67.9 26.8 %copy-start.24 = (f32[32]{0:T(128)}, f32[32]{0:T(128)S(1)}, u32[]{:S(2)}) copy-start(f32[32]{0:T(128)S(1)} %collective-permute-done.3) | copy-start | bytes 388
  67.9 26.8 %copy-start.2 = (f32[32,64,128]{2,1,0:T(8,128)}, f32[32,64,128]{2,1,0:T(8,128)S(1)}, u32[]{:S(2)}) copy-start(f32[32,64,128]{2,1,0:T(8,128)S(1)} %collective-permute-done.5) | copy-start | bytes 3145732
  69.2 25.0 %collective-permute-start.6 = (f32[32,64,128]{2,1,0:T(8,128)}, f32[32,64,128]{2,1,0:T(8,128)S(1)}, u32[]{:S(2)}, u32[]{:S(2)}) collective-permute-start(f32[32,64,128]{2,1,0:T(8,128)} %add_select_fusion.6), channel_id=1, source_target_pairs={{0,16},{4,20},{8,24},{12,28},{16,0},{20,4},{24,8},{28,12},{1,17},{... | collective-permute-start | bytes 3145736 | tf_op jit(solution)/shard_map/ppermute | solution.py:15
  97.2 204.3 %copy-start.30 = (f32[1,1024]{1,0:T(1,128)S(1)}, f32[1,1024]{1,0:T(1,128)}, u32[]{:S(2)}) copy-start(f32[1,1024]{1,0:T(1,128)} %param.27) | copy-start | bytes 12292
  97.2 46.6 %collective-permute-start.7 = (f32[512,1024]{1,0:T(8,128)}, f32[512,1024]{1,0:T(8,128)S(1)}, u32[]{:S(2)}, u32[]{:S(2)}) collective-permute-start(f32[512,1024]{1,0:T(8,128)} %get-tuple-element.1147), channel_id=1, source_target_pairs={{0,1},{1,0},{2,3},{3,2},{4,5},{5,4},{6,7},{7,6},{8,9},{9,8},{10,11... | collective-permute-start | bytes 6291464 | tf_op jit(solution)/shard_map/ppermute | solution.py:15
  146.3 155.2 %copy-start.3 = (bf16[512,1024]{1,0:T(8,128)(2,1)}, bf16[512,1024]{1,0:T(8,128)(2,1)S(1)}, u32[]{:S(2)}) copy-start(bf16[512,1024]{1,0:T(8,128)(2,1)S(1)} %add_convert_fusion.1) | copy-start | bytes 3145732
  146.3 155.2 %collective-permute-start.8 = (bf16[512,1024]{1,0:T(8,128)(2,1)S(1)}, bf16[512,1024]{1,0:T(8,128)(2,1)S(1)}, u32[]{:S(2)}, u32[]{:S(2)}) collective-permute-start(bf16[512,1024]{1,0:T(8,128)(2,1)S(1)} %add_convert_fusion.1), channel_id=1, source_target_pairs={{0,2},{1,3},{4,6},{5,7},{8,10},{9,11},{12,14},{13,15},{16,18},{17,... | collective-permute-start | bytes 3145736 | tf_op jit(solution)/shard_map/ppermute | solution.py:34
  301.5 1.0 copy-start.1
  315.7 4.3 collective-permute-start.9
  317.6 10.7 %collective-permute-start.10 = (bf16[3,2304]{1,0:T(4,128)(2,1)}, bf16[3,2304]{1,0:T(4,128)(2,1)}, u32[]{:S(2)}, u32[]{:S(2)}) collective-permute-start(bf16[3,2304]{1,0:T(4,128)(2,1)} %get-tuple-element.883), channel_id=1, source_target_pairs={{0,4},{4,8},{8,12},{12,16},{16,20},{20,24},{24,28},{1,5},{5,9},{9,... | collective-permute-start | bytes 41480 | tf_op jit(solution)/shard_map/ppermute | solution.py:25
  328.3 4.8 copy-start.22
  359.9 0.7 copy-start.14
  360.6 0.7 copy-start.15
  360.6 0.7 copy-start.16
  360.6 0.7 copy-start.17
  384.2 2.1 copy-start.8
  384.2 2.1 copy-start.10
  384.2 2.1 copy-start.11
  404.4 2.1 copy-start.8
  404.4 2.1 copy-start.10
  404.4 2.1 copy-start.11
  412.1 2.9 copy-start.32
  415.4 3.2 collective-permute-start.13
  416.3 53.1 %copy-start.19 = (f32[1,2048]{1,0:T(1,128)S(1)}, f32[1,2048]{1,0:T(1,128)}, u32[]{:S(2)}) copy-start(f32[1,2048]{1,0:T(1,128)} %param.34) | copy-start | bytes 24580
  416.3 53.1 %copy-start.25 = (f32[1,32]{1,0:T(1,128)S(1)}, f32[1,32]{1,0:T(1,128)}, u32[]{:S(2)}) copy-start(f32[1,32]{1,0:T(1,128)} %param.33) | copy-start | bytes 388
  416.3 53.1 %copy-start.27 = (pred[32]{0:T(512)(128)(4,1)S(1)}, pred[32]{0:T(512)(128)(4,1)}, u32[]{:S(2)}) copy-start(pred[32]{0:T(512)(128)(4,1)} %select_n.285) | copy-start | bytes 100
  416.3 53.1 %copy-start.28 = (f32[32]{0:T(128)S(1)}, f32[32]{0:T(128)}, u32[]{:S(2)}) copy-start(f32[32]{0:T(128)} %broadcast_in_dim.58) | copy-start | bytes 388
  416.3 2.3 collective-permute-start.11
  418.9 25.6 %collective-permute-start.14 = (f32[32,64,128]{2,1,0:T(8,128)S(1)}, f32[32,64,128]{2,1,0:T(8,128)S(1)}, u32[]{:S(2)}, u32[]{:S(2)}) collective-permute-start(f32[32,64,128]{2,1,0:T(8,128)S(1)} %add_select_fusion.5), channel_id=1, source_target_pairs={{0,8},{4,12},{8,0},{12,4},{16,24},{20,28},{24,16},{28,20},{1,9},{5... | collective-permute-start | bytes 3145736 | tf_op jit(solution)/shard_map/ppermute | solution.py:15
  420.3 24.2 %collective-permute-start.12 = (f32[32]{0:T(128)S(1)}, f32[32]{0:T(128)S(1)}, u32[]{:S(2)}, u32[]{:S(2)}) collective-permute-start(f32[32]{0:T(128)S(1)} %mul.607), channel_id=1, source_target_pairs={{0,8},{4,12},{8,0},{12,4},{16,24},{20,28},{24,16},{28,20},{1,9},{5... | collective-permute-start | bytes 392 | tf_op jit(solution)/shard_map/ppermute | solution.py:15
  444.7 24.7 %collective-permute-start.15 = (f32[32,64,128]{2,1,0:T(8,128)S(1)}, f32[32,64,128]{2,1,0:T(8,128)}, u32[]{:S(2)}, u32[]{:S(2)}) collective-permute-start(f32[32,64,128]{2,1,0:T(8,128)S(1)} %add_select_fusion.4), channel_id=1, source_target_pairs={{0,16},{4,20},{8,24},{12,28},{16,0},{20,4},{24,8},{28,12},{1,17},{... | collective-permute-start | bytes 3145736 | tf_op jit(solution)/shard_map/ppermute | solution.py:15
  547.3 71.2 %collective-permute-start.16 = (f32[512,1024]{1,0:T(8,128)}, f32[512,1024]{1,0:T(8,128)S(1)}, u32[]{:S(2)}, u32[]{:S(2)}) collective-permute-start(f32[512,1024]{1,0:T(8,128)} %get-tuple-element.1148), channel_id=1, source_target_pairs={{0,1},{1,0},{2,3},{3,2},{4,5},{5,4},{6,7},{7,6},{8,9},{9,8},{10,11... | collective-permute-start | bytes 6291464 | tf_op jit(solution)/shard_map/ppermute | solution.py:15
Sparse Core Ops, SparseCore 0:
  9.2 47.7 all-gather.2
where the time goes:
time: 637 us; the launch traced here: 629 us
  waiting for transfers between devices  357 us (56%)
  local copies, waits for them, and re-layouts  144 us (23%)
  starting transfers between devices  45 us (7%)
  matrix products  35.6 us (6%)
  other arithmetic  32.3 us (5%)
  between operations  13.9 us (2%)
    ppermute x12, waiting for transfers between devices, from_partner(): return lax.ppermute(value, axis, pairs)  199 us
    ppermute x1, waiting for transfers between devices, passed_along(): return lax.ppermute(block, axis, route)  154 us
    rev x4, local copies, waits for them, and re-layouts, orient(): return jnp.where(reverse_side, jnp.flip(values, 0), values)  70.8 us
    ppermute x12, starting transfers between devices, from_partner(): return lax.ppermute(value, axis, pairs)  34.6 us
    another operation x30, local copies, waits for them, and re-layouts  19.8 us
  transfers between devices with their start and end apart: 18, of which 10 were waited for; matrix products, arithmetic and copies ran while one was open for 4% of the time, Pallas kernels for 0%

commit v1 on v0

v1 whole, which is shorter than its diff:
```python
import functools

import jax
import jax.numpy as jnp
import numpy as np
from jax import lax
from jax.experimental import pallas as pl
from jax.experimental.pallas import tpu as pltpu
from jax.sharding import PartitionSpec as P

EPSILON = 1e-05
CHUNK = 128
WIDTH = 512
HALO = 16
LOG2E = 1.4426950408889634
F32 = jnp.float32
BF16 = jnp.bfloat16


def silu(value):
    half = 0.5 * value
    return half + half * jnp.tanh(half)


def dot(left, right):
    return jnp.dot(left, right, preferred_element_type=F32)


def order_matrix(size, reverse):
    row = lax.broadcasted_iota(jnp.int32, (size, size), 0)
    column = lax.broadcasted_iota(jnp.int32, (size, size), 1)
    target = jnp.where(reverse == 1, size - 1 - row, row)
    return jnp.where(column == target, 1.0, 0.0).astype(BF16)


def high_low(value):
    high = value.astype(BF16)
    low = (value - high.astype(F32)).astype(BF16)
    return jnp.concatenate([high, low], axis=1)


def norm_block(values, gain_row):
    widened = values.astype(F32)
    inverse_rms = lax.rsqrt(jnp.mean(widened * widened, axis=-1, keepdims=True) + EPSILON)
    return (widened * inverse_rms * gain_row).astype(BF16)


def prep_kernel(
    info,
    rows,
    halo,
    gain,
    wide,
    side_weight,
    taps,
    side_taps,
    bias,
    decay,
    spread,
    normed_out,
    x_out,
    b_out,
    c_out,
    cum_out,
    shifted_out,
    reach_out,
    local_out,
    state_out,
    extended,
    buffer,
    turned,
    shares,
    wide_shares,
    running,
):
    step_index = pl.program_id(0)
    reverse = info[0]
    length = rows.shape[0]
    heads = bias.shape[1]
    state = b_out.shape[1]
    chunks = length // CHUNK
    margin = taps.shape[0] - 1
    width = wide.shape[1]
    heads_here = cum_out.shape[2]

    def filtered(kernel, start, size, lanes):
        total = None
        for k in range(margin + 1):
            part = buffer[HALO - margin + k + start : HALO - margin + k + start + size, lanes]
            term = kernel[k : k + 1, lanes] * part
            total = term if total is None else total + term
        return silu(total).astype(BF16)

    @pl.when(step_index == 0)
    def _():
        turn = order_matrix(2 * CHUNK, reverse)
        small_turn = order_matrix(HALO, reverse)
        edge = norm_block(halo[...], gain[...])
        extended[0:HALO] = dot(small_turn, edge).astype(BF16)
        pairs = length // (2 * CHUNK)
        for pair in range(pairs):
            source = jnp.where(reverse == 1, pairs - 1 - pair, pair) * (2 * CHUNK)
            source = pl.multiple_of(source, 2 * CHUNK)
            piece = norm_block(rows[pl.ds(source, 2 * CHUNK), :], gain[...])
            start = HALO + pair * 2 * CHUNK
            extended[start : start + 2 * CHUNK] = dot(turn, piece).astype(BF16)
        normed_out[...] = extended[HALO:]
        side = dot(extended[...], side_weight[...]).astype(BF16).astype(F32)
        buffer[:, 0 : 2 * state] = side[:, 0 : 2 * state]
        raw = side[HALO:, 2 * state :] + bias[...]
        step = jnp.maximum(raw, 0.0) + jnp.log1p(jnp.exp(-jnp.abs(raw)))
        change = step * (decay[...] * (-LOG2E))
        row = lax.broadcasted_iota(jnp.int32, (CHUNK, CHUNK), 0)
        column = lax.broadcasted_iota(jnp.int32, (CHUNK, CHUNK), 1)
        triangle = jnp.where(row >= column, 1.0, 0.0).astype(F32)
        before = jnp.zeros((1, heads), F32)
        totals = []
        befores = []
        for c in range(chunks):
            here = slice(c * CHUNK, (c + 1) * CHUNK)
            cumulative = jnp.dot(
                triangle, change[here], preferred_element_type=F32, precision=lax.Precision.HIGHEST
            )
            last = cumulative[CHUNK - 1 :, :]
            befores.append(before)
            totals.append(last)
            before = before + last
            for j in range(heads // heads_here):
                cum_out[j, here, :] = cumulative[:, j * heads_here : (j + 1) * heads_here]
            moved = cumulative - jnp.log2(step[here])
            padded = jnp.concatenate([moved, jnp.zeros((CHUNK, 128 - heads), F32)], axis=1)
            shifted_out[:, here] = padded.T[0:heads]
            shares[here, :] = high_low(jnp.exp2(last - cumulative) * step[here])
            reach_out[here, :] = high_low(jnp.exp2(cumulative))
        befores.append(before)
        zero_rows = jnp.zeros((HALO - chunks, heads), F32)
        shares[length:, :] = high_low(jnp.exp2(jnp.concatenate(totals + [zero_rows], axis=0)))
        zero_rows = jnp.zeros((HALO - chunks - 1, heads), F32)
        reach_out[length:, :] = high_low(jnp.exp2(jnp.concatenate(befores + [zero_rows], axis=0)))
        for c in range(chunks):
            start = c * CHUNK
            here = slice(start, start + CHUNK)
            in_part = filtered(side_taps, start, CHUNK, slice(0, state))
            b_out[here] = in_part
            turned[:, here] = in_part.astype(F32).T.astype(BF16)
            c_out[here] = filtered(side_taps, start, CHUNK, slice(state, 2 * state))

    buffer[...] = dot(extended[...], wide[...]).astype(BF16).astype(F32)
    wide_shares[...] = dot(shares[...], spread[...])
    sub = 64
    running[...] = jnp.zeros_like(running)
    for c in range(chunks):
        here = slice(c * CHUNK, (c + 1) * CHUNK)
        for lane in range(0, width, 256):
            lanes = slice(lane, lane + 256)
            weighted = []
            for start in range(c * CHUNK, (c + 1) * CHUNK, sub):
                piece = filtered(taps, start, sub, lanes)
                x_out[start : start + sub, lanes] = piece
                weighted.append(
                    (piece.astype(F32) * wide_shares[start : start + sub, lanes]).astype(BF16)
                )
            states = dot(turned[:, here], jnp.concatenate(weighted, axis=0))
            entering = running[:, lanes]
            local_out[c, :, lanes] = entering.astype(BF16)
            total = wide_shares[length + c : length + c + 1, lanes]
            running[:, lanes] = total * entering + states
    state_out[0:state, :] = running[...].astype(BF16)
    through = wide_shares[length : length + 1, :]
    for c in range(1, chunks):
        through = through * wide_shares[length + c : length + c + 1, :]
    high = through.astype(BF16)
    low = (through - high.astype(F32)).astype(BF16)
    tail = jnp.concatenate(
        [high.astype(F32), low.astype(F32), jnp.zeros((HALO - 2, width), F32)], axis=0
    )
    state_out[state:, :] = tail.astype(BF16)


def mid_kernel(normed, gate_weight, x, b, c_rows, cumulative, shifted, skip, y_out, gate_out, scores):
    step_index = pl.program_id(0)
    length = x.shape[0]
    chunks = length // CHUNK
    heads_here = cumulative.shape[1]
    head_dim = x.shape[1] // heads_here
    row = lax.broadcasted_iota(jnp.int32, (CHUNK, CHUNK), 0)
    column = lax.broadcasted_iota(jnp.int32, (CHUNK, CHUNK), 1)
    causal = row >= column
    lane = lax.broadcasted_iota(jnp.int32, (CHUNK, 2 * head_dim), 1)

    @pl.when(step_index == 0)
    def _():
        for c in range(chunks):
            here = slice(c * CHUNK, (c + 1) * CHUNK)
            scores[here, :] = lax.dot_general(
                c_rows[here, :], b[here, :], (((1,), (1,)), ((), ())), preferred_element_type=F32
            )

    gate_out[...] = dot(normed[...], gate_weight[...]).astype(BF16)
    for c in range(chunks):
        here = slice(c * CHUNK, (c + 1) * CHUNK)
        score = scores[here, :]
        for pair in range(heads_here // 2):
            lanes = slice(2 * pair * head_dim, (2 * pair + 2) * head_dim)
            parts = []
            for h in (2 * pair, 2 * pair + 1):
                gap = cumulative[here, h : h + 1] - shifted[h : h + 1, here]
                parts.append((score * jnp.exp2(jnp.where(causal, gap, -jnp.inf))).astype(BF16))
            values = x[here, lanes]
            zero = jnp.zeros_like(values)
            stacked = jnp.concatenate(
                [jnp.where(lane < head_dim, values, zero), jnp.where(lane < head_dim, zero, values)],
                axis=0,
            )
            within = dot(jnp.concatenate(parts, axis=1), stacked)
            y_out[here, lanes] = within + skip[:, lanes] * values.astype(F32)


def finish_kernel(
    pieces,
    info,
    rows,
    y,
    gate,
    c_rows,
    reach,
    reach_tail,
    local,
    entering,
    gain,
    spread,
    *rest,
):
    weights = rest[:pieces]
    sent_out, base_out, normed = rest[pieces:]
    reverse = info[1]
    inner = y.shape[1]
    width = weights[0].shape[0]
    tail = dot(reach_tail[...], spread[...])
    pick = lax.broadcasted_iota(jnp.int32, (HALO, 1), 0) == info[0]
    before = jnp.sum(jnp.where(pick, tail, 0.0), axis=0, keepdims=True)
    squares = jnp.zeros((CHUNK, 1), F32)
    gated = []
    block = 256
    for start in range(0, inner, block):
        lanes = slice(start, start + block)
        full = (local[:, lanes].astype(F32) + before[:, lanes] * entering[:, lanes].astype(F32)).astype(BF16)
        carried = dot(c_rows[...], full) * dot(reach[...], spread[:, lanes])
        part = (y[:, lanes] + carried) * silu(gate[:, lanes].astype(F32))
        squares = squares + jnp.sum(part * part, axis=-1, keepdims=True)
        gated.append(part)
    inverse_rms = lax.rsqrt(squares * (1.0 / inner) + EPSILON)
    turn = order_matrix(CHUNK, reverse)
    for index, start in enumerate(range(0, inner, block)):
        lanes = slice(start, start + block)
        piece = (gated[index] * inverse_rms * gain[:, lanes]).astype(BF16)
        piece = dot(turn, piece).astype(BF16)
        if width == block:
            normed[index] = piece
        else:
            normed[0, :, lanes] = piece
    total = None
    for p in range(pieces):
        term = dot(normed[info[2 + p]], weights[p][...])
        total = term if total is None else total + term
    sent_out[...] = total.astype(BF16)
    base_out[...] = rows[...].astype(F32) + total


def whole_block(shape):
    return pl.BlockSpec(shape, lambda *_: (0,) * len(shape))


def prep(info, rows, halo, gain, main, side, conv, bias, decay, spread, inner, state):
    length, features = rows.shape
    heads = bias.shape[1]
    steps = inner // WIDTH
    heads_here = heads // steps
    chunks = length // CHUNK
    margin = conv.shape[1]
    side_taps = conv[0, :, inner:]
    grid_spec = pltpu.PrefetchScalarGridSpec(
        num_scalar_prefetch=1,
        grid=(steps,),
        in_specs=[
            whole_block((length, features)),
            whole_block((HALO, features)),
            whole_block((1, features)),
            pl.BlockSpec((None, features, WIDTH), lambda j, _: (0, 0, steps + j)),
            pl.BlockSpec((None, features, side.shape[2]), lambda j, _: (0, 0, 0)),
            pl.BlockSpec((None, margin, WIDTH), lambda j, _: (0, 0, j)),
            whole_block(side_taps.shape),
            whole_block((1, heads)),
            whole_block((1, heads)),
            pl.BlockSpec((2 * heads, WIDTH), lambda j, _: (0, j)),
        ],
        out_specs=[
            whole_block((length, features)),
            pl.BlockSpec((length, WIDTH), lambda j, _: (0, j)),
            whole_block((length, state)),
            whole_block((length, state)),
            whole_block((steps, length, heads_here)),
            whole_block((heads, length)),
            whole_block((length + HALO, 2 * heads)),
            pl.BlockSpec((chunks, state, WIDTH), lambda j, _: (0, 0, j)),
            pl.BlockSpec((state + HALO, WIDTH), lambda j, _: (0, j)),
        ],
        scratch_shapes=[
            pltpu.VMEM((length + HALO, features), BF16),
            pltpu.VMEM((length + HALO, WIDTH), F32),
            pltpu.VMEM((state, length), BF16),
            pltpu.VMEM((length + HALO, 2 * heads), BF16),
            pltpu.VMEM((length + HALO, WIDTH), F32),
            pltpu.VMEM((state, WIDTH), F32),
        ],
    )
    shape = jax.ShapeDtypeStruct
    return pl.pallas_call(
        prep_kernel,
        grid_spec=grid_spec,
        out_shape=[
            shape((length, features), BF16),
            shape((length, inner), BF16),
            shape((length, state), BF16),
            shape((length, state), BF16),
            shape((steps, length, heads_here), F32),
            shape((heads, length), F32),
            shape((length + HALO, 2 * heads), BF16),
            shape((chunks, state, inner), BF16),
            shape((state + HALO, inner), BF16),
        ],
        compiler_params=pltpu.CompilerParams(
            vmem_limit_bytes=40 * 2**20, dimension_semantics=("arbitrary",)
        ),
        cost_estimate=pl.CostEstimate(
            flops=2 * length * features * inner, bytes_accessed=12 * 2**20, transcendentals=0
        ),
        name="prep",
    )(info, rows, halo, gain, main, side, conv, side_taps, bias, decay, spread)


def mid(normed, main, x, b, c_rows, cumulative, shifted, skip, inner):
    length, features = normed.shape
    state = b.shape[1]
    steps = inner // WIDTH
    heads_here = cumulative.shape[2]
    return pl.pallas_call(
        mid_kernel,
        grid=(steps,),
        in_specs=[
            whole_block((length, features)),
            pl.BlockSpec((None, features, WIDTH), lambda j: (0, 0, j)),
            pl.BlockSpec((length, WIDTH), lambda j: (0, j)),
            whole_block((length, state)),
            whole_block((length, state)),
            pl.BlockSpec((None, length, heads_here), lambda j: (j, 0, 0)),
            pl.BlockSpec((heads_here, length), lambda j: (j, 0)),
            pl.BlockSpec((1, WIDTH), lambda j: (0, j)),
        ],
        out_specs=[
            pl.BlockSpec((length, WIDTH), lambda j: (0, j)),
            pl.BlockSpec((length, WIDTH), lambda j: (0, j)),
        ],
        out_shape=[
            jax.ShapeDtypeStruct((length, inner), F32),
            jax.ShapeDtypeStruct((length, inner), BF16),
        ],
        scratch_shapes=[pltpu.VMEM((length, CHUNK), F32)],
        compiler_params=pltpu.CompilerParams(
            vmem_limit_bytes=40 * 2**20, dimension_semantics=("arbitrary",)
        ),
        cost_estimate=pl.CostEstimate(
            flops=2 * length * features * inner, bytes_accessed=12 * 2**20, transcendentals=0
        ),
        name="mid",
    )(normed, main, x, b, c_rows, cumulative, shifted, skip)


def finish(info, rows, index, y, gate, c_rows, reach, local, entering, gain, spread, weights):
    features = rows.shape[1]
    length, inner = y.shape
    state = c_rows.shape[1]
    count = len(weights)
    width = weights[0].shape[0]
    reach_width = reach.shape[1]
    tail = length // HALO
    grid_spec = pltpu.PrefetchScalarGridSpec(
        num_scalar_prefetch=1,
        grid=(1,),
        in_specs=[
            pl.BlockSpec((CHUNK, features), lambda j, s: (index, 0)),
            pl.BlockSpec((CHUNK, inner), lambda j, s: (s[0], 0)),
            pl.BlockSpec((CHUNK, inner), lambda j, s: (s[0], 0)),
            pl.BlockSpec((CHUNK, state), lambda j, s: (s[0], 0)),
            pl.BlockSpec((CHUNK, reach_width), lambda j, s: (s[0], 0)),
            pl.BlockSpec((HALO, reach_width), lambda j, s: (tail, 0)),
            pl.BlockSpec((None, state, inner), lambda j, s: (s[0], 0, 0)),
            whole_block((state, inner)),
            whole_block((1, inner)),
            whole_block(spread.shape),
        ]
        + [whole_block(weight.shape) for weight in weights],
        out_specs=[whole_block((CHUNK, features)), whole_block((CHUNK, features))],
        scratch_shapes=[pltpu.VMEM((inner // width, CHUNK, width), BF16)],
    )
    return pl.pallas_call(
        functools.partial(finish_kernel, count),
        grid_spec=grid_spec,
        out_shape=[
            jax.ShapeDtypeStruct((CHUNK, features), BF16),
            jax.ShapeDtypeStruct((CHUNK, features), F32),
        ],
        compiler_params=pltpu.CompilerParams(
            vmem_limit_bytes=40 * 2**20, dimension_semantics=("arbitrary",)
        ),
        cost_estimate=pl.CostEstimate(
            flops=2 * CHUNK * features * inner, bytes_accessed=8 * 2**20, transcendentals=0
        ),
        name="finish",
    )(info, rows, y, gate, c_rows, reach, reach, local, entering, gain, spread, *weights)


def gathered_pieces(shard, seq_index, seq_count):
    if seq_count != 8:
        return [lax.all_gather(shard, "seq", axis=0, tiled=True)], [jnp.int32(0)]

    def swap(value, mask):
        return lax.ppermute(value, "seq", [(i, i ^ mask) for i in range(seq_count)])

    half = shard.shape[0] // 2
    across = swap(shard, 2)
    along = swap(shard, 4)
    upper = swap(along[:half], 2)
    lower = swap(across[half:], 4)
    diagonal = jnp.concatenate([upper, lower], axis=0)
    mine = [(shard, 0), (across, 2), (along, 4), (diagonal, 6)]
    pieces = mine + [(swap(piece, 1), mask + 1) for piece, mask in mine]
    return [piece for piece, _ in pieces], [seq_index ^ mask for _, mask in pieces]


def split_state(packed):
    state = packed.shape[0] - HALO
    values = packed[:state].astype(F32)
    through = packed[state : state + 1].astype(F32) + packed[state + 1 : state + 2].astype(F32)
    return values, through


def joined_state(values, through):
    high = through.astype(BF16)
    low = (through - high.astype(F32)).astype(BF16)
    rest = jnp.zeros((HALO - 2, through.shape[1]), BF16)
    return jnp.concatenate([values.astype(BF16), high, low, rest], axis=0)


def after(earlier, later):
    return later[1] * earlier[0] + later[0], earlier[1] * later[1]


def chosen(condition, first, second):
    return tuple(jnp.where(condition, a, b) for a, b in zip(first, second))


def entering_state(packed, sections, seq_index, seq_count, reverse):
    bits = seq_count.bit_length() - 1
    section_count = lax.axis_size("section")

    def swap(value, mask):
        pairs = [
            (i * section_count + s, (i ^ mask) * section_count + s)
            for s in sections
            for i in range(seq_count)
        ]
        return lax.ppermute(value, ("seq", "section"), pairs)

    def forward(value, mask, low_bit):
        pairs = []
        for s in sections:
            for i in range(seq_count):
                later = (i ^ mask) >> low_bit > i >> low_bit
                if later == (s % 2 == 0):
                    pairs.append((i * section_count + s, (i ^ mask) * section_count + s))
        return lax.ppermute(value, ("seq", "section"), pairs)

    inner = packed.shape[1]
    half = inner // 2
    partner = swap(packed, 1)
    upper = seq_index % 2 == 1
    first = jnp.logical_xor(upper, reverse) == 0
    mine_here = jnp.where(upper, packed[:, half:], packed[:, :half])
    other_here = jnp.where(upper, partner[:, half:], partner[:, :half])
    mine = split_state(mine_here)
    other = split_state(other_here)
    total = after(chosen(first, mine, other), chosen(first, other, mine))
    identity = (jnp.zeros_like(total[0]), jnp.ones_like(total[1]))
    entering = identity
    bit = 1
    while bit < bits:
        group = min(2, bits - bit)
        last = bit + group == bits
        packed_total = joined_state(*total)
        members = {}
        for code in range(1, 2**group):
            mask = code << bit
            send = forward(packed_total, mask, bit) if last else swap(packed_total, mask)
            members[code] = split_state(send)
        position = (seq_index >> bit) % 2**group
        rank = jnp.where(reverse, 2**group - 1 - position, position)
        before = identity
        whole = identity
        for place in range(2**group):
            value = total
            for code in range(1, 2**group):
                value = chosen((rank ^ code) == place, members[code], value)
            if place < 2**group - 1:
                step = after(before, value)
                before = chosen(place < rank, step, before)
            if not last:
                whole = after(whole, value)
        entering = after(before, entering) if bit > 1 else before
        if not last:
            total = whole
        bit += group
    return entering[0], packed, partner, upper, first, swap


def device_state(entering_half, packed, partner, upper, first, swap):
    half_state = entering_half.astype(BF16)
    other_half = swap(half_state, 1)
    left = jnp.where(upper, other_half, half_state)
    right = jnp.where(upper, half_state, other_half)
    full = jnp.concatenate([left, right], axis=1)
    values, through = split_state(partner)
    moved = (through * full.astype(F32) + values).astype(BF16)
    return jnp.where(first, full, moved)


def per_device(
    tokens,
    input_gain,
    main_weight,
    side_weight,
    conv_kernel,
    step_bias,
    decay_rate,
    skip_gain,
    output_gain,
    output_weight,
):
    length, features = tokens.shape
    inner = main_weight.shape[2] // 2
    heads = decay_rate.shape[1]
    state = (side_weight.shape[2] - heads) // 2
    head_dim = inner // heads
    chunks = length // CHUNK
    seq_count = lax.axis_size("seq")
    section_count = lax.axis_size("section")
    section_index = lax.axis_index("section")
    seq_index = lax.axis_index("seq")
    reverse = section_index % 2
    layer_here = section_index // 2
    weights, owners = gathered_pieces(output_weight[0], seq_index, seq_count)
    expand = np.repeat(np.eye(heads, dtype=np.float32), head_dim, axis=1)
    spread = jnp.asarray(np.concatenate([expand, expand], axis=0), BF16)
    skip_row = jnp.repeat(skip_gain, head_dim, axis=1)
    info = reverse.astype(jnp.int32).reshape(1)
    order = [chunks - 1, 0] + list(range(1, chunks - 1))

    def edges(first_rows, last_rows, sections):
        pairs = []
        for s in sections:
            for i in range(seq_count):
                target = i + 1 if s % 2 == 0 else i - 1
                if 0 <= target < seq_count:
                    pairs.append((i * section_count + s, target * section_count + s))
        value = jnp.where(reverse == 1, first_rows, last_rows)
        return lax.ppermute(value, ("seq", "section"), pairs)

    rounds = section_count // 2
    current = tokens
    halo = edges(tokens[:HALO], tokens[length - HALO :], (0, 1))
    finished = None
    for round_index in range(rounds):
        active = (2 * round_index, 2 * round_index + 1)
        normed, x, b, c_rows, cumulative, shifted, reach, local, packed = prep(
            info,
            current,
            halo,
            input_gain,
            main_weight,
            side_weight,
            conv_kernel,
            step_bias,
            decay_rate,
            spread,
            inner,
            state,
        )
        y, gate = mid(normed, main_weight, x, b, c_rows, cumulative, shifted, skip_row, inner)
        parts = entering_state(packed, active, seq_index, seq_count, reverse == 1)
        entering = device_state(*parts)
        here = layer_here == round_index
        sections = [active]
        done_rows = [None] * chunks
        next_rows = [None] * chunks
        last_round = round_index + 1 == rounds
        for index in order:
            chunk = jnp.where(reverse == 1, chunks - 1 - index, index).astype(jnp.int32)
            chunk_info = jnp.stack([chunk, info[0]] + [owner.astype(jnp.int32) for owner in owners])
            sent, base = finish(
                chunk_info, current, index, y, gate, c_rows, reach, local, entering,
                output_gain, spread, weights,
            )
            low, high = active
            other = lax.ppermute(sent, "section", [(low, high), (high, low)])
            layer_rows = (base + other.astype(F32)).astype(BF16)
            done_rows[index] = layer_rows
            if not last_round:
                near = lax.ppermute(layer_rows, "section", [(high, high + 1)])
                far = lax.ppermute(near, "section", [(high + 1, high + 2)])
                next_rows[index] = jnp.where(section_index == high + 2, far, near)
        result = jnp.concatenate(done_rows, axis=0)
        finished = result if finished is None else jnp.where(here, result, finished)
        if not last_round:
            next_active = (active[0] + 2, active[1] + 2)
            halo = edges(next_rows[0][:HALO], next_rows[chunks - 1][CHUNK - HALO :], next_active)
            current = jnp.concatenate(next_rows, axis=0)
    return finished[None]


def solution(mesh):
    placed = (
        P("seq", None),
        P("section", None),
        P("section", None, None),
        P("section", None, None),
        P("section", None, None),
        P("section", None),
        P("section", None),
        P("section", None),
        P("section", None),
        P("section", "seq", None),
    )
    return jax.shard_map(
        per_device, mesh=mesh, in_specs=placed, out_specs=P("section", "seq", None), check_vma=False
    )
```

time: 637 us -> 235 us (0.37)
  waiting for transfers between devices: 357 us -> 53.3 us
  local copies, waits for them, and re-layouts: 144 us -> 38.7 us
  Pallas kernels: 0 us -> 68.2 us
  matrix products: 35.6 us -> 0 us
  other arithmetic: 32.3 us -> 18.7 us
  between operations: 13.9 us -> 1.4 us
    ppermute x17 -> x36, waiting for transfers between devices: 356 us -> 53.3 us  [the longest x4 30 us: per_device(): near = lax.ppermute(layer_rows, 'section', [(high, high + 1)])]
    rev x6 -> x0, local copies, waits for them, and re-layouts: 79.5 us -> none  [the longest x4 70.8 us: orient(): return jnp.where(reverse_side, jnp.flip(values, 0), values)]
    pallas_call x0 -> x12, Pallas kernels: none -> 68.2 us  [the longest x8 29.8 us: finish(): pl.pallas_call(functools.partial(finish_kernel, count), grid_spec=grid_sp...]
    dot_general x10 -> x0, matrix products: 35.6 us -> none  [the longest x2 8.38 us: block_group(): jnp.einsum('chts,cshp->cthp', weights, inner_heads, preferred_element_typ...]
    unnamed x33 -> x172, local copies, waits for them, and re-layouts: 4.52 us -> 35 us
    another operation x30 -> x5, local copies, waits for them, and re-layouts: 19.8 us -> 2.71 us  [the longest x4 2.71 us: per_device(): jnp.stack([chunk, info[0]] + [owner.astype(jnp.int32) for owner in owners])]
    slice x9 -> x2, local copies, waits for them, and re-layouts: 10.1 us -> 0.04 us  [the longest x1 0.02 us: gathered_pieces(): upper = swap(along[:half], 2)]
    select_n x7 -> x17, other arithmetic: 3.68 us -> 11 us  [the longest x4 3.94 us: per_device(): next_rows[index] = jnp.where(section_index == high + 2, far, near)]
  transfers between devices with their start and end apart: 18 -> 36, of which waited for: 10 -> 13; matrix products, arithmetic and copies ran while one was open for 4% -> 9% of each run, Pallas kernels for 0% -> 15%
where the time goes in v1:
time: 235 us; the launch traced here: 231 us
  Pallas kernels  68.2 us (29%)
  waiting for transfers between devices  53.3 us (23%)
  starting transfers between devices  50.3 us (21%)
  local copies, waits for them, and re-layouts  38.7 us (16%)
  other arithmetic  18.7 us (8%)
    unnamed x172, local copies, waits for them, and re-layouts  35 us
    ppermute x4, waiting for transfers between devices, per_device(): near = lax.ppermute(layer_rows, 'section', [(high, high + 1)])  30 us
    pallas_call x8, Pallas kernels, finish(): pl.pallas_call(functools.partial(finish_kernel, count), grid_spec=grid_sp...  29.8 us
    pallas_call x2, Pallas kernels, prep(): pl.pallas_call(prep_kernel, grid_spec=grid_spec, out_shape=[shape((length...  25.5 us
    ppermute x8, starting transfers between devices, per_device(): other = lax.ppermute(sent, 'section', [(low, high), (high, low)])  15.3 us
    pallas_call x2, Pallas kernels, mid(): pl.pallas_call(mid_kernel, grid=(steps,), in_specs=[whole_block((length,...  12.8 us
    ppermute x6, starting transfers between devices, forward(): return lax.ppermute(value, ('seq', 'section'), pairs)  9.6 us
    ppermute x6, waiting for transfers between devices, forward(): return lax.ppermute(value, ('seq', 'section'), pairs)  7.64 us
  transfers between devices with their start and end apart: 36, of which 13 were waited for; matrix products, arithmetic and copies ran while one was open for 9% of the time, Pallas kernels for 15%

profile of v1, /device:TPU:20, one launch (start us, length us, event | category | flops | bytes accessed | tf_op | source)
XLA Modules:
  0.0 230.6 jit_solution(10626110948241521237)
XLA Ops:
  2.2 1.4 copy.12.side_weight
  7.6 13.1 %prep.2 = (bf16[512,1024]{1,0:T(8,128)(2,1)S(1)}, bf16[512,2048]{1,0:T(8,128)(2,1)S(1)}, bf16[512,128]{1,0:T(8,128)(2,1)S(1)}, bf16[512,128]{1,0:T(8,128)(2,1)S(...) custom-call(s32[1]{0:T(128)} %bitcast.1.info, ...), custom_call_target="tpu_custom_call" | custom-call | flops 2147483648 | bytes 12582912 | tf_op jit(solution)/shard_map/prep/pallas_call | solution.py:318
  25.3 1.6 collective-permute-start.1
  27.4 1.5 collective-permute-start.6
  33.0 1.4 collective-permute-start.4
  34.4 1.4 collective-permute-start.3
  35.8 1.4 collective-permute-start.2
  38.0 1.6 copy-done.43
  40.8 6.3 %mid.2 = (f32[512,2048]{1,0:T(8,128)S(1)}, bf16[512,2048]{1,0:T(8,128)(2,1)S(1)}) custom-call(bf16[512,1024]{1,0:T(8,128)(2,1)S(1)} %copy-done.45, bf16[1,1024,4096]{2,1,0:T(8,128)(2,1)} %gate_weight.3, bf16[512,2048]{1,0:T(8,128)(2,1)S(1)} %copy-done.43, bf16[512,128]{1,0:T(8,128)(2,1)S(1)} %get-tuple-element.45.b, ...), custom_call_target="tpu_custom_call" | custom-call | flops 2147483648 | bytes 12582912 | tf_op jit(solution)/shard_map/mid/pallas_call | solution.py:347
  48.0 1.6 collective-permute-start.9
  51.3 1.7 fusion.12
  58.8 4.3 %finish.11 = (bf16[128,1024]{1,0:T(8,128)(2,1)}, f32[128,1024]{1,0:T(8,128)S(1)}) custom-call(s32[10]{0:T(128)S(1)} %copy-done.59, bf16[512,1024]{1,0:T(8,128)(2,1)S(1)} %copy-done.27, f32[512,2048]{1,0:T(8,128)} %copy-done, bf16[512,2048]{1,0:T(8,128)(2,1)S(1)} %get-tuple-element.50.gate, bf16[512,128]{1,0:T(8,128)(2,1)S(1)} %copy-done.38, ...), custom_call_target="tpu_custom_call" | custom-call | flops 536870912 | bytes 8388608 | tf_op jit(solution)/shard_map/finish/pallas_call | solution.py:406
  63.9 1.4 collective-permute-start.23
  67.3 1.6 copy-done.4
  68.9 1.6 copy-done.8
  76.5 3.5 %finish.10 = (bf16[128,1024]{1,0:T(8,128)(2,1)S(1)}, f32[128,1024]{1,0:T(8,128)S(1)}) custom-call(s32[10]{0:T(128)S(1)} %copy-done.65, bf16[512,1024]{1,0:T(8,128)(2,1)S(1)} %copy-done.28, f32[512,2048]{1,0:T(8,128)} %copy-done, bf16[512,2048]{1,0:T(8,128)(2,1)S(1)} %copy-done.8, bf16[512,128]{1,0:T(8,128)(2,1)S(1)} %copy-done.39, ...), custom_call_target="tpu_custom_call" | custom-call | flops 536870912 | bytes 8388608 | tf_op jit(solution)/shard_map/finish/pallas_call | solution.py:406
  80.7 3.6 %finish.9 = (bf16[128,1024]{1,0:T(8,128)(2,1)S(1)}, f32[128,1024]{1,0:T(8,128)S(1)}) custom-call(s32[10]{0:T(128)S(1)} %copy-done.63, bf16[512,1024]{1,0:T(8,128)(2,1)S(1)} %copy-done.28, f32[512,2048]{1,0:T(8,128)} %copy-done, bf16[512,2048]{1,0:T(8,128)(2,1)S(1)} %copy-done.8, bf16[512,128]{1,0:T(8,128)(2,1)S(1)} %copy-done.39, ...), custom_call_target="tpu_custom_call" | custom-call | flops 536870912 | bytes 8388608 | tf_op jit(solution)/shard_map/finish/pallas_call | solution.py:406
  85.1 3.6 %finish.8 = (bf16[128,1024]{1,0:T(8,128)(2,1)S(1)}, f32[128,1024]{1,0:T(8,128)S(1)}) custom-call(s32[10]{0:T(128)S(1)} %copy-done.61, bf16[512,1024]{1,0:T(8,128)(2,1)S(1)} %copy-done.28, f32[512,2048]{1,0:T(8,128)} %copy-done, bf16[512,2048]{1,0:T(8,128)(2,1)S(1)} %copy-done.8, bf16[512,128]{1,0:T(8,128)(2,1)S(1)} %copy-done.39, ...), custom_call_target="tpu_custom_call" | custom-call | flops 536870912 | bytes 8388608 | tf_op jit(solution)/shard_map/finish/pallas_call | solution.py:406
  95.9 20.1 %collective-permute-done.24 = bf16[128,1024]{1,0:T(8,128)(2,1)} collective-permute-done((bf16[128,1024]{1,0:T(8,128)(2,1)S(1)}, bf16[128,1024]{1,0:T(8,128)(2,1)}, u32[]{:S(2)}, u32[]{:S(2)}) %collective-permute-start.24) | collective-permute-done | bytes 262176 | tf_op jit(solution)/shard_map/ppermute | solution.py:618
  116.0 2.0 collective-permute-start.25
  118.0 9.2 %collective-permute-done.15 = bf16[128,1024]{1,0:T(8,128)(2,1)} collective-permute-done((bf16[128,1024]{1,0:T(8,128)(2,1)S(1)}, bf16[128,1024]{1,0:T(8,128)(2,1)}, u32[]{:S(2)}, u32[]{:S(2)}) %collective-permute-start.15) | collective-permute-done | bytes 262176 | tf_op jit(solution)/shard_map/ppermute | solution.py:618
  127.2 2.0 collective-permute-start.16
  133.5 2.1 collective-permute-done.16
  136.6 1.9 collective-permute-start.26
  138.5 1.5 collective-permute-done.22
  141.0 1.8 collective-permute-done.19
  143.9 12.4 %prep.3 = (bf16[512,1024]{1,0:T(8,128)(2,1)S(1)}, bf16[512,2048]{1,0:T(8,128)(2,1)S(1)}, bf16[512,128]{1,0:T(8,128)(2,1)S(1)}, bf16[512,128]{1,0:T(8,128)(2,1)S(...) custom-call(s32[1]{0:T(128)} %bitcast.1.info, ...), custom_call_target="tpu_custom_call" | custom-call | flops 2147483648 | bytes 12582912 | tf_op jit(solution)/shard_map/prep/pallas_call | solution.py:318
  156.4 2.1 collective-permute-start.27
  158.5 1.9 collective-permute-done.27
  160.8 2.6 %collective-permute-start.30 = (bf16[144,1024]{1,0:T(8,128)(2,1)S(1)}, bf16[144,1024]{1,0:T(8,128)(2,1)S(1)}, u32[]{:S(2)}, u32[]{:S(2)}) collective-permute-start(bf16[144,1024]{1,0:T(8,128)(2,1)S(1)} %maximum_maximum_fusion.1), channel_id=1, source_target_pairs={{2,10},{6,14},{18,26},{22,30},{11,3},{15,7},{27,19},{31,23}} | collective-permute-start | bytes 884744 | tf_op jit(solution)/shard_map/ppermute | solution.py:482
  164.7 1.5 collective-permute-start.28
  166.3 6.5 %mid.3 = (f32[512,2048]{1,0:T(8,128)S(1)}, bf16[512,2048]{1,0:T(8,128)(2,1)S(1)}) custom-call(bf16[512,1024]{1,0:T(8,128)(2,1)S(1)} %get-tuple-element.62.normed, bf16[1,1024,4096]{2,1,0:T(8,128)(2,1)} %gate_weight.3, bf16[512,2048]{1,0:T(8,128)(2,1)S(1)} %get-tuple-element.63.x, bf16[512,128]{1,0:T(8,128)(2,1)S(1)} %get-tuple-element.64.b, ...), custom_call_target="tpu_custom_call" | custom-call | flops 2147483648 | bytes 12582912 | tf_op jit(solution)/shard_map/mid/pallas_call | solution.py:347
  172.8 7.6 %collective-permute-done.29 = bf16[144,1024]{1,0:T(8,128)(2,1)S(1)} collective-permute-done((bf16[144,1024]{1,0:T(8,128)(2,1)S(1)}, bf16[144,1024]{1,0:T(8,128)(2,1)S(1)}, u32[]{:S(2)}, u32[]{:S(2)}) %collective-permute-start.29) | collective-permute-done | bytes 294944 | tf_op jit(solution)/shard_map/ppermute | solution.py:482
  181.0 2.1 collective-permute-start.31
  183.1 1.5 collective-permute-done.31
  184.9 4.3 %finish.15 = (bf16[128,1024]{1,0:T(8,128)(2,1)}, f32[128,1024]{1,0:T(8,128)S(1)}) custom-call(s32[10]{0:T(128)S(1)} %copy-done.60, bf16[512,1024]{1,0:T(8,128)(2,1)S(1)} %pad_maximum_fusion.rows, f32[512,2048]{1,0:T(8,128)} %copy-done.1, bf16[512,2048]{1,0:T(8,128)(2,1)S(1)} %get-tuple-element.69.gate, bf16[512,128]{1,0:T(8,128)(2,1)S(1)} %get-tuple-element.65.c_rows, ...), custom_call_target="tpu_custom_call" | custom-call | flops 536870912 | bytes 8388608 | tf_op jit(solution)/shard_map/finish/pallas_call | solution.py:406
  189.2 1.4 copy-done.9
  191.3 1.9 collective-permute-start.35
  193.3 1.6 copy-done.6
  194.9 1.6 copy-done.10
  202.6 3.5 %finish.14 = (bf16[128,1024]{1,0:T(8,128)(2,1)S(1)}, f32[128,1024]{1,0:T(8,128)S(1)}) custom-call(s32[10]{0:T(128)S(1)} %copy-done.66, bf16[512,1024]{1,0:T(8,128)(2,1)S(1)} %pad_maximum_fusion.rows, f32[512,2048]{1,0:T(8,128)} %copy-done.1, bf16[512,2048]{1,0:T(8,128)(2,1)S(1)} %copy-done.10, bf16[512,128]{1,0:T(8,128)(2,1)S(1)} %copy-done.41, ...), custom_call_target="tpu_custom_call" | custom-call | flops 536870912 | bytes 8388608 | tf_op jit(solution)/shard_map/finish/pallas_call | solution.py:406
  206.1 3.9 %collective-permute-start.34 = (bf16[128,1024]{1,0:T(8,128)(2,1)S(1)}, bf16[128,1024]{1,0:T(8,128)(2,1)S(1)}, u32[]{:S(2)}, u32[]{:S(2)}) collective-permute-start(bf16[128,1024]{1,0:T(8,128)(2,1)S(1)} %get-tuple-element.78), channel_id=1, source_target_pairs={{2,3},{3,2},{6,7},{7,6},{10,11},{11,10},{14,15},{15,14},{18,19},{1... | collective-permute-start | bytes 786440 | tf_op jit(solution)/shard_map/ppermute | solution.py:614
  210.1 3.5 %finish.13 = (bf16[128,1024]{1,0:T(8,128)(2,1)S(1)}, f32[128,1024]{1,0:T(8,128)S(1)}) custom-call(s32[10]{0:T(128)S(1)} %copy-done.64, bf16[512,1024]{1,0:T(8,128)(2,1)S(1)} %pad_maximum_fusion.rows, f32[512,2048]{1,0:T(8,128)} %copy-done.1, bf16[512,2048]{1,0:T(8,128)(2,1)S(1)} %copy-done.10, bf16[512,128]{1,0:T(8,128)(2,1)S(1)} %copy-done.41, ...), custom_call_target="tpu_custom_call" | custom-call | flops 536870912 | bytes 8388608 | tf_op jit(solution)/shard_map/finish/pallas_call | solution.py:406
  213.6 2.1 collective-permute-start.33
  215.7 3.5 %finish.12 = (bf16[128,1024]{1,0:T(8,128)(2,1)S(1)}, f32[128,1024]{1,0:T(8,128)S(1)}) custom-call(s32[10]{0:T(128)S(1)} %copy-done.62, bf16[512,1024]{1,0:T(8,128)(2,1)S(1)} %pad_maximum_fusion.rows, f32[512,2048]{1,0:T(8,128)} %copy-done.1, bf16[512,2048]{1,0:T(8,128)(2,1)S(1)} %copy-done.10, bf16[512,128]{1,0:T(8,128)(2,1)S(1)} %copy-done.41, ...), custom_call_target="tpu_custom_call" | custom-call | flops 536870912 | bytes 8388608 | tf_op jit(solution)/shard_map/finish/pallas_call | solution.py:406
  219.3 3.9 %collective-permute-start.32 = (bf16[128,1024]{1,0:T(8,128)(2,1)S(1)}, bf16[128,1024]{1,0:T(8,128)(2,1)S(1)}, u32[]{:S(2)}, u32[]{:S(2)}) collective-permute-start(bf16[128,1024]{1,0:T(8,128)(2,1)S(1)} %get-tuple-element.74), channel_id=1, source_target_pairs={{2,3},{3,2},{6,7},{7,6},{10,11},{11,10},{14,15},{15,14},{18,19},{1... | collective-permute-start | bytes 786440 | tf_op jit(solution)/shard_map/ppermute | solution.py:614
  224.5 4.6 %collective-permute-done.32 = bf16[128,1024]{1,0:T(8,128)(2,1)S(1)} collective-permute-done((bf16[128,1024]{1,0:T(8,128)(2,1)S(1)}, bf16[128,1024]{1,0:T(8,128)(2,1)S(1)}, u32[]{:S(2)}, u32[]{:S(2)}) %collective-permute-start.32) | collective-permute-done | bytes 262176 | tf_op jit(solution)/shard_map/ppermute | solution.py:614
  229.2 1.5 maximum_select_fusion
  (260 shorter events, 60.7 us)
Async XLA Ops:
  0.9 2.8 %collective-permute-start = (bf16[16,1024]{1,0:T(8,128)(2,1)S(1)}, bf16[16,1024]{1,0:T(8,128)(2,1)S(1)}, u32[]{:S(2)}, u32[]{:S(2)}) collective-permute-start(bf16[16,1024]{1,0:T(8,128)(2,1)S(1)} %slice_select_fusion.5), channel_id=1, source_target_pairs={{0,4},{4,8},{8,12},{12,16},{16,20},{20,24},{24,28},{5,1},{9,5},{13... | collective-permute-start | bytes 98312 | tf_op jit(solution)/shard_map/ppermute | solution.py:576
  7.6 19.3 %copy-start.11 = (bf16[1,256,1024]{2,1,0:T(8,128)(2,1)S(1)}, bf16[1,256,1024]{2,1,0:T(8,128)(2,1)}, u32[]{:S(2)}) copy-start(bf16[1,256,1024]{2,1,0:T(8,128)(2,1)} %param.20) | copy-start | bytes 1572868
  25.3 21.9 %copy-start.37 = (bf16[512,128]{1,0:T(8,128)(2,1)}, bf16[512,128]{1,0:T(8,128)(2,1)S(1)}, u32[]{:S(2)}) copy-start(bf16[512,128]{1,0:T(8,128)(2,1)S(1)} %get-tuple-element.46.c_rows) | copy-start | bytes 393220
  25.3 4.8 %collective-permute-start.1 = (bf16[144,2048]{1,0:T(8,128)(2,1)}, bf16[144,2048]{1,0:T(8,128)(2,1)}, u32[]{:S(2)}, u32[]{:S(2)}) collective-permute-start(bf16[144,2048]{1,0:T(8,128)(2,1)} %get-tuple-element.53), channel_id=1, source_target_pairs={{0,4},{4,0},{8,12},{12,8},{16,20},{20,16},{24,28},{28,24},{1,5},{5... | collective-permute-start | bytes 1769480 | tf_op jit(solution)/shard_map/ppermute | solution.py:473
  26.9 20.3 %collective-permute-start.7 = (bf16[256,1024]{1,0:T(8,128)(2,1)S(1)}, bf16[256,1024]{1,0:T(8,128)(2,1)S(1)}, u32[]{:S(2)}, u32[]{:S(2)}) collective-permute-start(bf16[256,1024]{1,0:T(8,128)(2,1)S(1)} %bitcast.39), channel_id=1, source_target_pairs={{0,16},{4,20},{8,24},{12,28},{16,0},{20,4},{24,8},{28,12},{1,17},{... | collective-permute-start | bytes 1572872 | tf_op jit(solution)/shard_map/ppermute | solution.py:428
  27.4 19.9 %collective-permute-start.6 = (bf16[256,1024]{1,0:T(8,128)(2,1)S(1)}, bf16[256,1024]{1,0:T(8,128)(2,1)S(1)}, u32[]{:S(2)}, u32[]{:S(2)}) collective-permute-start(bf16[256,1024]{1,0:T(8,128)(2,1)S(1)} %bitcast.40), channel_id=1, source_target_pairs={{0,8},{4,12},{8,0},{12,4},{16,24},{20,28},{24,16},{28,20},{1,9},{5... | collective-permute-start | bytes 1572872 | tf_op jit(solution)/shard_map/ppermute | solution.py:428
  29.0 18.2 %copy-start.82 = (bf16[144]{0:T(256)(128)(2,1)}, bf16[144]{0:T(256)(128)(2,1)S(1)}, u32[]{:S(2)}) copy-start(bf16[144]{0:T(256)(128)(2,1)S(1)} %pad.23.clone) | copy-start | bytes 868
  30.1 17.1 %copy-start.71 = (bf16[144,1024]{1,0:T(8,128)(2,1)}, bf16[144,1024]{1,0:T(8,128)(2,1)S(1)}, u32[]{:S(2)}) copy-start(bf16[144,1024]{1,0:T(8,128)(2,1)S(1)} %slice_select_fusion.3) | copy-start | bytes 884740
  33.0 15.0 %collective-permute-start.4 = (bf16[144,1024]{1,0:T(8,128)(2,1)}, bf16[144,1024]{1,0:T(8,128)(2,1)}, u32[]{:S(2)}, u32[]{:S(2)}) collective-permute-start(bf16[144,1024]{1,0:T(8,128)(2,1)} %maximum_maximum_fusion), channel_id=1, source_target_pairs={{0,8},{4,12},{16,24},{20,28},{9,1},{13,5},{25,17},{29,21}} | collective-permute-start | bytes 884744 | tf_op jit(solution)/shard_map/ppermute | solution.py:482
  34.4 15.2 %collective-permute-start.3 = (bf16[144,1024]{1,0:T(8,128)(2,1)}, bf16[144,1024]{1,0:T(8,128)(2,1)}, u32[]{:S(2)}, u32[]{:S(2)}) collective-permute-start(bf16[144,1024]{1,0:T(8,128)(2,1)} %maximum_maximum_fusion), channel_id=1, source_target_pairs={{0,16},{4,20},{8,24},{12,28},{17,1},{21,5},{25,9},{29,13}} | collective-permute-start | bytes 884744 | tf_op jit(solution)/shard_map/ppermute | solution.py:482
  35.8 13.8 %collective-permute-start.2 = (bf16[144,1024]{1,0:T(8,128)(2,1)}, bf16[144,1024]{1,0:T(8,128)(2,1)}, u32[]{:S(2)}, u32[]{:S(2)}) collective-permute-start(bf16[144,1024]{1,0:T(8,128)(2,1)} %maximum_maximum_fusion), channel_id=1, source_target_pairs={{0,24},{4,28},{8,16},{12,20},{17,9},{21,13},{25,1},{29,5}} | collective-permute-start | bytes 884744 | tf_op jit(solution)/shard_map/ppermute | solution.py:482
  47.2 10.8 %collective-permute-start.10 = (bf16[256,1024]{1,0:T(8,128)(2,1)S(1)}, bf16[256,1024]{1,0:T(8,128)(2,1)S(1)}, u32[]{:S(2)}, u32[]{:S(2)}) collective-permute-start(bf16[256,1024]{1,0:T(8,128)(2,1)S(1)} %bitcast.41), channel_id=1, source_target_pairs={{0,4},{4,0},{8,12},{12,8},{16,20},{20,16},{24,28},{28,24},{1,5},{5... | collective-permute-start | bytes 1572872 | tf_op jit(solution)/shard_map/ppermute | solution.py:428
  47.4 8.8 %collective-permute-start.8 = (bf16[128,1024]{1,0:T(8,128)(2,1)S(1)}, bf16[128,1024]{1,0:T(8,128)(2,1)S(1)}, u32[]{:S(2)}, u32[]{:S(2)}) collective-permute-start(bf16[128,1024]{1,0:T(8,128)(2,1)S(1)} %slice.225), channel_id=1, source_target_pairs={{0,8},{4,12},{8,0},{12,4},{16,24},{20,28},{24,16},{28,20},{1,9},{5... | collective-permute-start | bytes 786440 | tf_op jit(solution)/shard_map/ppermute | solution.py:428
  48.0 8.5 %collective-permute-start.9 = (bf16[128,1024]{1,0:T(8,128)(2,1)S(1)}, bf16[128,1024]{1,0:T(8,128)(2,1)S(1)}, u32[]{:S(2)}, u32[]{:S(2)}) collective-permute-start(bf16[128,1024]{1,0:T(8,128)(2,1)S(1)} %slice.226), channel_id=1, source_target_pairs={{0,16},{4,20},{8,24},{12,28},{16,0},{20,4},{24,8},{28,12},{1,17},{... | collective-permute-start | bytes 786440 | tf_op jit(solution)/shard_map/ppermute | solution.py:428
  49.6 8.5 %collective-permute-start.12 = (bf16[256,1024]{1,0:T(8,128)(2,1)S(1)}, bf16[256,1024]{1,0:T(8,128)(2,1)S(1)}, u32[]{:S(2)}, u32[]{:S(2)}) collective-permute-start(bf16[256,1024]{1,0:T(8,128)(2,1)S(1)} %collective-permute-done.7.rest_2_), channel_id=1, source_target_pairs={{0,4},{4,0},{8,12},{12,8},{16,20},{20,16},{24,28},{28,24},{1,5},{5... | collective-permute-start | bytes 1572872 | tf_op jit(solution)/shard_map/ppermute | solution.py:428
  53.0 3.8 %collective-permute-start.5 = (bf16[128,1024]{1,0:T(8,128)(2,1)S(1)}, bf16[128,1024]{1,0:T(8,128)(2,1)S(1)}, u32[]{:S(2)}, u32[]{:S(2)}) collective-permute-start(bf16[128,1024]{1,0:T(8,128)(2,1)S(1)} %fusion.12), channel_id=1, source_target_pairs={{0,4},{4,0},{8,12},{12,8},{16,20},{20,16},{24,28},{28,24},{1,5},{5... | collective-permute-start | bytes 786440 | tf_op jit(solution)/shard_map/ppermute | solution.py:473
  56.1 2.0 collective-permute-start.11
  56.5 2.3 collective-permute-start.13
  58.1 27.0 %copy-start.12 = (bf16[256,1024]{1,0:T(8,128)(2,1)}, bf16[256,1024]{1,0:T(8,128)(2,1)S(1)}, u32[]{:S(2)}) copy-start(bf16[256,1024]{1,0:T(8,128)(2,1)S(1)} %collective-permute-done.10.rest_4_) | copy-start | bytes 1572868
  58.1 27.0 %copy-start.15 = (bf16[256,1024]{1,0:T(8,128)(2,1)}, bf16[256,1024]{1,0:T(8,128)(2,1)S(1)}, u32[]{:S(2)}) copy-start(bf16[256,1024]{1,0:T(8,128)(2,1)S(1)} %collective-permute-done.12.rest_6_) | copy-start | bytes 1572868
  63.9 25.5 %collective-permute-start.23 = (bf16[128,1024]{1,0:T(8,128)(2,1)}, bf16[128,1024]{1,0:T(8,128)(2,1)}, u32[]{:S(2)}, u32[]{:S(2)}) collective-permute-start(bf16[128,1024]{1,0:T(8,128)(2,1)} %get-tuple-element.61), channel_id=1, source_target_pairs={{0,1},{1,0},{4,5},{5,4},{8,9},{9,8},{12,13},{13,12},{16,17},{17,16... | collective-permute-start | bytes 786440 | tf_op jit(solution)/shard_map/ppermute | solution.py:614
  80.0 11.7 %collective-permute-start.20 = (bf16[128,1024]{1,0:T(8,128)(2,1)S(1)}, bf16[128,1024]{1,0:T(8,128)(2,1)S(1)}, u32[]{:S(2)}, u32[]{:S(2)}) collective-permute-start(bf16[128,1024]{1,0:T(8,128)(2,1)S(1)} %get-tuple-element.59), channel_id=1, source_target_pairs={{0,1},{1,0},{4,5},{5,4},{8,9},{9,8},{12,13},{13,12},{16,17},{17,16... | collective-permute-start | bytes 786440 | tf_op jit(solution)/shard_map/ppermute | solution.py:614
  84.3 10.2 %collective-permute-start.17 = (bf16[128,1024]{1,0:T(8,128)(2,1)S(1)}, bf16[128,1024]{1,0:T(8,128)(2,1)S(1)}, u32[]{:S(2)}, u32[]{:S(2)}) collective-permute-start(bf16[128,1024]{1,0:T(8,128)(2,1)S(1)} %get-tuple-element.57), channel_id=1, source_target_pairs={{0,1},{1,0},{4,5},{5,4},{8,9},{9,8},{12,13},{13,12},{16,17},{17,16... | collective-permute-start | bytes 786440 | tf_op jit(solution)/shard_map/ppermute | solution.py:614
  88.7 4.4 %collective-permute-start.14 = (bf16[128,1024]{1,0:T(8,128)(2,1)S(1)}, bf16[128,1024]{1,0:T(8,128)(2,1)S(1)}, u32[]{:S(2)}, u32[]{:S(2)}) collective-permute-start(bf16[128,1024]{1,0:T(8,128)(2,1)S(1)} %get-tuple-element.55), channel_id=1, source_target_pairs={{0,1},{1,0},{4,5},{5,4},{8,9},{9,8},{12,13},{13,12},{16,17},{17,16... | collective-permute-start | bytes 786440 | tf_op jit(solution)/shard_map/ppermute | solution.py:614
  90.4 46.1 %copy-start.74 = (bf16[128,1024]{1,0:T(8,128)(2,1)}, bf16[128,1024]{1,0:T(8,128)(2,1)S(1)}, u32[]{:S(2)}) copy-start(bf16[128,1024]{1,0:T(8,128)(2,1)S(1)} %add_convert_fusion.6) | copy-start | bytes 786436
  90.4 25.6 %collective-permute-start.24 = (bf16[128,1024]{1,0:T(8,128)(2,1)S(1)}, bf16[128,1024]{1,0:T(8,128)(2,1)}, u32[]{:S(2)}, u32[]{:S(2)}) collective-permute-start(bf16[128,1024]{1,0:T(8,128)(2,1)S(1)} %add_convert_fusion.6), channel_id=1, source_target_pairs={{1,2},{5,6},{9,10},{13,14},{17,18},{21,22},{25,26},{29,30}} | collective-permute-start | bytes 786440 | tf_op jit(solution)/shard_map/ppermute | solution.py:618
  91.8 49.2 %copy-start.76 = (bf16[128,1024]{1,0:T(8,128)(2,1)}, bf16[128,1024]{1,0:T(8,128)(2,1)S(1)}, u32[]{:S(2)}) copy-start(bf16[128,1024]{1,0:T(8,128)(2,1)S(1)} %add_convert_fusion.7) | copy-start | bytes 786436
  91.8 37.4 %collective-permute-start.21 = (bf16[128,1024]{1,0:T(8,128)(2,1)S(1)}, bf16[128,1024]{1,0:T(8,128)(2,1)}, u32[]{:S(2)}, u32[]{:S(2)}) collective-permute-start(bf16[128,1024]{1,0:T(8,128)(2,1)S(1)} %add_convert_fusion.7), channel_id=1, source_target_pairs={{1,2},{5,6},{9,10},{13,14},{17,18},{21,22},{25,26},{29,30}} | collective-permute-start | bytes 786440 | tf_op jit(solution)/shard_map/ppermute | solution.py:618
  93.2 49.6 %copy-start.78 = (bf16[128,1024]{1,0:T(8,128)(2,1)}, bf16[128,1024]{1,0:T(8,128)(2,1)S(1)}, u32[]{:S(2)}) copy-start(bf16[128,1024]{1,0:T(8,128)(2,1)S(1)} %add_convert_fusion.9) | copy-start | bytes 786436
  93.2 34.0 %collective-permute-start.15 = (bf16[128,1024]{1,0:T(8,128)(2,1)S(1)}, bf16[128,1024]{1,0:T(8,128)(2,1)}, u32[]{:S(2)}, u32[]{:S(2)}) collective-permute-start(bf16[128,1024]{1,0:T(8,128)(2,1)S(1)} %add_convert_fusion.9), channel_id=1, source_target_pairs={{1,2},{5,6},{9,10},{13,14},{17,18},{21,22},{25,26},{29,30}} | collective-permute-start | bytes 786440 | tf_op jit(solution)/shard_map/ppermute | solution.py:618
  94.6 48.2 %copy-start.80 = (bf16[128,1024]{1,0:T(8,128)(2,1)}, bf16[128,1024]{1,0:T(8,128)(2,1)S(1)}, u32[]{:S(2)}) copy-start(bf16[128,1024]{1,0:T(8,128)(2,1)S(1)} %add_convert_fusion.8) | copy-start | bytes 786436
  94.6 36.6 %collective-permute-start.18 = (bf16[128,1024]{1,0:T(8,128)(2,1)S(1)}, bf16[128,1024]{1,0:T(8,128)(2,1)}, u32[]{:S(2)}, u32[]{:S(2)}) collective-permute-start(bf16[128,1024]{1,0:T(8,128)(2,1)S(1)} %add_convert_fusion.8), channel_id=1, source_target_pairs={{1,2},{5,6},{9,10},{13,14},{17,18},{21,22},{25,26},{29,30}} | collective-permute-start | bytes 786440 | tf_op jit(solution)/shard_map/ppermute | solution.py:618
  116.0 16.5 %collective-permute-start.25 = (bf16[128,1024]{1,0:T(8,128)(2,1)}, bf16[128,1024]{1,0:T(8,128)(2,1)}, u32[]{:S(2)}, u32[]{:S(2)}) collective-permute-start(bf16[128,1024]{1,0:T(8,128)(2,1)} %collective-permute-done.24), channel_id=1, source_target_pairs={{2,3},{6,7},{10,11},{14,15},{18,19},{22,23},{26,27},{30,31}} | collective-permute-start | bytes 786440 | tf_op jit(solution)/shard_map/ppermute | solution.py:619
  127.2 8.3 %collective-permute-start.16 = (bf16[128,1024]{1,0:T(8,128)(2,1)}, bf16[128,1024]{1,0:T(8,128)(2,1)}, u32[]{:S(2)}, u32[]{:S(2)}) collective-permute-start(bf16[128,1024]{1,0:T(8,128)(2,1)} %collective-permute-done.15), channel_id=1, source_target_pairs={{2,3},{6,7},{10,11},{14,15},{18,19},{22,23},{26,27},{30,31}} | collective-permute-start | bytes 786440 | tf_op jit(solution)/shard_map/ppermute | solution.py:619
  129.2 10.8 %collective-permute-start.22 = (bf16[128,1024]{1,0:T(8,128)(2,1)}, bf16[128,1024]{1,0:T(8,128)(2,1)S(1)}, u32[]{:S(2)}, u32[]{:S(2)}) collective-permute-start(bf16[128,1024]{1,0:T(8,128)(2,1)} %collective-permute-done.21), channel_id=1, source_target_pairs={{2,3},{6,7},{10,11},{14,15},{18,19},{22,23},{26,27},{30,31}} | collective-permute-start | bytes 786440 | tf_op jit(solution)/shard_map/ppermute | solution.py:619
  131.2 11.6 %collective-permute-start.19 = (bf16[128,1024]{1,0:T(8,128)(2,1)}, bf16[128,1024]{1,0:T(8,128)(2,1)S(1)}, u32[]{:S(2)}, u32[]{:S(2)}) collective-permute-start(bf16[128,1024]{1,0:T(8,128)(2,1)} %collective-permute-done.18), channel_id=1, source_target_pairs={{2,3},{6,7},{10,11},{14,15},{18,19},{22,23},{26,27},{30,31}} | collective-permute-start | bytes 786440 | tf_op jit(solution)/shard_map/ppermute | solution.py:619
  136.6 7.3 %collective-permute-start.26 = (bf16[16,1024]{1,0:T(8,128)(2,1)S(1)}, bf16[16,1024]{1,0:T(8,128)(2,1)S(1)}, u32[]{:S(2)}, u32[]{:S(2)}) collective-permute-start(bf16[16,1024]{1,0:T(8,128)(2,1)S(1)} %slice_select_fusion.4), channel_id=1, source_target_pairs={{2,6},{6,10},{10,14},{14,18},{18,22},{22,26},{26,30},{7,3},{11,7},... | collective-permute-start | bytes 98312 | tf_op jit(solution)/shard_map/ppermute | solution.py:576
  156.4 28.5 %copy-start.5 = (bf16[4,128,2048]{2,1,0:T(8,128)(2,1)}, bf16[4,128,2048]{2,1,0:T(8,128)(2,1)S(1)}, u32[]{:S(2)}) copy-start(bf16[4,128,2048]{2,1,0:T(8,128)(2,1)S(1)} %get-tuple-element.71.local) | copy-start | bytes 6291460
  156.4 28.5 %copy-start.40 = (bf16[512,128]{1,0:T(8,128)(2,1)}, bf16[512,128]{1,0:T(8,128)(2,1)S(1)}, u32[]{:S(2)}) copy-start(bf16[512,128]{1,0:T(8,128)(2,1)S(1)} %get-tuple-element.65.c_rows) | copy-start | bytes 393220
  156.4 4.0 %collective-permute-start.27 = (bf16[144,2048]{1,0:T(8,128)(2,1)S(1)}, bf16[144,2048]{1,0:T(8,128)(2,1)S(1)}, u32[]{:S(2)}, u32[]{:S(2)}) collective-permute-start(bf16[144,2048]{1,0:T(8,128)(2,1)S(1)} %get-tuple-element.72), channel_id=1, source_target_pairs={{2,6},{6,2},{10,14},{14,10},{18,22},{22,18},{26,30},{30,26},{3,7},... | collective-permute-start | bytes 1769480 | tf_op jit(solution)/shard_map/ppermute | solution.py:473
  160.8 12.0 %collective-permute-start.30 = (bf16[144,1024]{1,0:T(8,128)(2,1)S(1)}, bf16[144,1024]{1,0:T(8,128)(2,1)S(1)}, u32[]{:S(2)}, u32[]{:S(2)}) collective-permute-start(bf16[144,1024]{1,0:T(8,128)(2,1)S(1)} %maximum_maximum_fusion.1), channel_id=1, source_target_pairs={{2,10},{6,14},{18,26},{22,30},{11,3},{15,7},{27,19},{31,23}} | collective-permute-start | bytes 884744 | tf_op jit(solution)/shard_map/ppermute | solution.py:482
  163.4 17.0 %collective-permute-start.29 = (bf16[144,1024]{1,0:T(8,128)(2,1)S(1)}, bf16[144,1024]{1,0:T(8,128)(2,1)S(1)}, u32[]{:S(2)}, u32[]{:S(2)}) collective-permute-start(bf16[144,1024]{1,0:T(8,128)(2,1)S(1)} %maximum_maximum_fusion.1), channel_id=1, source_target_pairs={{2,18},{6,22},{10,26},{14,30},{19,3},{23,7},{27,11},{31,15}} | collective-permute-start | bytes 884744 | tf_op jit(solution)/shard_map/ppermute | solution.py:482
  164.7 15.7 %collective-permute-start.28 = (bf16[144,1024]{1,0:T(8,128)(2,1)S(1)}, bf16[144,1024]{1,0:T(8,128)(2,1)S(1)}, u32[]{:S(2)}, u32[]{:S(2)}) collective-permute-start(bf16[144,1024]{1,0:T(8,128)(2,1)S(1)} %maximum_maximum_fusion.1), channel_id=1, source_target_pairs={{2,26},{6,30},{10,18},{14,22},{19,11},{23,15},{27,3},{31,7}} | collective-permute-start | bytes 884744 | tf_op jit(solution)/shard_map/ppermute | solution.py:482
  181.0 3.6 %collective-permute-start.31 = (bf16[128,1024]{1,0:T(8,128)(2,1)S(1)}, bf16[128,1024]{1,0:T(8,128)(2,1)S(1)}, u32[]{:S(2)}, u32[]{:S(2)}) collective-permute-start(bf16[128,1024]{1,0:T(8,128)(2,1)S(1)} %fusion.19), channel_id=1, source_target_pairs={{2,6},{6,2},{10,14},{14,10},{18,22},{22,18},{26,30},{30,26},{3,7},... | collective-permute-start | bytes 786440 | tf_op jit(solution)/shard_map/ppermute | solution.py:473
  191.3 31.8 %collective-permute-start.35 = (bf16[128,1024]{1,0:T(8,128)(2,1)}, bf16[128,1024]{1,0:T(8,128)(2,1)}, u32[]{:S(2)}, u32[]{:S(2)}) collective-permute-start(bf16[128,1024]{1,0:T(8,128)(2,1)} %get-tuple-element.80), channel_id=1, source_target_pairs={{2,3},{3,2},{6,7},{7,6},{10,11},{11,10},{14,15},{15,14},{18,19},{1... | collective-permute-start | bytes 786440 | tf_op jit(solution)/shard_map/ppermute | solution.py:614
  206.1 18.2 %collective-permute-start.34 = (bf16[128,1024]{1,0:T(8,128)(2,1)S(1)}, bf16[128,1024]{1,0:T(8,128)(2,1)S(1)}, u32[]{:S(2)}, u32[]{:S(2)}) collective-permute-start(bf16[128,1024]{1,0:T(8,128)(2,1)S(1)} %get-tuple-element.78), channel_id=1, source_target_pairs={{2,3},{3,2},{6,7},{7,6},{10,11},{11,10},{14,15},{15,14},{18,19},{1... | collective-permute-start | bytes 786440 | tf_op jit(solution)/shard_map/ppermute | solution.py:614
  213.6 10.8 %collective-permute-start.33 = (bf16[128,1024]{1,0:T(8,128)(2,1)S(1)}, bf16[128,1024]{1,0:T(8,128)(2,1)S(1)}, u32[]{:S(2)}, u32[]{:S(2)}) collective-permute-start(bf16[128,1024]{1,0:T(8,128)(2,1)S(1)} %get-tuple-element.76), channel_id=1, source_target_pairs={{2,3},{3,2},{6,7},{7,6},{10,11},{11,10},{14,15},{15,14},{18,19},{1... | collective-permute-start | bytes 786440 | tf_op jit(solution)/shard_map/ppermute | solution.py:614
  219.3 9.8 %collective-permute-start.32 = (bf16[128,1024]{1,0:T(8,128)(2,1)S(1)}, bf16[128,1024]{1,0:T(8,128)(2,1)S(1)}, u32[]{:S(2)}, u32[]{:S(2)}) collective-permute-start(bf16[128,1024]{1,0:T(8,128)(2,1)S(1)} %get-tuple-element.74), channel_id=1, source_target_pairs={{2,3},{3,2},{6,7},{7,6},{10,11},{11,10},{14,15},{15,14},{18,19},{1... | collective-permute-start | bytes 786440 | tf_op jit(solution)/shard_map/ppermute | solution.py:614
  (73 other events, 347.5 us)

commit v2 on v1

v2 whole, which is shorter than its diff:
```python
import functools

import jax
import jax.numpy as jnp
import numpy as np
from jax import lax
from jax.experimental import pallas as pl
from jax.experimental.pallas import tpu as pltpu
from jax.sharding import PartitionSpec as P

EPSILON = 1e-05
CHUNK = 128
WIDTH = 512
HALO = 16
LIMIT = 36 * 2**20
SMALL = 8 * 2**20
SKEW = 2
REVERSE, UPPER, FIRST, RANKS = 0, 1, 2, 3
LOG2E = 1.4426950408889634
F32 = jnp.float32
BF16 = jnp.bfloat16


def silu(value):
    half = 0.5 * value
    return half + half * jnp.tanh(half)


def dot(left, right):
    return jnp.dot(left, right, preferred_element_type=F32)


def order_matrix(size, reverse):
    row = lax.broadcasted_iota(jnp.int32, (size, size), 0)
    column = lax.broadcasted_iota(jnp.int32, (size, size), 1)
    target = jnp.where(reverse == 1, size - 1 - row, row)
    return jnp.where(column == target, 1.0, 0.0).astype(BF16)


def high_low(value):
    high = value.astype(BF16)
    low = (value - high.astype(F32)).astype(BF16)
    return jnp.concatenate([high, low], axis=1)


def norm_block(values, gain_row):
    widened = values.astype(F32)
    inverse_rms = lax.rsqrt(jnp.mean(widened * widened, axis=-1, keepdims=True) + EPSILON)
    return (widened * inverse_rms * gain_row).astype(BF16)


def prep_kernel(
    info,
    rows,
    halo,
    gain,
    wide,
    side_weight,
    taps,
    side_taps,
    bias,
    decay,
    spread,
    normed_out,
    x_out,
    b_out,
    c_out,
    cum_out,
    shifted_out,
    reach_out,
    local_out,
    state_out,
    extended,
    buffer,
    turned,
    shares,
    wide_shares,
    running,
):
    step_index = pl.program_id(0)
    reverse = info[REVERSE]
    length = rows.shape[0]
    heads = bias.shape[1]
    state = b_out.shape[1]
    chunks = length // CHUNK
    margin = taps.shape[0] - 1
    width = wide.shape[1]

    def filtered(kernel, start, size, lanes):
        total = None
        for k in range(margin + 1):
            part = buffer[HALO - margin + k + start : HALO - margin + k + start + size, lanes]
            term = kernel[k : k + 1, lanes] * part
            total = term if total is None else total + term
        return silu(total).astype(BF16)

    @pl.when(step_index == 0)
    def _():
        turn = order_matrix(2 * CHUNK, reverse)
        small_turn = order_matrix(HALO, reverse)
        edge = norm_block(halo[...], gain[...])
        extended[0:HALO] = dot(small_turn, edge).astype(BF16)
        pairs = length // (2 * CHUNK)
        for pair in range(pairs):
            source = jnp.where(reverse == 1, pairs - 1 - pair, pair) * (2 * CHUNK)
            source = pl.multiple_of(source, 2 * CHUNK)
            piece = norm_block(rows[pl.ds(source, 2 * CHUNK), :], gain[...])
            start = HALO + pair * 2 * CHUNK
            extended[start : start + 2 * CHUNK] = dot(turn, piece).astype(BF16)
        normed_out[...] = extended[HALO:]
        side = dot(extended[...], side_weight[...]).astype(BF16).astype(F32)
        buffer[:, 0 : 2 * state] = side[:, 0 : 2 * state]
        raw = side[HALO:, 2 * state :] + bias[...]
        step = jnp.maximum(raw, 0.0) + jnp.log1p(jnp.exp(-jnp.abs(raw)))
        change = step * (decay[...] * (-LOG2E))
        row = lax.broadcasted_iota(jnp.int32, (CHUNK, CHUNK), 0)
        column = lax.broadcasted_iota(jnp.int32, (CHUNK, CHUNK), 1)
        triangle = jnp.where(row >= column, 1.0, 0.0).astype(F32)
        before = jnp.zeros((1, heads), F32)
        totals = []
        befores = []
        for c in range(chunks):
            here = slice(c * CHUNK, (c + 1) * CHUNK)
            cumulative = jnp.dot(
                triangle, change[here], preferred_element_type=F32, precision=lax.Precision.HIGHEST
            )
            last = cumulative[CHUNK - 1 :, :]
            befores.append(before)
            totals.append(last)
            before = before + last
            moved = cumulative - jnp.log2(step[here])
            blank = jnp.zeros((CHUNK, 128 - 2 * heads), F32)
            flipped = jnp.concatenate([cumulative, moved, blank], axis=1).T
            cum_out[:, here] = flipped[0:heads]
            shifted_out[:, here] = flipped[heads : 2 * heads]
            shares[here, :] = high_low(jnp.exp2(last - cumulative) * step[here])
            reach_out[here, :] = high_low(jnp.exp2(cumulative))
        befores.append(before)
        zero_rows = jnp.zeros((HALO - chunks, heads), F32)
        shares[length:, :] = high_low(jnp.exp2(jnp.concatenate(totals + [zero_rows], axis=0)))
        zero_rows = jnp.zeros((HALO - chunks - 1, heads), F32)
        reach_out[length:, :] = high_low(jnp.exp2(jnp.concatenate(befores + [zero_rows], axis=0)))
        for c in range(chunks):
            start = c * CHUNK
            here = slice(start, start + CHUNK)
            in_part = filtered(side_taps, start, CHUNK, slice(0, state))
            b_out[here] = in_part
            turned[:, here] = in_part.astype(F32).T.astype(BF16)
            c_out[here] = filtered(side_taps, start, CHUNK, slice(state, 2 * state))

    buffer[...] = dot(extended[...], wide[...]).astype(BF16).astype(F32)
    wide_shares[...] = dot(shares[...], spread[...])
    sub = 64
    running[...] = jnp.zeros_like(running)
    for c in range(chunks):
        here = slice(c * CHUNK, (c + 1) * CHUNK)
        for lane in range(0, width, 256):
            lanes = slice(lane, lane + 256)
            weighted = []
            for start in range(c * CHUNK, (c + 1) * CHUNK, sub):
                piece = filtered(taps, start, sub, lanes)
                x_out[start : start + sub, lanes] = piece
                weighted.append(
                    (piece.astype(F32) * wide_shares[start : start + sub, lanes]).astype(BF16)
                )
            states = dot(turned[:, here], jnp.concatenate(weighted, axis=0))
            entering = running[:, lanes]
            local_out[c, :, lanes] = entering.astype(BF16)
            total = wide_shares[length + c : length + c + 1, lanes]
            running[:, lanes] = total * entering + states
    state_out[0:state, :] = running[...].astype(BF16)
    through = wide_shares[length : length + 1, :]
    for c in range(1, chunks):
        through = through * wide_shares[length + c : length + c + 1, :]
    high = through.astype(BF16)
    low = (through - high.astype(F32)).astype(BF16)
    tail = jnp.concatenate(
        [high.astype(F32), low.astype(F32), jnp.zeros((HALO - 2, width), F32)], axis=0
    )
    state_out[state:, :] = tail.astype(BF16)


def mid_kernel(normed, gate_weight, x, b, c_rows, cumulative, shifted, skip, y_out, gate_out, scores):
    step_index = pl.program_id(0)
    length = x.shape[0]
    chunks = length // CHUNK
    heads_here = cumulative.shape[0]
    head_dim = x.shape[1] // heads_here
    row = lax.broadcasted_iota(jnp.int32, (CHUNK, CHUNK), 0)
    column = lax.broadcasted_iota(jnp.int32, (CHUNK, CHUNK), 1)
    causal = row >= column
    lane = lax.broadcasted_iota(jnp.int32, (CHUNK, 2 * head_dim), 1)

    @pl.when(step_index == 0)
    def _():
        for c in range(chunks):
            here = slice(c * CHUNK, (c + 1) * CHUNK)
            scores[here, :] = lax.dot_general(
                c_rows[here, :], b[here, :], (((1,), (1,)), ((), ())), preferred_element_type=F32
            )

    gate_out[...] = dot(normed[...], gate_weight[...]).astype(BF16)
    for c in range(chunks):
        here = slice(c * CHUNK, (c + 1) * CHUNK)
        score = scores[here, :]
        blank = jnp.zeros((128 - heads_here, CHUNK), F32)
        columns = jnp.concatenate([cumulative[:, here], blank], axis=0).T
        for pair in range(heads_here // 2):
            lanes = slice(2 * pair * head_dim, (2 * pair + 2) * head_dim)
            parts = []
            for h in (2 * pair, 2 * pair + 1):
                gap = columns[:, h : h + 1] - shifted[h : h + 1, here]
                parts.append((score * jnp.exp2(jnp.where(causal, gap, -jnp.inf))).astype(BF16))
            values = x[here, lanes]
            zero = jnp.zeros_like(values)
            stacked = jnp.concatenate(
                [jnp.where(lane < head_dim, values, zero), jnp.where(lane < head_dim, zero, values)],
                axis=0,
            )
            within = dot(jnp.concatenate(parts, axis=1), stacked)
            y_out[here, lanes] = within + skip[:, lanes] * values.astype(F32)


def finish_kernel(
    count,
    mode,
    info,
    rows,
    y,
    gate,
    c_rows,
    reach,
    reach_tail,
    local,
    mine,
    other,
    partner,
    gain,
    spread,
    weight_far,
    *rest,
):
    outs = rest[:-4]
    normed, entering, weight, arrived = rest[-4:]
    step_index = pl.program_id(0)
    steps = pl.num_programs(0)
    reverse = info[REVERSE]
    size, inner = y.shape
    parts = size // CHUNK
    state = mine.shape[0]
    fetch = pltpu.make_async_copy(weight_far, weight, arrived)

    @pl.when(step_index == 0)
    def _():
        fetch.start()
        half = inner // 2
        upper = info[UPPER] == 1
        first = info[FIRST] == 1
        for start in range(0, inner, 256):
            lanes = slice(start, start + 256)
            inside = slice(start % half, start % half + 256)
            pair = (other, mine) if start < half else (mine, other)
            full = jnp.where(upper, pair[0][:, inside], pair[1][:, inside])
            tail = partner[state:, lanes].astype(F32)
            through = tail[0:1] + tail[1:2]
            moved = (through * full.astype(F32) + partner[:state, lanes].astype(F32)).astype(BF16)
            entering[:, lanes] = jnp.where(first, full, moved)

    position = jnp.where(reverse == 1, steps - 1 - step_index, step_index)
    tail = dot(reach_tail[...], spread[...])
    index_row = lax.broadcasted_iota(jnp.int32, (HALO, 1), 0)
    turn = order_matrix(size, reverse)
    block = 256
    befores = [
        jnp.sum(jnp.where(index_row == position * parts + p, tail, 0.0), axis=0, keepdims=True)
        for p in range(parts)
    ]
    squares = [jnp.zeros((CHUNK, 1), F32) for _ in range(parts)]
    gated = {}
    for start in range(0, inner, block):
        lanes = slice(start, start + block)
        for p in range(parts):
            here = slice(p * CHUNK, (p + 1) * CHUNK)
            full = local[p, :, lanes].astype(F32) + befores[p][:, lanes] * entering[:, lanes].astype(F32)
            carried = dot(c_rows[here, :], full.astype(BF16)) * dot(reach[here, :], spread[:, lanes])
            part = (y[here, lanes] + carried) * silu(gate[here, lanes].astype(F32))
            squares[p] = squares[p] + jnp.sum(part * part, axis=-1, keepdims=True)
            gated[p, start] = part
    inverse_rms = [lax.rsqrt(total * (1.0 / inner) + EPSILON) for total in squares]
    for start in range(0, inner, block):
        lanes = slice(start, start + block)
        piece = jnp.concatenate(
            [(gated[p, start] * inverse_rms[p] * gain[:, lanes]).astype(BF16) for p in range(parts)],
            axis=0,
        )
        piece = dot(turn, piece).astype(BF16)
        normed[:, lanes] = piece

    @pl.when(step_index == 0)
    def _():
        fetch.wait()

    total = dot(normed[...], weight[...])
    base = rows[...].astype(F32) + total
    if mode[0] == "exchange":
        earlier = outs[:count]
        sent = outs[count : 2 * count]
        outs[2 * count][...] = base
        for k in range(count):

            @pl.when(step_index == k // parts)
            def _(k=k):
                start = k % parts * CHUNK
                mine_now = total[start : start + CHUNK].astype(BF16)
                sent[k][...] = jnp.where(info[mode[1]] == 1, earlier[k][...], mine_now)

        return
    order, skew, place_slot = mode
    place = info[place_slot]

    @pl.when(step_index == 0)
    def _():
        for out in outs:
            out[...] = jnp.zeros_like(out)

    for k, index in enumerate(order):
        start = index % parts * CHUNK
        here = slice(start, start + CHUNK)

        @pl.when((step_index == index // parts) & (place == 0))
        def _(k=k, here=here):
            outs[k][...] = total[here].astype(outs[k].dtype)

        @pl.when((step_index == index // parts) & (place == 1))
        def _(k=k, here=here):
            outs[k + skew][...] = base[here]


def kept(shape, dtype):
    return pltpu.VMEM(shape, dtype)


def near(*values):
    return tuple(pltpu.with_memory_space_constraint(v, pltpu.VMEM) for v in values)


def far(value):
    return pltpu.with_memory_space_constraint(value, pltpu.HBM)


def whole_block(shape):
    return pl.BlockSpec(shape, lambda *_: (0,) * len(shape))


def prep(info, rows, halo, gain, main, side, conv, bias, decay, spread, inner, state):
    length, features = rows.shape
    heads = bias.shape[1]
    steps = inner // WIDTH
    chunks = length // CHUNK
    margin = conv.shape[1]
    side_taps = conv[0, :, inner:]
    grid_spec = pltpu.PrefetchScalarGridSpec(
        num_scalar_prefetch=1,
        grid=(steps,),
        in_specs=[
            whole_block((length, features)),
            whole_block((HALO, features)),
            whole_block((1, features)),
            pl.BlockSpec((None, features, WIDTH), lambda j, _: (0, 0, steps + j)),
            pl.BlockSpec((None, features, side.shape[2]), lambda j, _: (0, 0, 0)),
            pl.BlockSpec((None, margin, WIDTH), lambda j, _: (0, 0, j)),
            whole_block(side_taps.shape),
            whole_block((1, heads)),
            whole_block((1, heads)),
            pl.BlockSpec((2 * heads, WIDTH), lambda j, _: (0, j)),
        ],
        out_specs=[
            whole_block((length, features)),
            pl.BlockSpec((length, WIDTH), lambda j, _: (0, j)),
            whole_block((length, state)),
            whole_block((length, state)),
            whole_block((heads, length)),
            whole_block((heads, length)),
            whole_block((length + HALO, 2 * heads)),
            pl.BlockSpec((chunks, state, WIDTH), lambda j, _: (0, 0, j)),
            pl.BlockSpec((state + HALO, WIDTH), lambda j, _: (0, j)),
        ],
        scratch_shapes=[
            pltpu.VMEM((length + HALO, features), BF16),
            pltpu.VMEM((length + HALO, WIDTH), F32),
            pltpu.VMEM((state, length), BF16),
            pltpu.VMEM((length + HALO, 2 * heads), BF16),
            pltpu.VMEM((length + HALO, WIDTH), F32),
            pltpu.VMEM((state, WIDTH), F32),
        ],
    )
    shape = jax.ShapeDtypeStruct
    return pl.pallas_call(
        prep_kernel,
        grid_spec=grid_spec,
        out_shape=[
            kept((length, features), BF16),
            kept((length, inner), BF16),
            kept((length, state), BF16),
            kept((length, state), BF16),
            kept((heads, length), F32),
            kept((heads, length), F32),
            kept((length + HALO, 2 * heads), BF16),
            kept((chunks, state, inner), BF16),
            shape((state + HALO, inner), BF16),
        ],
        compiler_params=pltpu.CompilerParams(
            vmem_limit_bytes=LIMIT, dimension_semantics=("arbitrary",)
        ),
        cost_estimate=pl.CostEstimate(
            flops=2 * length * features * inner, bytes_accessed=12 * 2**20, transcendentals=0
        ),
        name="prep",
    )(info, rows, halo, gain, far(main), side, conv, side_taps, bias, decay, spread)


def mid(normed, main, x, b, c_rows, cumulative, shifted, skip, inner):
    length, features = normed.shape
    state = b.shape[1]
    steps = inner // WIDTH
    heads_here = cumulative.shape[0] // steps
    return pl.pallas_call(
        mid_kernel,
        grid=(steps,),
        in_specs=[
            whole_block((length, features)),
            pl.BlockSpec((None, features, WIDTH), lambda j: (0, 0, j)),
            pl.BlockSpec((length, WIDTH), lambda j: (0, j)),
            whole_block((length, state)),
            whole_block((length, state)),
            pl.BlockSpec((heads_here, length), lambda j: (j, 0)),
            pl.BlockSpec((heads_here, length), lambda j: (j, 0)),
            pl.BlockSpec((1, WIDTH), lambda j: (0, j)),
        ],
        out_specs=[
            pl.BlockSpec((length, WIDTH), lambda j: (0, j)),
            pl.BlockSpec((length, WIDTH), lambda j: (0, j)),
        ],
        out_shape=[
            kept((length, inner), F32),
            kept((length, inner), BF16),
        ],
        scratch_shapes=[pltpu.VMEM((length, CHUNK), F32)],
        compiler_params=pltpu.CompilerParams(
            vmem_limit_bytes=LIMIT, dimension_semantics=("arbitrary",)
        ),
        cost_estimate=pl.CostEstimate(
            flops=2 * length * features * inner, bytes_accessed=12 * 2**20, transcendentals=0
        ),
        name="mid",
    )(*near(normed), far(main), *near(x, b, c_rows, cumulative, shifted), skip)


def finish(mode, info, rows, y, gate, c_rows, reach, local, state_parts, gain, spread, weight, earlier):
    features = rows.shape[1]
    length, inner = y.shape
    state = c_rows.shape[1]
    mine, other, partner = state_parts
    reach_width = reach.shape[1]
    tail = length // HALO
    size = 2 * CHUNK
    steps = length // size
    chunks = length // CHUNK

    if mode[0] == "exchange":
        out_specs = [whole_block((CHUNK, features))] * chunks
        out_specs = out_specs + [pl.BlockSpec((size, features), lambda j, s: (j, 0))]
        out_shape = [jax.ShapeDtypeStruct((CHUNK, features), BF16)] * chunks
        out_shape = out_shape + [kept((length, features), F32)]
    else:
        skew = mode[1]
        out_specs = [whole_block((CHUNK, features))] * (chunks + skew)
        out_shape = [jax.ShapeDtypeStruct((CHUNK, features), BF16)] * skew
        out_shape = out_shape + [kept((CHUNK, features), F32)] * chunks

    def turned_block(shape):
        def place(j, s):
            return (jnp.where(s[0] == 1, steps - 1 - j, j),) + (0,) * (len(shape) - 1)

        return pl.BlockSpec(shape, place)

    grid_spec = pltpu.PrefetchScalarGridSpec(
        num_scalar_prefetch=1,
        grid=(steps,),
        in_specs=[
            pl.BlockSpec((size, features), lambda j, s: (j, 0)),
            turned_block((size, inner)),
            turned_block((size, inner)),
            turned_block((size, state)),
            turned_block((size, reach_width)),
            pl.BlockSpec((HALO, reach_width), lambda j, s: (tail, 0)),
            turned_block((size // CHUNK, state, inner)),
            whole_block(mine.shape),
            whole_block(other.shape),
            whole_block(partner.shape),
            whole_block((1, inner)),
            whole_block(spread.shape),
            pl.BlockSpec(memory_space=pl.ANY),
        ]
        + [whole_block(value.shape) for value in earlier],
        out_specs=out_specs,
        scratch_shapes=[
            pltpu.VMEM((size, inner), BF16),
            pltpu.VMEM((state, inner), BF16),
            pltpu.VMEM(weight.shape, BF16),
            pltpu.SemaphoreType.DMA,
        ],
    )
    return pl.pallas_call(
        functools.partial(finish_kernel, chunks, mode),
        grid_spec=grid_spec,
        out_shape=out_shape,
        compiler_params=pltpu.CompilerParams(
            vmem_limit_bytes=LIMIT, dimension_semantics=("arbitrary",)
        ),
        cost_estimate=pl.CostEstimate(
            flops=2 * length * features * inner, bytes_accessed=16 * 2**20, transcendentals=0
        ),
        name="finish",
    )(
        info, rows, *near(y, gate, c_rows, reach, reach, local), mine, other, partner,
        gain, spread, far(weight), *earlier,
    )


def split_state(packed):
    state = packed.shape[0] - HALO
    values = packed[:state].astype(F32)
    tail = packed[state:].astype(F32)
    return values, tail[0:1] + tail[1:2]


def joined_state(values, through):
    high = through.astype(BF16)
    low = (through - high.astype(F32)).astype(BF16)
    rest = jnp.zeros((HALO - 2, through.shape[1]), F32)
    tail = jnp.concatenate([high.astype(F32), low.astype(F32), rest], axis=0)
    return values.astype(BF16), tail.astype(BF16)


def after(earlier, later):
    return later[1] * earlier[0] + later[0], earlier[1] * later[1]


def chosen(condition, first, second):
    return tuple(jnp.where(condition, a, b) for a, b in zip(first, second))


def pair_kernel(info, mine, partner, out):
    half = out.shape[1]
    first = info[FIRST] == 1
    state = out.shape[0] - HALO
    for start in range(0, half, 256):
        place = pl.multiple_of(info[UPPER] * half + start, 256)
        one = split_state(mine[:, pl.ds(place, 256)])
        two = split_state(partner[:, pl.ds(place, 256)])
        total = after(chosen(first, one, two), chosen(first, two, one))
        out[:state, start : start + 256], out[state:, start : start + 256] = joined_state(*total)


def merge_kernel(group, slot, has_entering, last, info, *refs):
    members = refs[: 2**group]
    entering_out = refs[2**group + has_entering]
    rank = info[slot]
    state, half = entering_out.shape
    for start in range(0, half, 256):
        lanes = slice(start, start + 256)
        values = [split_state(member[:, lanes]) for member in members]
        before = (jnp.zeros((state, 256), F32), jnp.ones((1, 256), F32))
        whole = before
        for place in range(2**group):
            value = values[0]
            for code in range(1, 2**group):
                value = chosen((rank ^ code) == place, values[code], value)
            if place < 2**group - 1:
                before = chosen(place < rank, after(before, value), before)
            if not last:
                whole = after(whole, value)
        if has_entering:
            inside = refs[2**group][:, lanes].astype(F32)
            through = jnp.ones((1, 256), F32)
            before = after(before, (inside, through))
        entering_out[:, lanes] = before[0].astype(BF16)
        if not last:
            out = refs[-1]
            out[:state, lanes], out[state:, lanes] = joined_state(*whole)


def small_call(kernel, name, out_shape, info, *operands):
    return pl.pallas_call(
        kernel,
        in_specs=[pl.BlockSpec(memory_space=pltpu.SMEM)] + [whole_block(v.shape) for v in operands],
        out_specs=[whole_block(v.shape) for v in out_shape],
        out_shape=out_shape,
        compiler_params=pltpu.CompilerParams(vmem_limit_bytes=SMALL),
        cost_estimate=pl.CostEstimate(flops=10**6, bytes_accessed=10**6, transcendentals=0),
        name=name,
    )(info, *operands)


def settle_kernel(place, info, base, sent, other, *rest):
    section = info[place]
    rows = (base[...] + other[...].astype(F32)).astype(BF16)
    rows = jnp.where(section == 1, sent[...], rows)
    rest[-1][...] = jnp.where(section == 0, other[...], rows)


def settle(index, place, info, base, sent, other, finished):
    length, features = base.shape
    block = pl.BlockSpec((CHUNK, features), lambda j: (index, 0))
    out_block = pl.BlockSpec((None, CHUNK, features), lambda j: (0, index, 0))
    passed = [] if finished is None else [finished]
    return pl.pallas_call(
        functools.partial(settle_kernel, place),
        grid=(1,),
        in_specs=[pl.BlockSpec(memory_space=pltpu.SMEM), block]
        + [whole_block((CHUNK, features))] * 2
        + [pl.BlockSpec(memory_space=pl.ANY)] * len(passed),
        out_specs=out_block,
        out_shape=jax.ShapeDtypeStruct((1, length, features), BF16),
        input_output_aliases={4: 0} if passed else {},
        compiler_params=pltpu.CompilerParams(vmem_limit_bytes=SMALL),
        cost_estimate=pl.CostEstimate(flops=10**6, bytes_accessed=10**6, transcendentals=0),
        name="settle",
    )(info, base, sent, other, *passed)


def stages_of(seq_count):
    bits = seq_count.bit_length() - 1
    found = []
    bit = 1
    while bit < bits:
        group = min(2, bits - bit)
        found.append((bit, group))
        bit += group
    return found


def entering_state(packed, info, sections, seq_count, meanwhile):
    section_count = lax.axis_size("section")
    stages = stages_of(seq_count)

    def swap(value, mask):
        pairs = [
            (i * section_count + s, (i ^ mask) * section_count + s)
            for s in sections
            for i in range(seq_count)
        ]
        return lax.ppermute(value, ("seq", "section"), pairs)

    def forward(value, mask, low_bit):
        pairs = []
        for s in sections:
            for i in range(seq_count):
                later = (i ^ mask) >> low_bit > i >> low_bit
                if later == (s % 2 == 0):
                    pairs.append((i * section_count + s, (i ^ mask) * section_count + s))
        return lax.ppermute(value, ("seq", "section"), pairs)

    depth, inner = packed.shape
    half = jax.ShapeDtypeStruct((depth, inner // 2), BF16)
    states = jax.ShapeDtypeStruct((depth - HALO, inner // 2), BF16)
    partner = swap(packed, 1)
    (total,) = small_call(pair_kernel, "pair", [half], info, packed, partner)
    done = meanwhile(total)
    info, _ = lax.optimization_barrier((info, done[0]))
    entering = []
    for index, (bit, group) in enumerate(stages):
        last = index + 1 == len(stages)
        members = [total]
        for code in range(1, 2**group):
            mask = code << bit
            members.append(forward(total, mask, bit) if last else swap(total, mask))
        kernel = functools.partial(merge_kernel, group, RANKS + index, len(entering), last)
        shapes = [states] if last else [states, half]
        results = small_call(kernel, "merge", shapes, info, *members, *entering)
        entering = [results[0]]
        total = results[-1]
    return (entering[0], swap(entering[0], 1), partner), done


def per_device(
    tokens,
    input_gain,
    main_weight,
    side_weight,
    conv_kernel,
    step_bias,
    decay_rate,
    skip_gain,
    output_gain,
    output_weight,
):
    length, features = tokens.shape
    inner = main_weight.shape[2] // 2
    heads = decay_rate.shape[1]
    state = (side_weight.shape[2] - heads) // 2
    head_dim = inner // heads
    chunks = length // CHUNK
    seq_count = lax.axis_size("seq")
    section_count = lax.axis_size("section")
    section_index = lax.axis_index("section")
    seq_index = lax.axis_index("seq")
    reverse = section_index % 2
    weight = lax.all_gather(output_weight[0], "seq", axis=0, tiled=True)
    expand = np.repeat(np.eye(heads, dtype=np.float32), head_dim, axis=1)
    spread = jnp.asarray(np.concatenate([expand, expand], axis=0), BF16)
    skip_row = jnp.repeat(skip_gain, head_dim, axis=1)
    upper = seq_index % 2
    facts = [reverse, upper, (upper == reverse).astype(jnp.int32)]
    for bit, group in stages_of(seq_count):
        position = (seq_index >> bit) % 2**group
        facts.append(jnp.where(reverse == 1, 2**group - 1 - position, position))
    places = len(facts)
    rounds = section_count // 2
    for round_index in range(rounds):
        facts.append(section_index - 2 * round_index)
    info = jnp.stack([fact.astype(jnp.int32) for fact in facts])
    info, skip_row = lax.optimization_barrier((info, skip_row))
    order = [chunks - 1, 0] + list(range(1, chunks - 1))

    def edges(first_rows, last_rows, sections):
        pairs = []
        for s in sections:
            for i in range(seq_count):
                target = i + 1 if s % 2 == 0 else i - 1
                if 0 <= target < seq_count:
                    pairs.append((i * section_count + s, target * section_count + s))
        value = jnp.where(reverse == 1, first_rows, last_rows)
        return lax.ppermute(value, ("seq", "section"), pairs)

    current = tokens
    halo = edges(tokens[:HALO], tokens[length - HALO :], (0, 1))
    previous = None
    for round_index in range(rounds):
        active = (2 * round_index, 2 * round_index + 1)
        normed, x, b, c_rows, cumulative, shifted, reach, local, packed = prep(
            info,
            current,
            halo,
            input_gain,
            main_weight,
            side_weight,
            conv_kernel,
            step_bias,
            decay_rate,
            spread,
            inner,
            state,
        )
        def meanwhile(total):
            ready, _ = lax.optimization_barrier((normed, total))
            return mid(ready, main_weight, x, b, c_rows, cumulative, shifted, skip_row, inner)

        state_parts, (y, gate) = entering_state(packed, info, active, seq_count, meanwhile)
        last_round = round_index + 1 == rounds
        low, high = active
        place = section_index - low
        mode = ("exchange", places) if last_round else (tuple(order), SKEW, places + round_index)
        outs = finish(
            mode, info, current, y, gate, c_rows, reach, local, state_parts,
            output_gain, spread, weight, previous if last_round else [],
        )
        if last_round:
            *sent, base = outs
            break
        hops = 3
        received = []
        values = []
        for step in range(chunks + (hops - 1) * SKEW):
            pairs = [
                (low + hop, low + hop + 1) for hop in range(hops) if 0 <= step - hop * SKEW < chunks
            ]
            if step < SKEW:
                value = outs[step]
            elif step < len(outs):
                value = (outs[step] + received[step - SKEW].astype(F32)).astype(BF16)
            else:
                value = received[step - SKEW]
            values.append(value)
            received.append(lax.ppermute(value, "section", pairs))
        layer_rows = [None] * chunks
        next_rows = [None] * chunks
        for step, index in enumerate(order):
            layer_rows[index] = values[step + SKEW]
            next_rows[index] = jnp.where(place == 3, received[step + 2 * SKEW], received[step + SKEW])
        previous = layer_rows
        halo = edges(
            next_rows[0][:HALO], next_rows[chunks - 1][CHUNK - HALO :], (low + 2, high + 2)
        )
        current = jnp.concatenate(next_rows, axis=0)
    finished = None
    for index in range(chunks):
        other = lax.ppermute(sent[index], "section", [(low, high), (high, low), (1, 0)])
        finished = settle(index, places, info, base, sent[index], other, finished)
    return finished


def solution(mesh):
    placed = (
        P("seq", None),
        P("section", None),
        P("section", None, None),
        P("section", None, None),
        P("section", None, None),
        P("section", None),
        P("section", None),
        P("section", None),
        P("section", None),
        P("section", "seq", None),
    )
    return jax.shard_map(
        per_device, mesh=mesh, in_specs=placed, out_specs=P("section", "seq", None), check_vma=False
    )
```

time: 235 us -> 209 us (0.89)
  local copies, waits for them, and re-layouts: 38.7 us -> 13.1 us
  waiting for transfers between devices: 53.3 us -> 75.5 us
  other arithmetic: 18.7 us -> 3.09 us
  between operations: 1.4 us -> 13.9 us
  starting transfers between devices: 50.3 us -> 39.1 us
  Pallas kernels: 68.2 us -> 62.1 us
    unnamed x172 -> x27, local copies, waits for them, and re-layouts: 35 us -> 11.6 us
    ppermute x24 -> x12, waiting for transfers between devices: 42.2 us -> 53.8 us  [the longest x8 42.4 us: per_device(): received.append(lax.ppermute(value, 'section', pairs))]
    select_n x15 -> x2, other arithmetic: 10.1 us -> 1.99 us  [per_device(): jnp.where(place == 3, received[step + 2 * SKEW], received[step + SKEW])]
    ppermute x24 -> x12, starting transfers between devices: 31.6 us -> 23.5 us  [the longest x8 11.8 us: per_device(): received.append(lax.ppermute(value, 'section', pairs))]
    pallas_call x10 -> x12, Pallas kernels: 55.4 us -> 48.9 us  [the longest x2 25.8 us: prep(): pl.pallas_call(prep_kernel, grid_spec=grid_spec, out_shape=[kept((length,...]
    all_gather x0 -> x1, waiting for transfers between devices: none -> 5.65 us  [per_device(): weight = lax.all_gather(output_weight[0], 'seq', axis=0, tiled=True)]
    ppermute x2, waiting for transfers between devices: 0.01 us -> 3.95 us  [edges(): return lax.ppermute(value, ('seq', 'section'), pairs)]
    convert_element_type x12 -> x4, other arithmetic: 3.61 us -> 0.23 us  [per_device(): value = (outs[step] + received[step - SKEW].astype(F32)).astype(BF16)]
  transfers between devices with their start and end apart: 36 -> 25, of which waited for: 13 -> 13; matrix products, arithmetic and copies ran while one was open for 9% -> 2% of each run, Pallas kernels for 15% -> 15%
where the time goes in v2:
time: 209 us; the launch traced here: 207 us
  waiting for transfers between devices  75.5 us (36%)
  Pallas kernels  62.1 us (30%)
  starting transfers between devices  39.1 us (19%)
  between operations  13.9 us (7%)
  local copies, waits for them, and re-layouts  13.1 us (6%)
  other arithmetic  3.09 us (1%)
    ppermute x8, waiting for transfers between devices, per_device(): received.append(lax.ppermute(value, 'section', pairs))  42.4 us
    pallas_call x2, Pallas kernels, prep(): pl.pallas_call(prep_kernel, grid_spec=grid_spec, out_shape=[kept((length,...  25.8 us
    pallas_call x2, Pallas kernels, finish(): pl.pallas_call(functools.partial(finish_kernel, chunks, mode), grid_spec=...  14.6 us
    pallas_call x2, Pallas kernels, mid(): pl.pallas_call(mid_kernel, grid=(steps,), in_specs=[whole_block((length,...  13.2 us
    ppermute x8, starting transfers between devices, per_device(): received.append(lax.ppermute(value, 'section', pairs))  11.8 us
    ppermute x4, starting transfers between devices, per_device(): lax.ppermute(sent[index], 'section', [(low, high), (high, low), (1, 0)])  11.7 us
    unnamed x27, local copies, waits for them, and re-layouts  11.6 us
    ppermute x4, waiting for transfers between devices, per_device(): lax.ppermute(sent[index], 'section', [(low, high), (high, low), (1, 0)])  11.4 us
  transfers between devices with their start and end apart: 25, of which 13 were waited for; matrix products, arithmetic and copies ran while one was open for 2% of the time, Pallas kernels for 15%

profile of v2, /device:TPU:20, one launch (start us, length us, event | category | flops | bytes accessed | tf_op | source)
XLA Modules:
  0.0 206.8 jit_solution(11020592487572007416)
XLA Ops:
  10.3 1.4 copy.15.side_weight
  11.8 12.9 %prep.2 = (bf16[512,1024]{1,0:T(8,128)(2,1)S(1)}, bf16[512,2048]{1,0:T(8,128)(2,1)S(1)}, bf16[512,128]{1,0:T(8,128)(2,1)S(1)}, bf16[512,128]{1,0:T(8,128)(2,1)S(...) custom-call(s32[6]{0:T(128)S(1)} %stack.31.info, ...), custom_call_target="tpu_custom_call" | custom-call | flops 2147483648 | bytes 12582912 | tf_op jit(solution)/shard_map/prep/pallas_call | solution.py:398
  24.7 1.3 copy-done.4
  29.5 6.6 %mid.2 = (f32[512,2048]{1,0:T(8,128)S(1)}, bf16[512,2048]{1,0:T(8,128)(2,1)S(1)}) custom-call(bf16[512,1024]{1,0:T(8,128)(2,1)S(1)} %get-tuple-element.47.normed, bf16[1,1024,4096]{2,1,0:T(8,128)(2,1)} %gate_weight.3, bf16[512,2048]{1,0:T(8,128)(2,1)S(1)} %get-tuple-element.48.x, bf16[512,128]{1,0:T(8,128)(2,1)S(1)} %get-tuple-element.49.b, ...), custom_call_target="tpu_custom_call" | custom-call | flops 2147483648 | bytes 12582912 | tf_op jit(solution)/shard_map/mid/pallas_call | solution.py:427
  36.2 2.0 copy-done.2
  38.2 1.4 copy-done.6
  41.3 5.7 %all-gather.3.cloned.1.call-done = bf16[1,2048,1024]{2,1,0:T(8,128)(2,1)} async-done(((bf16[1,256,1024]{2,1,0:T(8,128)(2,1)}), bf16[1,2048,1024]{2,1,0:T(8,128)(2,1)}) %all-gather.3.cloned.1.call-update) | async-done | bytes 4194320 | tf_op jit(solution)/shard_map/all_gather | solution.py:710
  46.9 2.2 %copy-done.3 = f32[512,2048]{1,0:T(8,128)S(1)} copy-done((f32[512,2048]{1,0:T(8,128)S(1)}, f32[512,2048]{1,0:T(8,128)}, u32[]{:S(2)}) %copy-start.3) | copy-done | bytes 4194328
  49.1 1.6 copy-done.5
  50.7 1.6 copy-done.7
  52.3 7.4 %finish.2 = (bf16[128,1024]{1,0:T(8,128)(2,1)S(1)}, bf16[128,1024]{1,0:T(8,128)(2,1)S(1)}, f32[128,1024]{1,0:T(8,128)S(1)}, f32[128,1024]{1,0:T(8,128)S(1)}, f32...) custom-call(s32[6]{0:T(128)S(1)} %stack.31.info, bf16[512,1024]{1,0:T(8,128)(2,1)S(1)} %copy-done, ...), custom_call_target="tpu_custom_call" | custom-call | flops 2147483648 | bytes 16777216 | tf_op jit(solution)/shard_map/finish/pallas_call | solution.py:514
  61.1 1.3 collective-permute-start.7
  62.5 1.3 collective-permute-start.10
  63.8 27.3 %collective-permute-done.7 = bf16[128,1024]{1,0:T(8,128)(2,1)S(1)} collective-permute-done((bf16[128,1024]{1,0:T(8,128)(2,1)S(1)}, bf16[128,1024]{1,0:T(8,128)(2,1)S(1)}, u32[]{:S(2)}, u32[]{:S(2)}) %collective-permute-start.7) | collective-permute-done | bytes 262176 | tf_op jit(solution)/shard_map/ppermute | solution.py:786
  91.1 1.9 collective-permute-start.8
  93.1 4.2 %collective-permute-done.10 = bf16[128,1024]{1,0:T(8,128)(2,1)S(1)} collective-permute-done((bf16[128,1024]{1,0:T(8,128)(2,1)S(1)}, bf16[128,1024]{1,0:T(8,128)(2,1)S(1)}, u32[]{:S(2)}, u32[]{:S(2)}) %collective-permute-start.10) | collective-permute-done | bytes 262176 | tf_op jit(solution)/shard_map/ppermute | solution.py:786
  97.3 1.9 collective-permute-start.11
  99.2 3.7 %collective-permute-done.8 = bf16[128,1024]{1,0:T(8,128)(2,1)} collective-permute-done((bf16[128,1024]{1,0:T(8,128)(2,1)S(1)}, bf16[128,1024]{1,0:T(8,128)(2,1)}, u32[]{:S(2)}, u32[]{:S(2)}) %collective-permute-start.8) | collective-permute-done | bytes 262176 | tf_op jit(solution)/shard_map/ppermute | solution.py:786
  102.9 2.0 collective-permute-start.13
  104.9 3.1 %collective-permute-done.11 = bf16[128,1024]{1,0:T(8,128)(2,1)} collective-permute-done((bf16[128,1024]{1,0:T(8,128)(2,1)S(1)}, bf16[128,1024]{1,0:T(8,128)(2,1)}, u32[]{:S(2)}, u32[]{:S(2)}) %collective-permute-start.11) | collective-permute-done | bytes 262176 | tf_op jit(solution)/shard_map/ppermute | solution.py:786
  108.0 2.0 collective-permute-start.12
  110.0 1.0 broadcast_select_fusion.3
  111.0 4.2 %collective-permute-done.12 = bf16[128,1024]{1,0:T(8,128)(2,1)} collective-permute-done((bf16[128,1024]{1,0:T(8,128)(2,1)}, bf16[128,1024]{1,0:T(8,128)(2,1)}, u32[]{:S(2)}, u32[]{:S(2)}) %collective-permute-start.12) | collective-permute-done | bytes 262176 | tf_op jit(solution)/shard_map/ppermute | solution.py:786
  115.2 1.0 broadcast_select_fusion.2
  116.2 2.1 %collective-permute-start.14 = (bf16[16,1024]{1,0:T(8,128)(2,1)S(1)}, bf16[16,1024]{1,0:T(8,128)(2,1)S(1)}, u32[]{:S(2)}, u32[]{:S(2)}) collective-permute-start(bf16[16,1024]{1,0:T(8,128)(2,1)S(1)} %slice_select_fusion), channel_id=1, source_target_pairs={{2,6},{6,10},{10,14},{14,18},{18,22},{22,26},{26,30},{7,3},{11,7},... | collective-permute-start | bytes 98312 | tf_op jit(solution)/shard_map/ppermute | solution.py:735
  118.4 3.9 %collective-permute-done.14.halo = bf16[16,1024]{1,0:T(8,128)(2,1)S(1)} collective-permute-done((bf16[16,1024]{1,0:T(8,128)(2,1)S(1)}, bf16[16,1024]{1,0:T(8,128)(2,1)S(1)}, u32[]{:S(2)}, u32[]{:S(2)}) %collective-permute-start.14) | collective-permute-done | bytes 32800 | tf_op jit(solution)/shard_map/ppermute | solution.py:735
  122.3 12.9 %prep.3 = (bf16[512,1024]{1,0:T(8,128)(2,1)S(1)}, bf16[512,2048]{1,0:T(8,128)(2,1)S(1)}, bf16[512,128]{1,0:T(8,128)(2,1)S(1)}, bf16[512,128]{1,0:T(8,128)(2,1)S(...) custom-call(s32[6]{0:T(128)S(1)} %stack.31.info, ...), custom_call_target="tpu_custom_call" | custom-call | flops 2147483648 | bytes 12582912 | tf_op jit(solution)/shard_map/prep/pallas_call | solution.py:398
  135.2 1.9 collective-permute-start.15
  137.2 2.0 collective-permute-done.15.partner
  139.8 3.0 %collective-permute-start.16 = (bf16[144,1024]{1,0:T(8,128)(2,1)S(1)}, bf16[144,1024]{1,0:T(8,128)(2,1)S(1)}, u32[]{:S(2)}, u32[]{:S(2)}) collective-permute-start(bf16[144,1024]{1,0:T(8,128)(2,1)S(1)} %pair.3.refs_0_), channel_id=1, source_target_pairs={{2,10},{6,14},{18,26},{22,30},{11,3},{15,7},{27,19},{31,23}} | collective-permute-start | bytes 884744 | tf_op jit(solution)/shard_map/ppermute | solution.py:663
  142.8 1.3 collective-permute-start.17
  144.1 1.3 collective-permute-start.18
  145.4 6.5 %mid.3 = (f32[512,2048]{1,0:T(8,128)S(1)}, bf16[512,2048]{1,0:T(8,128)(2,1)S(1)}) custom-call(bf16[512,1024]{1,0:T(8,128)(2,1)S(1)} %get-tuple-element.67.normed, bf16[1,1024,4096]{2,1,0:T(8,128)(2,1)} %gate_weight.3, bf16[512,2048]{1,0:T(8,128)(2,1)S(1)} %get-tuple-element.68.x, bf16[512,128]{1,0:T(8,128)(2,1)S(1)} %get-tuple-element.69.b, ...), custom_call_target="tpu_custom_call" | custom-call | flops 2147483648 | bytes 12582912 | tf_op jit(solution)/shard_map/mid/pallas_call | solution.py:427
  152.0 7.9 %collective-permute-done.17.refs_2_ = bf16[144,1024]{1,0:T(8,128)(2,1)S(1)} collective-permute-done((bf16[144,1024]{1,0:T(8,128)(2,1)S(1)}, bf16[144,1024]{1,0:T(8,128)(2,1)S(1)}, u32[]{:S(2)}, u32[]{:S(2)}) %collective-permute-start.17) | collective-permute-done | bytes 294944 | tf_op jit(solution)/shard_map/ppermute | solution.py:663
  160.9 1.9 collective-permute-start.19
  162.8 1.5 collective-permute-done.19.other
  164.3 7.2 %finish.3 = (bf16[128,1024]{1,0:T(8,128)(2,1)S(1)}, bf16[128,1024]{1,0:T(8,128)(2,1)S(1)}, bf16[128,1024]{1,0:T(8,128)(2,1)S(1)}, bf16[128,1024]{1,0:T(8,128)(2,1)S(1)}, f32[512,1024]{1,0:T(8,128)S(1)}) custom-call(s32[6]{0:T(128)S(1)} %stack.31.info, bf16[512,1024]{1,0:T(8,128)(2,1)S(1)} %pad_maximum_fusion.rows, f32[512,2048]{1,0:T(8,128)S(1)} %get-tuple-element.73.y, ...), custom_call_target="tpu_custom_call" | custom-call | flops 2147483648 | bytes 16777216 | tf_op jit(solution)/shard_map/finish/pallas_call | solution.py:514
  171.5 2.2 %collective-permute-start.23 = (bf16[128,1024]{1,0:T(8,128)(2,1)S(1)}, bf16[128,1024]{1,0:T(8,128)(2,1)S(1)}, u32[]{:S(2)}, u32[]{:S(2)}) collective-permute-start(bf16[128,1024]{1,0:T(8,128)(2,1)S(1)} %get-tuple-element.82.sent), channel_id=1, source_target_pairs={{2,3},{3,2},{1,0},{6,7},{7,6},{5,4},{10,11},{11,10},{9,8},{14,15},... | collective-permute-start | bytes 786440 | tf_op jit(solution)/shard_map/ppermute | solution.py:799
  173.8 3.6 %collective-permute-start.22 = (bf16[128,1024]{1,0:T(8,128)(2,1)S(1)}, bf16[128,1024]{1,0:T(8,128)(2,1)S(1)}, u32[]{:S(2)}, u32[]{:S(2)}) collective-permute-start(bf16[128,1024]{1,0:T(8,128)(2,1)S(1)} %get-tuple-element.81.sent), channel_id=1, source_target_pairs={{2,3},{3,2},{1,0},{6,7},{7,6},{5,4},{10,11},{11,10},{9,8},{14,15},... | collective-permute-start | bytes 786440 | tf_op jit(solution)/shard_map/ppermute | solution.py:799
  177.4 2.2 %collective-permute-start.21 = (bf16[128,1024]{1,0:T(8,128)(2,1)S(1)}, bf16[128,1024]{1,0:T(8,128)(2,1)S(1)}, u32[]{:S(2)}, u32[]{:S(2)}) collective-permute-start(bf16[128,1024]{1,0:T(8,128)(2,1)S(1)} %get-tuple-element.80.sent), channel_id=1, source_target_pairs={{2,3},{3,2},{1,0},{6,7},{7,6},{5,4},{10,11},{11,10},{9,8},{14,15},... | collective-permute-start | bytes 786440 | tf_op jit(solution)/shard_map/ppermute | solution.py:799
  179.6 3.6 %collective-permute-start.20 = (bf16[128,1024]{1,0:T(8,128)(2,1)S(1)}, bf16[128,1024]{1,0:T(8,128)(2,1)S(1)}, u32[]{:S(2)}, u32[]{:S(2)}) collective-permute-start(bf16[128,1024]{1,0:T(8,128)(2,1)S(1)} %get-tuple-element.79.sent), channel_id=1, source_target_pairs={{2,3},{3,2},{1,0},{6,7},{7,6},{5,4},{10,11},{11,10},{9,8},{14,15},... | collective-permute-start | bytes 786440 | tf_op jit(solution)/shard_map/ppermute | solution.py:799
  183.2 1.3 settle.4.rest_0_
  184.6 3.6 %collective-permute-done.22.other = bf16[128,1024]{1,0:T(8,128)(2,1)S(1)} collective-permute-done((bf16[128,1024]{1,0:T(8,128)(2,1)S(1)}, bf16[128,1024]{1,0:T(8,128)(2,1)S(1)}, u32[]{:S(2)}, u32[]{:S(2)}) %collective-permute-start.22) | collective-permute-done | bytes 262176 | tf_op jit(solution)/shard_map/ppermute | solution.py:799
  188.2 1.3 settle.5.rest_0_
  189.5 4.3 %collective-permute-done.21.other = bf16[128,1024]{1,0:T(8,128)(2,1)S(1)} collective-permute-done((bf16[128,1024]{1,0:T(8,128)(2,1)S(1)}, bf16[128,1024]{1,0:T(8,128)(2,1)S(1)}, u32[]{:S(2)}, u32[]{:S(2)}) %collective-permute-start.21) | collective-permute-done | bytes 262176 | tf_op jit(solution)/shard_map/ppermute | solution.py:799
  193.8 1.3 settle.6.rest_0_
  195.1 3.5 %collective-permute-done.20.other = bf16[128,1024]{1,0:T(8,128)(2,1)S(1)} collective-permute-done((bf16[128,1024]{1,0:T(8,128)(2,1)S(1)}, bf16[128,1024]{1,0:T(8,128)(2,1)S(1)}, u32[]{:S(2)}, u32[]{:S(2)}) %collective-permute-start.20) | collective-permute-done | bytes 262176 | tf_op jit(solution)/shard_map/ppermute | solution.py:799
  198.6 1.3 settle.7
  (57 shorter events, 12.1 us)
Async XLA Ops:
  6.5 5.2 %copy-start.1 = (bf16[64,2048]{1,0:T(8,128)(2,1)S(1)}, bf16[64,2048]{1,0:T(8,128)(2,1)}, u32[]{:S(2)}) copy-start(bf16[64,2048]{1,0:T(8,128)(2,1)} %constant.42.clone.spread) | copy-start | bytes 786436
  6.5 5.2 %copy-start = (bf16[512,1024]{1,0:T(8,128)(2,1)S(1)}, bf16[512,1024]{1,0:T(8,128)(2,1)}, u32[]{:S(2)}) copy-start(bf16[512,1024]{1,0:T(8,128)(2,1)} %rows.3) | copy-start | bytes 3145732
  6.5 5.3 %copy-start.8 = (f32[1,4,2304]{2,1,0:T(4,128)S(1)}, f32[1,4,2304]{2,1,0:T(4,128)}, u32[]{:S(2)}) copy-start(f32[1,4,2304]{2,1,0:T(4,128)} %taps.3) | copy-start | bytes 110596
  6.5 5.3 %copy-start.10 = (f32[1,1024]{1,0:T(1,128)S(1)}, f32[1,1024]{1,0:T(1,128)}, u32[]{:S(2)}) copy-start(f32[1,1024]{1,0:T(1,128)} %gain.6) | copy-start | bytes 12292
  6.5 5.3 %copy-start.11 = (f32[1,32]{1,0:T(1,128)S(1)}, f32[1,32]{1,0:T(1,128)}, u32[]{:S(2)}) copy-start(f32[1,32]{1,0:T(1,128)} %bias.3) | copy-start | bytes 388
  6.5 5.3 %copy-start.12 = (f32[1,32]{1,0:T(1,128)S(1)}, f32[1,32]{1,0:T(1,128)}, u32[]{:S(2)}) copy-start(f32[1,32]{1,0:T(1,128)} %decay.3) | copy-start | bytes 388
  6.6 40.3 %all-gather.3.cloned.1.call-start = ((), (), s32[]{:S(2)}) async-start(), calls=%async_computation | async-start | bytes 4718592 | tf_op jit(solution)/shard_map/all_gather | solution.py:710
  8.1 3.7 %collective-permute-start = (bf16[16,1024]{1,0:T(8,128)(2,1)S(1)}, bf16[16,1024]{1,0:T(8,128)(2,1)S(1)}, u32[]{:S(2)}, u32[]{:S(2)}) collective-permute-start(bf16[16,1024]{1,0:T(8,128)(2,1)S(1)} %slice_select_fusion.1), channel_id=1, source_target_pairs={{0,4},{4,8},{8,12},{12,16},{16,20},{20,24},{24,28},{5,1},{9,5},{13... | collective-permute-start | bytes 98312 | tf_op jit(solution)/shard_map/ppermute | solution.py:735
  24.7 1.3 copy-start.4
  26.1 0.7 collective-permute-start.1
  27.4 12.2 %collective-permute-start.2 = (bf16[144,1024]{1,0:T(8,128)(2,1)S(1)}, bf16[144,1024]{1,0:T(8,128)(2,1)S(1)}, u32[]{:S(2)}, u32[]{:S(2)}) collective-permute-start(bf16[144,1024]{1,0:T(8,128)(2,1)S(1)} %pair.2.refs_0_), channel_id=1, source_target_pairs={{0,8},{4,12},{16,24},{20,28},{9,1},{13,5},{25,17},{29,21}} | collective-permute-start | bytes 884744 | tf_op jit(solution)/shard_map/ppermute | solution.py:663
  28.1 11.5 %collective-permute-start.3 = (bf16[144,1024]{1,0:T(8,128)(2,1)S(1)}, bf16[144,1024]{1,0:T(8,128)(2,1)S(1)}, u32[]{:S(2)}, u32[]{:S(2)}) collective-permute-start(bf16[144,1024]{1,0:T(8,128)(2,1)S(1)} %pair.2.refs_0_), channel_id=1, source_target_pairs={{0,16},{4,20},{8,24},{12,28},{17,1},{21,5},{25,9},{29,13}} | collective-permute-start | bytes 884744 | tf_op jit(solution)/shard_map/ppermute | solution.py:663
  28.8 10.8 %collective-permute-start.4 = (bf16[144,1024]{1,0:T(8,128)(2,1)S(1)}, bf16[144,1024]{1,0:T(8,128)(2,1)S(1)}, u32[]{:S(2)}, u32[]{:S(2)}) collective-permute-start(bf16[144,1024]{1,0:T(8,128)(2,1)S(1)} %pair.2.refs_0_), channel_id=1, source_target_pairs={{0,24},{4,28},{8,16},{12,20},{17,9},{21,13},{25,1},{29,5}} | collective-permute-start | bytes 884744 | tf_op jit(solution)/shard_map/ppermute | solution.py:663
  29.5 17.4 %copy-start.9 = (f32[1,2048]{1,0:T(1,128)S(1)}, f32[1,2048]{1,0:T(1,128)}, u32[]{:S(2)}) copy-start(f32[1,2048]{1,0:T(1,128)} %gain.7) | copy-start | bytes 24580
  36.2 2.0 copy-start.2
  38.2 1.4 copy-start.6
  40.6 0.7 collective-permute-start.5
  46.9 2.2 %copy-start.3 = (f32[512,2048]{1,0:T(8,128)S(1)}, f32[512,2048]{1,0:T(8,128)}, u32[]{:S(2)}) copy-start(f32[512,2048]{1,0:T(8,128)} %copy-done.2) | copy-start | bytes 12582916
  49.1 1.6 copy-start.5
  50.7 1.6 copy-start.7
  59.6 1.4 collective-permute-start.6
  60.3 2.1 collective-permute-start.9
  61.1 30.0 %collective-permute-start.7 = (bf16[128,1024]{1,0:T(8,128)(2,1)S(1)}, bf16[128,1024]{1,0:T(8,128)(2,1)S(1)}, u32[]{:S(2)}, u32[]{:S(2)}) collective-permute-start(bf16[128,1024]{1,0:T(8,128)(2,1)S(1)} %add_convert_fusion.3.rest_0_), channel_id=1, source_target_pairs={{0,1},{1,2},{4,5},{5,6},{8,9},{9,10},{12,13},{13,14},{16,17},{17,1... | collective-permute-start | bytes 786440 | tf_op jit(solution)/shard_map/ppermute | solution.py:786
  62.5 34.8 %collective-permute-start.10 = (bf16[128,1024]{1,0:T(8,128)(2,1)S(1)}, bf16[128,1024]{1,0:T(8,128)(2,1)S(1)}, u32[]{:S(2)}, u32[]{:S(2)}) collective-permute-start(bf16[128,1024]{1,0:T(8,128)(2,1)S(1)} %add_convert_fusion.1.rest_3_), channel_id=1, source_target_pairs={{0,1},{1,2},{4,5},{5,6},{8,9},{9,10},{12,13},{13,14},{16,17},{17,1... | collective-permute-start | bytes 786440 | tf_op jit(solution)/shard_map/ppermute | solution.py:786
  91.1 11.8 %collective-permute-start.8 = (bf16[128,1024]{1,0:T(8,128)(2,1)S(1)}, bf16[128,1024]{1,0:T(8,128)(2,1)}, u32[]{:S(2)}, u32[]{:S(2)}) collective-permute-start(bf16[128,1024]{1,0:T(8,128)(2,1)S(1)} %add_convert_fusion.2.rest_2_), channel_id=1, source_target_pairs={{1,2},{2,3},{5,6},{6,7},{9,10},{10,11},{13,14},{14,15},{17,18},{18... | collective-permute-start | bytes 786440 | tf_op jit(solution)/shard_map/ppermute | solution.py:786
  97.3 10.7 %collective-permute-start.11 = (bf16[128,1024]{1,0:T(8,128)(2,1)S(1)}, bf16[128,1024]{1,0:T(8,128)(2,1)}, u32[]{:S(2)}, u32[]{:S(2)}) collective-permute-start(bf16[128,1024]{1,0:T(8,128)(2,1)S(1)} %add_convert_fusion.rest_1_), channel_id=1, source_target_pairs={{1,2},{2,3},{5,6},{6,7},{9,10},{10,11},{13,14},{14,15},{17,18},{18... | collective-permute-start | bytes 786440 | tf_op jit(solution)/shard_map/ppermute | solution.py:786
  102.9 7.1 %collective-permute-start.13 = (bf16[128,1024]{1,0:T(8,128)(2,1)}, bf16[128,1024]{1,0:T(8,128)(2,1)}, u32[]{:S(2)}, u32[]{:S(2)}) collective-permute-start(bf16[128,1024]{1,0:T(8,128)(2,1)} %collective-permute-done.8), channel_id=1, source_target_pairs={{2,3},{6,7},{10,11},{14,15},{18,19},{22,23},{26,27},{30,31}} | collective-permute-start | bytes 786440 | tf_op jit(solution)/shard_map/ppermute | solution.py:786
  108.0 7.2 %collective-permute-start.12 = (bf16[128,1024]{1,0:T(8,128)(2,1)}, bf16[128,1024]{1,0:T(8,128)(2,1)}, u32[]{:S(2)}, u32[]{:S(2)}) collective-permute-start(bf16[128,1024]{1,0:T(8,128)(2,1)} %collective-permute-done.11), channel_id=1, source_target_pairs={{2,3},{6,7},{10,11},{14,15},{18,19},{22,23},{26,27},{30,31}} | collective-permute-start | bytes 786440 | tf_op jit(solution)/shard_map/ppermute | solution.py:786
  116.2 6.1 %collective-permute-start.14 = (bf16[16,1024]{1,0:T(8,128)(2,1)S(1)}, bf16[16,1024]{1,0:T(8,128)(2,1)S(1)}, u32[]{:S(2)}, u32[]{:S(2)}) collective-permute-start(bf16[16,1024]{1,0:T(8,128)(2,1)S(1)} %slice_select_fusion), channel_id=1, source_target_pairs={{2,6},{6,10},{10,14},{14,18},{18,22},{22,26},{26,30},{7,3},{11,7},... | collective-permute-start | bytes 98312 | tf_op jit(solution)/shard_map/ppermute | solution.py:735
  135.2 3.9 %collective-permute-start.15 = (bf16[144,2048]{1,0:T(8,128)(2,1)S(1)}, bf16[144,2048]{1,0:T(8,128)(2,1)S(1)}, u32[]{:S(2)}, u32[]{:S(2)}) collective-permute-start(bf16[144,2048]{1,0:T(8,128)(2,1)S(1)} %get-tuple-element.66.mine), channel_id=1, source_target_pairs={{2,6},{6,2},{10,14},{14,10},{18,22},{22,18},{26,30},{30,26},{3,7},... | collective-permute-start | bytes 1769480 | tf_op jit(solution)/shard_map/ppermute | solution.py:654
  139.8 12.2 %collective-permute-start.16 = (bf16[144,1024]{1,0:T(8,128)(2,1)S(1)}, bf16[144,1024]{1,0:T(8,128)(2,1)S(1)}, u32[]{:S(2)}, u32[]{:S(2)}) collective-permute-start(bf16[144,1024]{1,0:T(8,128)(2,1)S(1)} %pair.3.refs_0_), channel_id=1, source_target_pairs={{2,10},{6,14},{18,26},{22,30},{11,3},{15,7},{27,19},{31,23}} | collective-permute-start | bytes 884744 | tf_op jit(solution)/shard_map/ppermute | solution.py:663
  142.8 17.1 %collective-permute-start.17 = (bf16[144,1024]{1,0:T(8,128)(2,1)S(1)}, bf16[144,1024]{1,0:T(8,128)(2,1)S(1)}, u32[]{:S(2)}, u32[]{:S(2)}) collective-permute-start(bf16[144,1024]{1,0:T(8,128)(2,1)S(1)} %pair.3.refs_0_), channel_id=1, source_target_pairs={{2,18},{6,22},{10,26},{14,30},{19,3},{23,7},{27,11},{31,15}} | collective-permute-start | bytes 884744 | tf_op jit(solution)/shard_map/ppermute | solution.py:663
  144.1 15.8 %collective-permute-start.18 = (bf16[144,1024]{1,0:T(8,128)(2,1)S(1)}, bf16[144,1024]{1,0:T(8,128)(2,1)S(1)}, u32[]{:S(2)}, u32[]{:S(2)}) collective-permute-start(bf16[144,1024]{1,0:T(8,128)(2,1)S(1)} %pair.3.refs_0_), channel_id=1, source_target_pairs={{2,26},{6,30},{10,18},{14,22},{19,11},{23,15},{27,3},{31,7}} | collective-permute-start | bytes 884744 | tf_op jit(solution)/shard_map/ppermute | solution.py:663
  160.9 3.4 %collective-permute-start.19 = (bf16[128,1024]{1,0:T(8,128)(2,1)S(1)}, bf16[128,1024]{1,0:T(8,128)(2,1)S(1)}, u32[]{:S(2)}, u32[]{:S(2)}) collective-permute-start(bf16[128,1024]{1,0:T(8,128)(2,1)S(1)} %merge.3.mine), channel_id=1, source_target_pairs={{2,6},{6,2},{10,14},{14,10},{18,22},{22,18},{26,30},{30,26},{3,7},... | collective-permute-start | bytes 786440 | tf_op jit(solution)/shard_map/ppermute | solution.py:654
  171.5 11.7 %collective-permute-start.23 = (bf16[128,1024]{1,0:T(8,128)(2,1)S(1)}, bf16[128,1024]{1,0:T(8,128)(2,1)S(1)}, u32[]{:S(2)}, u32[]{:S(2)}) collective-permute-start(bf16[128,1024]{1,0:T(8,128)(2,1)S(1)} %get-tuple-element.82.sent), channel_id=1, source_target_pairs={{2,3},{3,2},{1,0},{6,7},{7,6},{5,4},{10,11},{11,10},{9,8},{14,15},... | collective-permute-start | bytes 786440 | tf_op jit(solution)/shard_map/ppermute | solution.py:799
  173.8 14.4 %collective-permute-start.22 = (bf16[128,1024]{1,0:T(8,128)(2,1)S(1)}, bf16[128,1024]{1,0:T(8,128)(2,1)S(1)}, u32[]{:S(2)}, u32[]{:S(2)}) collective-permute-start(bf16[128,1024]{1,0:T(8,128)(2,1)S(1)} %get-tuple-element.81.sent), channel_id=1, source_target_pairs={{2,3},{3,2},{1,0},{6,7},{7,6},{5,4},{10,11},{11,10},{9,8},{14,15},... | collective-permute-start | bytes 786440 | tf_op jit(solution)/shard_map/ppermute | solution.py:799
  177.4 16.4 %collective-permute-start.21 = (bf16[128,1024]{1,0:T(8,128)(2,1)S(1)}, bf16[128,1024]{1,0:T(8,128)(2,1)S(1)}, u32[]{:S(2)}, u32[]{:S(2)}) collective-permute-start(bf16[128,1024]{1,0:T(8,128)(2,1)S(1)} %get-tuple-element.80.sent), channel_id=1, source_target_pairs={{2,3},{3,2},{1,0},{6,7},{7,6},{5,4},{10,11},{11,10},{9,8},{14,15},... | collective-permute-start | bytes 786440 | tf_op jit(solution)/shard_map/ppermute | solution.py:799
  179.6 19.0 %collective-permute-start.20 = (bf16[128,1024]{1,0:T(8,128)(2,1)S(1)}, bf16[128,1024]{1,0:T(8,128)(2,1)S(1)}, u32[]{:S(2)}, u32[]{:S(2)}) collective-permute-start(bf16[128,1024]{1,0:T(8,128)(2,1)S(1)} %get-tuple-element.79.sent), channel_id=1, source_target_pairs={{2,3},{3,2},{1,0},{6,7},{7,6},{5,4},{10,11},{11,10},{9,8},{14,15},... | collective-permute-start | bytes 786440 | tf_op jit(solution)/shard_map/ppermute | solution.py:799
Sparse Core Ops, SparseCore 0:
  9.3 37.5 all-gather.2

commit v3 on v2

--- a/solution.py
+++ b/solution.py
@@ -15,7 +15,7 @@
 LIMIT = 36 * 2**20
 SMALL = 8 * 2**20
 SKEW = 2
-REVERSE, UPPER, FIRST, RANKS = 0, 1, 2, 3
+REVERSE, UPPER, FIRST, SEQ, RANKS = 0, 1, 2, 3, 4
 LOG2E = 1.4426950408889634
 F32 = jnp.float32
 BF16 = jnp.bfloat16
@@ -108,7 +108,10 @@
             start = HALO + pair * 2 * CHUNK
             extended[start : start + 2 * CHUNK] = dot(turn, piece).astype(BF16)
         normed_out[...] = extended[HALO:]
-        side = dot(extended[...], side_weight[...]).astype(BF16).astype(F32)
+        side = lax.dot_general(
+            extended[...], side_weight[...], (((1,), (1,)), ((), ())), preferred_element_type=F32
+        )
+        side = side.astype(BF16).astype(F32)
         buffer[:, 0 : 2 * state] = side[:, 0 : 2 * state]
         raw = side[HALO:, 2 * state :] + bias[...]
         step = jnp.maximum(raw, 0.0) + jnp.log1p(jnp.exp(-jnp.abs(raw)))
@@ -180,7 +183,9 @@
     state_out[state:, :] = tail.astype(BF16)
 
 
-def mid_kernel(normed, gate_weight, x, b, c_rows, cumulative, shifted, skip, y_out, gate_out, scores):
+def mid_kernel(
+    normed, gate_weight, x, b, c_rows, cumulative, shifted, skip, spread, y_out, gate_out, scores
+):
     step_index = pl.program_id(0)
     length = x.shape[0]
     chunks = length // CHUNK
@@ -200,6 +205,8 @@
             )
 
     gate_out[...] = dot(normed[...], gate_weight[...]).astype(BF16)
+    skip_rows = jnp.broadcast_to(skip[...], (HALO, skip.shape[1]))
+    skips = dot(high_low(skip_rows), spread[...])[0:1]
     for c in range(chunks):
         here = slice(c * CHUNK, (c + 1) * CHUNK)
         score = scores[here, :]
@@ -218,11 +225,13 @@
                 axis=0,
             )
             within = dot(jnp.concatenate(parts, axis=1), stacked)
-            y_out[here, lanes] = within + skip[:, lanes] * values.astype(F32)
+            y_out[here, lanes] = within + skips[:, lanes] * values.astype(F32)
 
 
 def finish_kernel(
     count,
+    plan,
+    shard_rows,
     mode,
     info,
     rows,
@@ -237,10 +246,10 @@
     partner,
     gain,
     spread,
-    weight_far,
     *rest,
 ):
-    outs = rest[:-4]
+    far_pieces = rest[: len(plan)]
+    outs = rest[len(plan) : -4]
     normed, entering, weight, arrived = rest[-4:]
     step_index = pl.program_id(0)
     steps = pl.num_programs(0)
@@ -248,11 +257,24 @@
     size, inner = y.shape
     parts = size // CHUNK
     state = mine.shape[0]
-    fetch = pltpu.make_async_copy(weight_far, weight, arrived)
+    fetches = []
+    for piece, ranges in zip(far_pieces, plan):
+        for mask, source, offset, extent in ranges:
+            place = 0
+            if mask is not None:
+                place = pl.multiple_of((info[SEQ] ^ mask) * shard_rows + offset, 16)
+            fetches.append(
+                pltpu.make_async_copy(
+                    piece.at[source : source + extent],
+                    weight.at[pl.ds(place, extent)],
+                    arrived.at[len(fetches)],
+                )
+            )
 
     @pl.when(step_index == 0)
     def _():
-        fetch.start()
+        for fetch in fetches:
+            fetch.start()
         half = inner // 2
         upper = info[UPPER] == 1
         first = info[FIRST] == 1
@@ -298,7 +320,8 @@
 
     @pl.when(step_index == 0)
     def _():
-        fetch.wait()
+        for fetch in fetches:
+            fetch.wait()
 
     total = dot(normed[...], weight[...])
     base = rows[...].astype(F32) + total
@@ -358,7 +381,7 @@
     steps = inner // WIDTH
     chunks = length // CHUNK
     margin = conv.shape[1]
-    side_taps = conv[0, :, inner:]
+    side_width = 2 * state
     grid_spec = pltpu.PrefetchScalarGridSpec(
         num_scalar_prefetch=1,
         grid=(steps,),
@@ -367,9 +390,9 @@
             whole_block((HALO, features)),
             whole_block((1, features)),
             pl.BlockSpec((None, features, WIDTH), lambda j, _: (0, 0, steps + j)),
-            pl.BlockSpec((None, features, side.shape[2]), lambda j, _: (0, 0, 0)),
+            pl.BlockSpec((None, side.shape[1], features), lambda j, _: (0, 0, 0)),
             pl.BlockSpec((None, margin, WIDTH), lambda j, _: (0, 0, j)),
-            whole_block(side_taps.shape),
+            pl.BlockSpec((None, margin, side_width), lambda j, _: (0, 0, inner // side_width)),
             whole_block((1, heads)),
             whole_block((1, heads)),
             pl.BlockSpec((2 * heads, WIDTH), lambda j, _: (0, j)),
@@ -416,10 +439,10 @@
             flops=2 * length * features * inner, bytes_accessed=12 * 2**20, transcendentals=0
         ),
         name="prep",
-    )(info, rows, halo, gain, far(main), side, conv, side_taps, bias, decay, spread)
-
-
-def mid(normed, main, x, b, c_rows, cumulative, shifted, skip, inner):
+    )(info, rows, halo, far(gain), far(main), far(side), far(conv), far(conv), far(bias), far(decay), far(spread))
+
+
+def mid(normed, main, x, b, c_rows, cumulative, shifted, skip, spread, inner):
     length, features = normed.shape
     state = b.shape[1]
     steps = inner // WIDTH
@@ -435,7 +458,8 @@
             whole_block((length, state)),
             pl.BlockSpec((heads_here, length), lambda j: (j, 0)),
             pl.BlockSpec((heads_here, length), lambda j: (j, 0)),
-            pl.BlockSpec((1, WIDTH), lambda j: (0, j)),
+            whole_block(skip.shape),
+            pl.BlockSpec((spread.shape[0], WIDTH), lambda j: (0, j)),
         ],
         out_specs=[
             pl.BlockSpec((length, WIDTH), lambda j: (0, j)),
@@ -453,14 +477,16 @@
             flops=2 * length * features * inner, bytes_accessed=12 * 2**20, transcendentals=0
         ),
         name="mid",
-    )(*near(normed), far(main), *near(x, b, c_rows, cumulative, shifted), skip)
-
-
-def finish(mode, info, rows, y, gate, c_rows, reach, local, state_parts, gain, spread, weight, earlier):
+    )(*near(normed), far(main), *near(x, b, c_rows, cumulative, shifted), far(skip), far(spread))
+
+
+def finish(mode, info, rows, y, gate, c_rows, reach, local, state_parts, gain, spread, pieces, earlier):
     features = rows.shape[1]
     length, inner = y.shape
     state = c_rows.shape[1]
     mine, other, partner = state_parts
+    plan = [ranges for _, ranges in pieces]
+    shard_rows = inner // lax.axis_size("seq")
     reach_width = reach.shape[1]
     tail = length // HALO
     size = 2 * CHUNK
@@ -500,19 +526,19 @@
             whole_block(partner.shape),
             whole_block((1, inner)),
             whole_block(spread.shape),
-            pl.BlockSpec(memory_space=pl.ANY),
         ]
+        + [pl.BlockSpec(memory_space=pl.ANY)] * len(pieces)
         + [whole_block(value.shape) for value in earlier],
         out_specs=out_specs,
         scratch_shapes=[
             pltpu.VMEM((size, inner), BF16),
             pltpu.VMEM((state, inner), BF16),
-            pltpu.VMEM(weight.shape, BF16),
-            pltpu.SemaphoreType.DMA,
+            pltpu.VMEM((inner, features), BF16),
+            pltpu.SemaphoreType.DMA((sum(len(ranges) for ranges in plan),)),
         ],
     )
     return pl.pallas_call(
-        functools.partial(finish_kernel, chunks, mode),
+        functools.partial(finish_kernel, chunks, plan, shard_rows, mode),
         grid_spec=grid_spec,
         out_shape=out_shape,
         compiler_params=pltpu.CompilerParams(
@@ -524,8 +550,47 @@
         name="finish",
     )(
         info, rows, *near(y, gate, c_rows, reach, reach, local), mine, other, partner,
-        gain, spread, far(weight), *earlier,
+        far(gain), far(spread), *[far(piece) for piece, _ in pieces], *earlier,
     )
+
+
+def stack_kernel(counts, *refs):
+    sources, outs = refs[: -len(counts)], refs[-len(counts) :]
+    position = 0
+    for out, count in zip(outs, counts):
+        start = 0
+        for source in sources[position : position + count]:
+            out[start : start + source.shape[0]] = source[...]
+            start += source.shape[0]
+        position += count
+
+
+def stacked(groups):
+    operands = []
+    specs = []
+    out_shape = []
+    for group in groups:
+        total = 0
+        for value, index, rows in group:
+            operands.append(value)
+            specs.append(pl.BlockSpec((rows, value.shape[1]), lambda j, index=index: (index, 0)))
+            total += rows
+        out_shape.append(pltpu.HBM((total, group[0][0].shape[1]), BF16))
+    return pl.pallas_call(
+        functools.partial(stack_kernel, [len(group) for group in groups]),
+        grid=(1,),
+        in_specs=specs,
+        out_specs=[whole_block(shape.shape) for shape in out_shape],
+        out_shape=out_shape,
+        compiler_params=pltpu.CompilerParams(vmem_limit_bytes=16 * 2**20),
+        cost_estimate=pl.CostEstimate(flops=10**6, bytes_accessed=10**6, transcendentals=0),
+        name="stack",
+    )(*[far(value) for value in operands])
+
+
+def seq_swap(value, mask):
+    count = lax.axis_size("seq")
+    return lax.ppermute(value, "seq", [(i, i ^ mask) for i in range(count)])
 
 
 def split_state(packed):
@@ -707,12 +772,11 @@
     section_index = lax.axis_index("section")
     seq_index = lax.axis_index("seq")
     reverse = section_index % 2
-    weight = lax.all_gather(output_weight[0], "seq", axis=0, tiled=True)
+    shard = output_weight[0]
     expand = np.repeat(np.eye(heads, dtype=np.float32), head_dim, axis=1)
     spread = jnp.asarray(np.concatenate([expand, expand], axis=0), BF16)
-    skip_row = jnp.repeat(skip_gain, head_dim, axis=1)
     upper = seq_index % 2
-    facts = [reverse, upper, (upper == reverse).astype(jnp.int32)]
+    facts = [reverse, upper, (upper == reverse).astype(jnp.int32), seq_index]
     for bit, group in stages_of(seq_count):
         position = (seq_index >> bit) % 2**group
         facts.append(jnp.where(reverse == 1, 2**group - 1 - position, position))
@@ -721,7 +785,6 @@
     for round_index in range(rounds):
         facts.append(section_index - 2 * round_index)
     info = jnp.stack([fact.astype(jnp.int32) for fact in facts])
-    info, skip_row = lax.optimization_barrier((info, skip_row))
     order = [chunks - 1, 0] + list(range(1, chunks - 1))
 
     def edges(first_rows, last_rows, sections):
@@ -737,6 +800,14 @@
     current = tokens
     halo = edges(tokens[:HALO], tokens[length - HALO :], (0, 1))
     previous = None
+    shards = None
+    if seq_count == 8:
+        halo, shard = lax.optimization_barrier((halo, shard))
+        shards = [shard, seq_swap(shard, 2), seq_swap(shard, 4)]
+        pieces = None
+    else:
+        whole = lax.all_gather(shard, "seq", axis=0, tiled=True)
+        pieces = [(whole, [(None, 0, 0, inner)])]
     for round_index in range(rounds):
         active = (2 * round_index, 2 * round_index + 1)
         normed, x, b, c_rows, cumulative, shifted, reach, local, packed = prep(
@@ -745,7 +816,7 @@
             halo,
             input_gain,
             main_weight,
-            side_weight,
+            jnp.swapaxes(side_weight, 1, 2),
             conv_kernel,
             step_bias,
             decay_rate,
@@ -753,9 +824,36 @@
             inner,
             state,
         )
-        def meanwhile(total):
+        early = round_index == 0 and shards
+        if early:
+            packed, *shards[1:] = lax.optimization_barrier((packed, *shards[1:]))
+
+        def meanwhile(total, normed=normed):
+            nonlocal pieces
+            if early:
+                *parts, _ = lax.optimization_barrier((*shards, total))
+                rows = parts[0].shape[0] // 2
+                up, down, three = stacked(
+                    [
+                        [(parts[2], 0, rows)],
+                        [(parts[1], 1, rows)],
+                        [(part, 0, 2 * rows) for part in parts],
+                    ]
+                )
+                halves = [seq_swap(up, 2), seq_swap(down, 4)]
+                swapped = seq_swap(three, 1)
             ready, _ = lax.optimization_barrier((normed, total))
-            return mid(ready, main_weight, x, b, c_rows, cumulative, shifted, skip_row, inner)
+            y, gate = mid(ready, main_weight, x, b, c_rows, cumulative, shifted, skip_gain, spread, inner)
+            if early:
+                *halves, _ = lax.optimization_barrier((*halves, y))
+                rows = halves[0].shape[0]
+                (joined,) = stacked([[(half, 0, rows) for half in halves]])
+                diagonal = seq_swap(joined, 1)
+                pieces = [(value, [(mask, 0, 0, 2 * rows)]) for value, mask in zip(shards, (0, 2, 4))]
+                pieces += [(half, [(6, 0, i * rows, rows)]) for i, half in enumerate(halves)]
+                pieces.append((swapped, [(m, i * 2 * rows, 0, 2 * rows) for i, m in enumerate((1, 3, 5))]))
+                pieces.append((diagonal, [(7, 0, 0, 2 * rows)]))
+            return y, gate
 
         state_parts, (y, gate) = entering_state(packed, info, active, seq_count, meanwhile)
         last_round = round_index + 1 == rounds
@@ -764,7 +862,7 @@
         mode = ("exchange", places) if last_round else (tuple(order), SKEW, places + round_index)
         outs = finish(
             mode, info, current, y, gate, c_rows, reach, local, state_parts,
-            output_gain, spread, weight, previous if last_round else [],
+            output_gain, spread, pieces, previous if last_round else [],
         )
         if last_round:
             *sent, base = outs

time: 209 us -> 193 us (0.923)
  between operations: 13.9 us -> 0.5 us
  local copies, waits for them, and re-layouts: 13.1 us -> 3.36 us
  Pallas kernels: 62.1 us -> 69.4 us
  starting transfers between devices: 39.1 us -> 41.4 us
    unnamed x27 -> x16, local copies, waits for them, and re-layouts: 11.6 us -> 3.28 us
    pallas_call x2 -> x4, Pallas kernels: 14.6 us -> 21.3 us  [the longest x2 16.6 us: finish(): pl.pallas_call(functools.partial(finish_kernel, chunks, plan, shard_rows,...]
    ppermute x0 -> x6, waiting for transfers between devices: none -> 5.98 us  [seq_swap(): return lax.ppermute(value, 'seq', [(i, i ^ mask) for i in range(count)])]
    all_gather x1 -> x0, waiting for transfers between devices: 5.65 us -> none  [per_device(): weight = lax.all_gather(output_weight[0], 'seq', axis=0, tiled=True)]
    ppermute x0 -> x6, starting transfers between devices: none -> 4.11 us  [seq_swap(): return lax.ppermute(value, 'seq', [(i, i ^ mask) for i in range(count)])]
  transfers between devices with their start and end apart: 25 -> 30, of which waited for: 13 -> 14; matrix products, arithmetic and copies ran while one was open for 2% -> 0% of each run, Pallas kernels for 15% -> 17%
where the time goes in v3:
time: 193 us; the launch traced here: 192 us
  waiting for transfers between devices  76.5 us (40%)
  Pallas kernels  69.4 us (36%)
  starting transfers between devices  41.4 us (21%)
  local copies, waits for them, and re-layouts  3.36 us (2%)
    ppermute x8, waiting for transfers between devices, per_device(): received.append(lax.ppermute(value, 'section', pairs))  43.9 us
    pallas_call x2, Pallas kernels, prep(): pl.pallas_call(prep_kernel, grid_spec=grid_spec, out_shape=[kept((length,...  26.2 us
    pallas_call x2, Pallas kernels, finish(): pl.pallas_call(functools.partial(finish_kernel, chunks, plan, shard_rows,...  16.6 us
    pallas_call x2, Pallas kernels, mid(): pl.pallas_call(mid_kernel, grid=(steps,), in_specs=[whole_block((length,...  13.4 us
    ppermute x4, starting transfers between devices, per_device(): lax.ppermute(sent[index], 'section', [(low, high), (high, low), (1, 0)])  11.7 us
    ppermute x4, waiting for transfers between devices, per_device(): lax.ppermute(sent[index], 'section', [(low, high), (high, low), (1, 0)])  11.4 us
    ppermute x8, starting transfers between devices, per_device(): received.append(lax.ppermute(value, 'section', pairs))  10.4 us
    ppermute x6, waiting for transfers between devices, forward(): return lax.ppermute(value, ('seq', 'section'), pairs)  7.69 us
  transfers between devices with their start and end apart: 30, of which 14 were waited for; matrix products, arithmetic and copies ran while one was open for 0% of the time, Pallas kernels for 17%

profile of v3, /device:TPU:20, one launch (start us, length us, event | category | flops | bytes accessed | tf_op | source)
XLA Modules:
  0.0 192.4 jit_solution(14325921723025516054)
XLA Ops:
  0.0 0.8 slice_select_fusion.1
  1.5 1.6 collective-permute-start.1
  3.6 1.2 copy-done
  4.8 13.1 %prep.2 = (bf16[512,1024]{1,0:T(8,128)(2,1)S(1)}, bf16[512,2048]{1,0:T(8,128)(2,1)S(1)}, bf16[512,128]{1,0:T(8,128)(2,1)S(1)}, bf16[512,128]{1,0:T(8,128)(2,1)S(...) custom-call(s32[7]{0:T(128)S(1)} %stack.37.info, ...), custom_call_target="tpu_custom_call" | custom-call | flops 2147483648 | bytes 12582912 | tf_op jit(solution)/shard_map/prep/pallas_call | solution.py:421
  19.4 2.9 %stack.39 = (bf16[128,1024]{1,0:T(8,128)(2,1)}, bf16[128,1024]{1,0:T(8,128)(2,1)}, bf16[768,1024]{1,0:T(8,128)(2,1)}) custom-call(bf16[256,1024]{1,0:T(8,128)(2,1)} %copy-done.3, bf16[256,1024]{1,0:T(8,128)(2,1)} %copy-done.2, bf16[256,1024]{1,0:T(8,128)(2,1)} %bitcast.11, bf16[256,1024]{1,0:T(8,128)(2,1)} %copy-done.2, bf16[256,1024]{1,0:T(8,128)(2,1)} %copy-done.3), custom_call_target="tpu_custom_call" | custom-call | flops 1000000 | bytes 1000000 | tf_op jit(solution)/shard_map/stack/pallas_call | solution.py:579
  22.8 1.5 collective-permute-start.9
  25.7 5.5 %collective-permute-done.8.refs_0_.rest_3_ = bf16[128,1024]{1,0:T(8,128)(2,1)S(1)} collective-permute-done((bf16[128,1024]{1,0:T(8,128)(2,1)}, bf16[128,1024]{1,0:T(8,128)(2,1)S(1)}, u32[]{:S(2)}, u32[]{:S(2)}) %collective-permute-start.8) | collective-permute-done | bytes 262176 | tf_op jit(solution)/shard_map/ppermute | solution.py:593
  31.9 6.7 %mid.2 = (f32[512,2048]{1,0:T(8,128)S(1)}, bf16[512,2048]{1,0:T(8,128)(2,1)S(1)}) custom-call(bf16[512,1024]{1,0:T(8,128)(2,1)S(1)} %get-tuple-element.60.normed, bf16[1,1024,4096]{2,1,0:T(8,128)(2,1)} %gate_weight.3, bf16[512,2048]{1,0:T(8,128)(2,1)S(1)} %get-tuple-element.61.x, bf16[512,128]{1,0:T(8,128)(2,1)S(1)} %get-tuple-element.62.b, ...), custom_call_target="tpu_custom_call" | custom-call | flops 2147483648 | bytes 12582912 | tf_op jit(solution)/shard_map/mid/pallas_call | solution.py:450
  39.4 1.9 stack.40
  41.3 0.9 merge.2.mine
  43.4 0.8 copy-done.7
  44.7 8.3 %finish.2 = (bf16[128,1024]{1,0:T(8,128)(2,1)S(1)}, bf16[128,1024]{1,0:T(8,128)(2,1)S(1)}, f32[128,1024]{1,0:T(8,128)S(1)}, f32[128,1024]{1,0:T(8,128)S(1)}, f32...) custom-call(s32[7]{0:T(128)S(1)} %stack.37.info, bf16[512,1024]{1,0:T(8,128)(2,1)S(1)} %copy-done.1, ...), custom_call_target="tpu_custom_call" | custom-call | flops 2147483648 | bytes 16777216 | tf_op jit(solution)/shard_map/finish/pallas_call | solution.py:540
  54.5 1.3 collective-permute-start.13
  55.8 1.3 collective-permute-start.16
  57.1 26.9 %collective-permute-done.13 = bf16[128,1024]{1,0:T(8,128)(2,1)S(1)} collective-permute-done((bf16[128,1024]{1,0:T(8,128)(2,1)S(1)}, bf16[128,1024]{1,0:T(8,128)(2,1)S(1)}, u32[]{:S(2)}, u32[]{:S(2)}) %collective-permute-start.13) | collective-permute-done | bytes 262176 | tf_op jit(solution)/shard_map/ppermute | solution.py:884
  84.1 1.9 collective-permute-start.14
  86.0 4.2 %collective-permute-done.16 = bf16[128,1024]{1,0:T(8,128)(2,1)S(1)} collective-permute-done((bf16[128,1024]{1,0:T(8,128)(2,1)S(1)}, bf16[128,1024]{1,0:T(8,128)(2,1)S(1)}, u32[]{:S(2)}, u32[]{:S(2)}) %collective-permute-start.16) | collective-permute-done | bytes 262176 | tf_op jit(solution)/shard_map/ppermute | solution.py:884
  90.3 1.9 collective-permute-start.17
  92.2 3.6 %collective-permute-done.14 = bf16[128,1024]{1,0:T(8,128)(2,1)S(1)} collective-permute-done((bf16[128,1024]{1,0:T(8,128)(2,1)S(1)}, bf16[128,1024]{1,0:T(8,128)(2,1)S(1)}, u32[]{:S(2)}, u32[]{:S(2)}) %collective-permute-start.14) | collective-permute-done | bytes 262176 | tf_op jit(solution)/shard_map/ppermute | solution.py:884
  95.8 1.3 collective-permute-start.19
  97.1 3.8 %collective-permute-done.17 = bf16[128,1024]{1,0:T(8,128)(2,1)S(1)} collective-permute-done((bf16[128,1024]{1,0:T(8,128)(2,1)S(1)}, bf16[128,1024]{1,0:T(8,128)(2,1)S(1)}, u32[]{:S(2)}, u32[]{:S(2)}) %collective-permute-start.17) | collective-permute-done | bytes 262176 | tf_op jit(solution)/shard_map/ppermute | solution.py:884
  100.9 1.3 collective-permute-start.18
  102.3 5.5 %collective-permute-done.18 = bf16[128,1024]{1,0:T(8,128)(2,1)S(1)} collective-permute-done((bf16[128,1024]{1,0:T(8,128)(2,1)S(1)}, bf16[128,1024]{1,0:T(8,128)(2,1)S(1)}, u32[]{:S(2)}, u32[]{:S(2)}) %collective-permute-start.18) | collective-permute-done | bytes 262176 | tf_op jit(solution)/shard_map/ppermute | solution.py:884
  107.8 2.1 %collective-permute-start.20 = (bf16[16,1024]{1,0:T(8,128)(2,1)S(1)}, bf16[16,1024]{1,0:T(8,128)(2,1)S(1)}, u32[]{:S(2)}, u32[]{:S(2)}) collective-permute-start(bf16[16,1024]{1,0:T(8,128)(2,1)S(1)} %slice_select_fusion), channel_id=1, source_target_pairs={{2,6},{6,10},{10,14},{14,18},{18,22},{22,26},{26,30},{7,3},{11,7},... | collective-permute-start | bytes 98312 | tf_op jit(solution)/shard_map/ppermute | solution.py:798
  110.0 3.9 %collective-permute-done.20.halo = bf16[16,1024]{1,0:T(8,128)(2,1)S(1)} collective-permute-done((bf16[16,1024]{1,0:T(8,128)(2,1)S(1)}, bf16[16,1024]{1,0:T(8,128)(2,1)S(1)}, u32[]{:S(2)}, u32[]{:S(2)}) %collective-permute-start.20) | collective-permute-done | bytes 32800 | tf_op jit(solution)/shard_map/ppermute | solution.py:798
  113.9 13.1 %prep.3 = (bf16[512,1024]{1,0:T(8,128)(2,1)S(1)}, bf16[512,2048]{1,0:T(8,128)(2,1)S(1)}, bf16[512,128]{1,0:T(8,128)(2,1)S(1)}, bf16[512,128]{1,0:T(8,128)(2,1)S(...) custom-call(s32[7]{0:T(128)S(1)} %stack.37.info, ...), custom_call_target="tpu_custom_call" | custom-call | flops 2147483648 | bytes 12582912 | tf_op jit(solution)/shard_map/prep/pallas_call | solution.py:421
  127.0 1.9 collective-permute-start.21
  129.0 2.0 %collective-permute-done.21.partner = bf16[144,2048]{1,0:T(8,128)(2,1)S(1)} collective-permute-done((bf16[144,2048]{1,0:T(8,128)(2,1)S(1)}, bf16[144,2048]{1,0:T(8,128)(2,1)S(1)}, u32[]{:S(2)}, u32[]{:S(2)}) %collective-permute-start.21) | collective-permute-done | bytes 589856 | tf_op jit(solution)/shard_map/ppermute | solution.py:719
  131.6 2.7 %collective-permute-start.22 = (bf16[144,1024]{1,0:T(8,128)(2,1)S(1)}, bf16[144,1024]{1,0:T(8,128)(2,1)S(1)}, u32[]{:S(2)}, u32[]{:S(2)}) collective-permute-start(bf16[144,1024]{1,0:T(8,128)(2,1)S(1)} %pair.3.refs_0_), channel_id=1, source_target_pairs={{2,10},{6,14},{18,26},{22,30},{11,3},{15,7},{27,19},{31,23}} | collective-permute-start | bytes 884744 | tf_op jit(solution)/shard_map/ppermute | solution.py:728
  134.3 1.3 collective-permute-start.23
  135.6 1.3 collective-permute-start.24
  136.9 6.7 %mid.3 = (f32[512,2048]{1,0:T(8,128)S(1)}, bf16[512,2048]{1,0:T(8,128)(2,1)S(1)}) custom-call(bf16[512,1024]{1,0:T(8,128)(2,1)S(1)} %get-tuple-element.89.normed, bf16[1,1024,4096]{2,1,0:T(8,128)(2,1)} %gate_weight.3, bf16[512,2048]{1,0:T(8,128)(2,1)S(1)} %get-tuple-element.90.x, bf16[512,128]{1,0:T(8,128)(2,1)S(1)} %get-tuple-element.91.b, ...), custom_call_target="tpu_custom_call" | custom-call | flops 2147483648 | bytes 12582912 | tf_op jit(solution)/shard_map/mid/pallas_call | solution.py:450
  143.6 7.7 %collective-permute-done.23.refs_2_ = bf16[144,1024]{1,0:T(8,128)(2,1)S(1)} collective-permute-done((bf16[144,1024]{1,0:T(8,128)(2,1)S(1)}, bf16[144,1024]{1,0:T(8,128)(2,1)S(1)}, u32[]{:S(2)}, u32[]{:S(2)}) %collective-permute-start.23) | collective-permute-done | bytes 294944 | tf_op jit(solution)/shard_map/ppermute | solution.py:728
  151.3 0.9 merge.3.mine
  152.3 1.9 collective-permute-start.25
  154.2 1.5 collective-permute-done.25.other
  155.7 8.3 %finish.3 = (bf16[128,1024]{1,0:T(8,128)(2,1)S(1)}, bf16[128,1024]{1,0:T(8,128)(2,1)S(1)}, bf16[128,1024]{1,0:T(8,128)(2,1)S(1)}, bf16[128,1024]{1,0:T(8,128)(2,1)S(1)}, f32[512,1024]{1,0:T(8,128)S(1)}) custom-call(s32[7]{0:T(128)S(1)} %stack.37.info, bf16[512,1024]{1,0:T(8,128)(2,1)S(1)} %pad_maximum_fusion.rows, f32[512,2048]{1,0:T(8,128)S(1)} %get-tuple-element.95.y, ...), custom_call_target="tpu_custom_call" | custom-call | flops 2147483648 | bytes 16777216 | tf_op jit(solution)/shard_map/finish/pallas_call | solution.py:540
  164.0 1.9 collective-permute-start.29
  165.9 3.9 %collective-permute-start.28 = (bf16[128,1024]{1,0:T(8,128)(2,1)S(1)}, bf16[128,1024]{1,0:T(8,128)(2,1)S(1)}, u32[]{:S(2)}, u32[]{:S(2)}) collective-permute-start(bf16[128,1024]{1,0:T(8,128)(2,1)S(1)} %get-tuple-element.103.sent), channel_id=1, source_target_pairs={{2,3},{3,2},{1,0},{6,7},{7,6},{5,4},{10,11},{11,10},{9,8},{14,15},... | collective-permute-start | bytes 786440 | tf_op jit(solution)/shard_map/ppermute | solution.py:897
  169.8 1.9 collective-permute-start.27
  171.8 3.9 %collective-permute-start.26 = (bf16[128,1024]{1,0:T(8,128)(2,1)S(1)}, bf16[128,1024]{1,0:T(8,128)(2,1)S(1)}, u32[]{:S(2)}, u32[]{:S(2)}) collective-permute-start(bf16[128,1024]{1,0:T(8,128)(2,1)S(1)} %get-tuple-element.101.sent), channel_id=1, source_target_pairs={{2,3},{3,2},{1,0},{6,7},{7,6},{5,4},{10,11},{11,10},{9,8},{14,15},... | collective-permute-start | bytes 786440 | tf_op jit(solution)/shard_map/ppermute | solution.py:897
  175.7 1.3 settle.4.rest_0_
  177.0 3.6 %collective-permute-done.28.other = bf16[128,1024]{1,0:T(8,128)(2,1)S(1)} collective-permute-done((bf16[128,1024]{1,0:T(8,128)(2,1)S(1)}, bf16[128,1024]{1,0:T(8,128)(2,1)S(1)}, u32[]{:S(2)}, u32[]{:S(2)}) %collective-permute-start.28) | collective-permute-done | bytes 262176 | tf_op jit(solution)/shard_map/ppermute | solution.py:897
  180.6 1.3 settle.5.rest_0_
  181.9 4.3 %collective-permute-done.27.other = bf16[128,1024]{1,0:T(8,128)(2,1)S(1)} collective-permute-done((bf16[128,1024]{1,0:T(8,128)(2,1)S(1)}, bf16[128,1024]{1,0:T(8,128)(2,1)S(1)}, u32[]{:S(2)}, u32[]{:S(2)}) %collective-permute-start.27) | collective-permute-done | bytes 262176 | tf_op jit(solution)/shard_map/ppermute | solution.py:897
  186.3 1.3 settle.6.rest_0_
  187.6 3.5 %collective-permute-done.26.other = bf16[128,1024]{1,0:T(8,128)(2,1)S(1)} collective-permute-done((bf16[128,1024]{1,0:T(8,128)(2,1)S(1)}, bf16[128,1024]{1,0:T(8,128)(2,1)S(1)}, u32[]{:S(2)}, u32[]{:S(2)}) %collective-permute-start.26) | collective-permute-done | bytes 262176 | tf_op jit(solution)/shard_map/ppermute | solution.py:897
  191.0 1.3 settle.7
  (54 shorter events, 10.0 us)
Async XLA Ops:
  0.8 0.7 collective-permute-start
  1.5 16.5 %collective-permute-start.1 = (bf16[256,1024]{1,0:T(8,128)(2,1)}, bf16[256,1024]{1,0:T(8,128)(2,1)S(1)}, u32[]{:S(2)}, u32[]{:S(2)}) collective-permute-start(bf16[256,1024]{1,0:T(8,128)(2,1)} %bitcast.9), channel_id=1, source_target_pairs={{0,8},{4,12},{8,0},{12,4},{16,24},{20,28},{24,16},{28,20},{1,9},{5... | collective-permute-start | bytes 1572872 | tf_op jit(solution)/shard_map/ppermute | solution.py:593
  3.0 15.0 %collective-permute-start.2 = (bf16[256,1024]{1,0:T(8,128)(2,1)}, bf16[256,1024]{1,0:T(8,128)(2,1)S(1)}, u32[]{:S(2)}, u32[]{:S(2)}) collective-permute-start(bf16[256,1024]{1,0:T(8,128)(2,1)} %bitcast.10), channel_id=1, source_target_pairs={{0,16},{4,20},{8,24},{12,28},{16,0},{20,4},{24,8},{28,12},{1,17},{... | collective-permute-start | bytes 1572872 | tf_op jit(solution)/shard_map/ppermute | solution.py:593
  3.6 1.2 copy-start
  18.0 1.4 copy-start.2
  18.0 1.4 copy-start.3
  18.0 0.7 collective-permute-start.3
  22.3 21.1 %collective-permute-start.10 = (bf16[768,1024]{1,0:T(8,128)(2,1)}, bf16[768,1024]{1,0:T(8,128)(2,1)S(1)}, u32[]{:S(2)}, u32[]{:S(2)}) collective-permute-start(bf16[768,1024]{1,0:T(8,128)(2,1)} %get-tuple-element.80), channel_id=1, source_target_pairs={{0,4},{4,0},{8,12},{12,8},{16,20},{20,16},{24,28},{28,24},{1,5},{5... | collective-permute-start | bytes 4718600 | tf_op jit(solution)/shard_map/ppermute | solution.py:593
  22.3 8.9 %collective-permute-start.8 = (bf16[128,1024]{1,0:T(8,128)(2,1)}, bf16[128,1024]{1,0:T(8,128)(2,1)S(1)}, u32[]{:S(2)}, u32[]{:S(2)}) collective-permute-start(bf16[128,1024]{1,0:T(8,128)(2,1)} %get-tuple-element.76), channel_id=1, source_target_pairs={{0,8},{4,12},{8,0},{12,4},{16,24},{20,28},{24,16},{28,20},{1,9},{5... | collective-permute-start | bytes 786440 | tf_op jit(solution)/shard_map/ppermute | solution.py:593
  22.8 15.8 %collective-permute-start.9 = (bf16[128,1024]{1,0:T(8,128)(2,1)}, bf16[128,1024]{1,0:T(8,128)(2,1)S(1)}, u32[]{:S(2)}, u32[]{:S(2)}) collective-permute-start(bf16[128,1024]{1,0:T(8,128)(2,1)} %get-tuple-element.77), channel_id=1, source_target_pairs={{0,16},{4,20},{8,24},{12,28},{16,0},{20,4},{24,8},{28,12},{1,17},{... | collective-permute-start | bytes 786440 | tf_op jit(solution)/shard_map/ppermute | solution.py:593
  24.4 16.9 %collective-permute-start.4 = (bf16[144,1024]{1,0:T(8,128)(2,1)S(1)}, bf16[144,1024]{1,0:T(8,128)(2,1)S(1)}, u32[]{:S(2)}, u32[]{:S(2)}) collective-permute-start(bf16[144,1024]{1,0:T(8,128)(2,1)S(1)} %pair.2.refs_0_), channel_id=1, source_target_pairs={{0,8},{4,12},{16,24},{20,28},{9,1},{13,5},{25,17},{29,21}} | collective-permute-start | bytes 884744 | tf_op jit(solution)/shard_map/ppermute | solution.py:728
  25.0 16.2 %collective-permute-start.5 = (bf16[144,1024]{1,0:T(8,128)(2,1)S(1)}, bf16[144,1024]{1,0:T(8,128)(2,1)S(1)}, u32[]{:S(2)}, u32[]{:S(2)}) collective-permute-start(bf16[144,1024]{1,0:T(8,128)(2,1)S(1)} %pair.2.refs_0_), channel_id=1, source_target_pairs={{0,16},{4,20},{8,24},{12,28},{17,1},{21,5},{25,9},{29,13}} | collective-permute-start | bytes 884744 | tf_op jit(solution)/shard_map/ppermute | solution.py:728
  31.2 7.4 %copy-start.5 = (bf16[128,1024]{1,0:T(8,128)(2,1)}, bf16[128,1024]{1,0:T(8,128)(2,1)S(1)}, u32[]{:S(2)}) copy-start(bf16[128,1024]{1,0:T(8,128)(2,1)S(1)} %collective-permute-done.8.refs_0_.rest_3_) | copy-start | bytes 786436
  31.2 10.0 %collective-permute-start.6 = (bf16[144,1024]{1,0:T(8,128)(2,1)S(1)}, bf16[144,1024]{1,0:T(8,128)(2,1)S(1)}, u32[]{:S(2)}, u32[]{:S(2)}) collective-permute-start(bf16[144,1024]{1,0:T(8,128)(2,1)S(1)} %pair.2.refs_0_), channel_id=1, source_target_pairs={{0,24},{4,28},{8,16},{12,20},{17,9},{21,13},{25,1},{29,5}} | collective-permute-start | bytes 884744 | tf_op jit(solution)/shard_map/ppermute | solution.py:728
  38.6 6.1 %copy-start.1 = (bf16[512,1024]{1,0:T(8,128)(2,1)S(1)}, bf16[512,1024]{1,0:T(8,128)(2,1)}, u32[]{:S(2)}) copy-start(bf16[512,1024]{1,0:T(8,128)(2,1)} %rows.3) | copy-start | bytes 3145732
  38.7 0.7 copy-start.6
  41.2 2.1 %collective-permute-start.11 = (bf16[256,1024]{1,0:T(8,128)(2,1)}, bf16[256,1024]{1,0:T(8,128)(2,1)S(1)}, u32[]{:S(2)}, u32[]{:S(2)}) collective-permute-start(bf16[256,1024]{1,0:T(8,128)(2,1)} %stack.40), channel_id=1, source_target_pairs={{0,4},{4,0},{8,12},{12,8},{16,20},{20,16},{24,28},{28,24},{1,5},{5... | collective-permute-start | bytes 1572872 | tf_op jit(solution)/shard_map/ppermute | solution.py:593
  42.2 0.7 collective-permute-start.7
  43.4 0.8 copy-start.7
  43.4 1.3 copy-start.4
  53.0 1.4 collective-permute-start.12
  53.7 2.1 %collective-permute-start.15 = (bf16[128,1024]{1,0:T(8,128)(2,1)S(1)}, bf16[128,1024]{1,0:T(8,128)(2,1)S(1)}, u32[]{:S(2)}, u32[]{:S(2)}) collective-permute-start(bf16[128,1024]{1,0:T(8,128)(2,1)S(1)} %get-tuple-element.86), channel_id=1, source_target_pairs={{0,1},{4,5},{8,9},{12,13},{16,17},{20,21},{24,25},{28,29}} | collective-permute-start | bytes 786440 | tf_op jit(solution)/shard_map/ppermute | solution.py:884
  54.5 29.6 %collective-permute-start.13 = (bf16[128,1024]{1,0:T(8,128)(2,1)S(1)}, bf16[128,1024]{1,0:T(8,128)(2,1)S(1)}, u32[]{:S(2)}, u32[]{:S(2)}) collective-permute-start(bf16[128,1024]{1,0:T(8,128)(2,1)S(1)} %add_convert_fusion.3.rest_7_), channel_id=1, source_target_pairs={{0,1},{1,2},{4,5},{5,6},{8,9},{9,10},{12,13},{13,14},{16,17},{17,1... | collective-permute-start | bytes 786440 | tf_op jit(solution)/shard_map/ppermute | solution.py:884
  55.8 34.4 %collective-permute-start.16 = (bf16[128,1024]{1,0:T(8,128)(2,1)S(1)}, bf16[128,1024]{1,0:T(8,128)(2,1)S(1)}, u32[]{:S(2)}, u32[]{:S(2)}) collective-permute-start(bf16[128,1024]{1,0:T(8,128)(2,1)S(1)} %add_convert_fusion.1.rest_10_), channel_id=1, source_target_pairs={{0,1},{1,2},{4,5},{5,6},{8,9},{9,10},{12,13},{13,14},{16,17},{17,1... | collective-permute-start | bytes 786440 | tf_op jit(solution)/shard_map/ppermute | solution.py:884
  84.1 11.7 %collective-permute-start.14 = (bf16[128,1024]{1,0:T(8,128)(2,1)S(1)}, bf16[128,1024]{1,0:T(8,128)(2,1)S(1)}, u32[]{:S(2)}, u32[]{:S(2)}) collective-permute-start(bf16[128,1024]{1,0:T(8,128)(2,1)S(1)} %add_convert_fusion.2.rest_9_), channel_id=1, source_target_pairs={{1,2},{2,3},{5,6},{6,7},{9,10},{10,11},{13,14},{14,15},{17,18},{18... | collective-permute-start | bytes 786440 | tf_op jit(solution)/shard_map/ppermute | solution.py:884
  90.3 10.6 %collective-permute-start.17 = (bf16[128,1024]{1,0:T(8,128)(2,1)S(1)}, bf16[128,1024]{1,0:T(8,128)(2,1)S(1)}, u32[]{:S(2)}, u32[]{:S(2)}) collective-permute-start(bf16[128,1024]{1,0:T(8,128)(2,1)S(1)} %add_convert_fusion.rest_8_), channel_id=1, source_target_pairs={{1,2},{2,3},{5,6},{6,7},{9,10},{10,11},{13,14},{14,15},{17,18},{18... | collective-permute-start | bytes 786440 | tf_op jit(solution)/shard_map/ppermute | solution.py:884
  95.8 6.4 %collective-permute-start.19 = (bf16[128,1024]{1,0:T(8,128)(2,1)S(1)}, bf16[128,1024]{1,0:T(8,128)(2,1)S(1)}, u32[]{:S(2)}, u32[]{:S(2)}) collective-permute-start(bf16[128,1024]{1,0:T(8,128)(2,1)S(1)} %collective-permute-done.14), channel_id=1, source_target_pairs={{2,3},{6,7},{10,11},{14,15},{18,19},{22,23},{26,27},{30,31}} | collective-permute-start | bytes 786440 | tf_op jit(solution)/shard_map/ppermute | solution.py:884
  100.9 6.8 %collective-permute-start.18 = (bf16[128,1024]{1,0:T(8,128)(2,1)S(1)}, bf16[128,1024]{1,0:T(8,128)(2,1)S(1)}, u32[]{:S(2)}, u32[]{:S(2)}) collective-permute-start(bf16[128,1024]{1,0:T(8,128)(2,1)S(1)} %collective-permute-done.17), channel_id=1, source_target_pairs={{2,3},{6,7},{10,11},{14,15},{18,19},{22,23},{26,27},{30,31}} | collective-permute-start | bytes 786440 | tf_op jit(solution)/shard_map/ppermute | solution.py:884
  107.8 6.1 %collective-permute-start.20 = (bf16[16,1024]{1,0:T(8,128)(2,1)S(1)}, bf16[16,1024]{1,0:T(8,128)(2,1)S(1)}, u32[]{:S(2)}, u32[]{:S(2)}) collective-permute-start(bf16[16,1024]{1,0:T(8,128)(2,1)S(1)} %slice_select_fusion), channel_id=1, source_target_pairs={{2,6},{6,10},{10,14},{14,18},{18,22},{22,26},{26,30},{7,3},{11,7},... | collective-permute-start | bytes 98312 | tf_op jit(solution)/shard_map/ppermute | solution.py:798
  127.0 3.9 %collective-permute-start.21 = (bf16[144,2048]{1,0:T(8,128)(2,1)S(1)}, bf16[144,2048]{1,0:T(8,128)(2,1)S(1)}, u32[]{:S(2)}, u32[]{:S(2)}) collective-permute-start(bf16[144,2048]{1,0:T(8,128)(2,1)S(1)} %get-tuple-element.88.mine), channel_id=1, source_target_pairs={{2,6},{6,2},{10,14},{14,10},{18,22},{22,18},{26,30},{30,26},{3,7},... | collective-permute-start | bytes 1769480 | tf_op jit(solution)/shard_map/ppermute | solution.py:719
  131.6 12.0 %collective-permute-start.22 = (bf16[144,1024]{1,0:T(8,128)(2,1)S(1)}, bf16[144,1024]{1,0:T(8,128)(2,1)S(1)}, u32[]{:S(2)}, u32[]{:S(2)}) collective-permute-start(bf16[144,1024]{1,0:T(8,128)(2,1)S(1)} %pair.3.refs_0_), channel_id=1, source_target_pairs={{2,10},{6,14},{18,26},{22,30},{11,3},{15,7},{27,19},{31,23}} | collective-permute-start | bytes 884744 | tf_op jit(solution)/shard_map/ppermute | solution.py:728
  134.3 17.0 %collective-permute-start.23 = (bf16[144,1024]{1,0:T(8,128)(2,1)S(1)}, bf16[144,1024]{1,0:T(8,128)(2,1)S(1)}, u32[]{:S(2)}, u32[]{:S(2)}) collective-permute-start(bf16[144,1024]{1,0:T(8,128)(2,1)S(1)} %pair.3.refs_0_), channel_id=1, source_target_pairs={{2,18},{6,22},{10,26},{14,30},{19,3},{23,7},{27,11},{31,15}} | collective-permute-start | bytes 884744 | tf_op jit(solution)/shard_map/ppermute | solution.py:728
  135.6 15.7 %collective-permute-start.24 = (bf16[144,1024]{1,0:T(8,128)(2,1)S(1)}, bf16[144,1024]{1,0:T(8,128)(2,1)S(1)}, u32[]{:S(2)}, u32[]{:S(2)}) collective-permute-start(bf16[144,1024]{1,0:T(8,128)(2,1)S(1)} %pair.3.refs_0_), channel_id=1, source_target_pairs={{2,26},{6,30},{10,18},{14,22},{19,11},{23,15},{27,3},{31,7}} | collective-permute-start | bytes 884744 | tf_op jit(solution)/shard_map/ppermute | solution.py:728
  152.3 3.4 %collective-permute-start.25 = (bf16[128,1024]{1,0:T(8,128)(2,1)S(1)}, bf16[128,1024]{1,0:T(8,128)(2,1)S(1)}, u32[]{:S(2)}, u32[]{:S(2)}) collective-permute-start(bf16[128,1024]{1,0:T(8,128)(2,1)S(1)} %merge.3.mine), channel_id=1, source_target_pairs={{2,6},{6,2},{10,14},{14,10},{18,22},{22,18},{26,30},{30,26},{3,7},... | collective-permute-start | bytes 786440 | tf_op jit(solution)/shard_map/ppermute | solution.py:719
  164.0 11.7 %collective-permute-start.29 = (bf16[128,1024]{1,0:T(8,128)(2,1)S(1)}, bf16[128,1024]{1,0:T(8,128)(2,1)S(1)}, u32[]{:S(2)}, u32[]{:S(2)}) collective-permute-start(bf16[128,1024]{1,0:T(8,128)(2,1)S(1)} %get-tuple-element.104.sent), channel_id=1, source_target_pairs={{2,3},{3,2},{1,0},{6,7},{7,6},{5,4},{10,11},{11,10},{9,8},{14,15},... | collective-permute-start | bytes 786440 | tf_op jit(solution)/shard_map/ppermute | solution.py:897
  165.9 14.7 %collective-permute-start.28 = (bf16[128,1024]{1,0:T(8,128)(2,1)S(1)}, bf16[128,1024]{1,0:T(8,128)(2,1)S(1)}, u32[]{:S(2)}, u32[]{:S(2)}) collective-permute-start(bf16[128,1024]{1,0:T(8,128)(2,1)S(1)} %get-tuple-element.103.sent), channel_id=1, source_target_pairs={{2,3},{3,2},{1,0},{6,7},{7,6},{5,4},{10,11},{11,10},{9,8},{14,15},... | collective-permute-start | bytes 786440 | tf_op jit(solution)/shard_map/ppermute | solution.py:897
  169.8 16.4 %collective-permute-start.27 = (bf16[128,1024]{1,0:T(8,128)(2,1)S(1)}, bf16[128,1024]{1,0:T(8,128)(2,1)S(1)}, u32[]{:S(2)}, u32[]{:S(2)}) collective-permute-start(bf16[128,1024]{1,0:T(8,128)(2,1)S(1)} %get-tuple-element.102.sent), channel_id=1, source_target_pairs={{2,3},{3,2},{1,0},{6,7},{7,6},{5,4},{10,11},{11,10},{9,8},{14,15},... | collective-permute-start | bytes 786440 | tf_op jit(solution)/shard_map/ppermute | solution.py:897
  171.8 19.3 %collective-permute-start.26 = (bf16[128,1024]{1,0:T(8,128)(2,1)S(1)}, bf16[128,1024]{1,0:T(8,128)(2,1)S(1)}, u32[]{:S(2)}, u32[]{:S(2)}) collective-permute-start(bf16[128,1024]{1,0:T(8,128)(2,1)S(1)} %get-tuple-element.101.sent), channel_id=1, source_target_pairs={{2,3},{3,2},{1,0},{6,7},{7,6},{5,4},{10,11},{11,10},{9,8},{14,15},... | collective-permute-start | bytes 786440 | tf_op jit(solution)/shard_map/ppermute | solution.py:897

commit v4 on v3

--- a/solution.py
+++ b/solution.py
@@ -12,7 +12,7 @@
 CHUNK = 128
 WIDTH = 512
 HALO = 16
-LIMIT = 36 * 2**20
+LIMIT = 28 * 2**20
 SMALL = 8 * 2**20
 SKEW = 2
 REVERSE, UPPER, FIRST, SEQ, RANKS = 0, 1, 2, 3, 4
@@ -228,135 +228,77 @@
             y_out[here, lanes] = within + skips[:, lanes] * values.astype(F32)
 
 
-def finish_kernel(
-    count,
-    plan,
-    shard_rows,
-    mode,
-    info,
-    rows,
-    y,
-    gate,
-    c_rows,
-    reach,
-    reach_tail,
-    local,
-    mine,
-    other,
-    partner,
-    gain,
-    spread,
-    *rest,
-):
-    far_pieces = rest[: len(plan)]
-    outs = rest[len(plan) : -4]
-    normed, entering, weight, arrived = rest[-4:]
-    step_index = pl.program_id(0)
-    steps = pl.num_programs(0)
+def finish_kernel(plan, shard_rows, members, place_slot, last, info, *refs):
+    count = len(members)
+    rows, y_all, gate_all, c_all, reach_all, local_all = refs[:6]
+    mine, other, partner, gain, spread = refs[6:11]
+    rest = refs[11:]
+    if plan:
+        far_pieces = rest[: len(plan)]
+        outs = rest[len(plan) : -4]
+        normed, entering, weight, arrived = rest[-4:]
+    else:
+        weight = rest[0]
+        outs = rest[1:-2]
+        normed, entering = rest[-2:]
     reverse = info[REVERSE]
-    size, inner = y.shape
-    parts = size // CHUNK
+    inner = weight.shape[0]
+    length = y_all.shape[0]
     state = mine.shape[0]
+    block = 256
     fetches = []
-    for piece, ranges in zip(far_pieces, plan):
-        for mask, source, offset, extent in ranges:
-            place = 0
-            if mask is not None:
-                place = pl.multiple_of((info[SEQ] ^ mask) * shard_rows + offset, 16)
-            fetches.append(
-                pltpu.make_async_copy(
-                    piece.at[source : source + extent],
-                    weight.at[pl.ds(place, extent)],
-                    arrived.at[len(fetches)],
-                )
-            )
-
-    @pl.when(step_index == 0)
-    def _():
-        for fetch in fetches:
-            fetch.start()
-        half = inner // 2
-        upper = info[UPPER] == 1
-        first = info[FIRST] == 1
-        for start in range(0, inner, 256):
-            lanes = slice(start, start + 256)
-            inside = slice(start % half, start % half + 256)
-            pair = (other, mine) if start < half else (mine, other)
-            full = jnp.where(upper, pair[0][:, inside], pair[1][:, inside])
-            tail = partner[state:, lanes].astype(F32)
-            through = tail[0:1] + tail[1:2]
-            moved = (through * full.astype(F32) + partner[:state, lanes].astype(F32)).astype(BF16)
-            entering[:, lanes] = jnp.where(first, full, moved)
-
-    position = jnp.where(reverse == 1, steps - 1 - step_index, step_index)
-    tail = dot(reach_tail[...], spread[...])
-    index_row = lax.broadcasted_iota(jnp.int32, (HALO, 1), 0)
-    turn = order_matrix(size, reverse)
-    block = 256
-    befores = [
-        jnp.sum(jnp.where(index_row == position * parts + p, tail, 0.0), axis=0, keepdims=True)
-        for p in range(parts)
-    ]
-    squares = [jnp.zeros((CHUNK, 1), F32) for _ in range(parts)]
-    gated = {}
+    if plan:
+        fetches = piece_copies(plan, shard_rows, info, far_pieces, weight, arrived, 0)
+    for fetch in fetches:
+        fetch.start()
+    half = inner // 2
+    upper = info[UPPER] == 1
+    first = info[FIRST] == 1
     for start in range(0, inner, block):
         lanes = slice(start, start + block)
-        for p in range(parts):
-            here = slice(p * CHUNK, (p + 1) * CHUNK)
-            full = local[p, :, lanes].astype(F32) + befores[p][:, lanes] * entering[:, lanes].astype(F32)
-            carried = dot(c_rows[here, :], full.astype(BF16)) * dot(reach[here, :], spread[:, lanes])
-            part = (y[here, lanes] + carried) * silu(gate[here, lanes].astype(F32))
-            squares[p] = squares[p] + jnp.sum(part * part, axis=-1, keepdims=True)
-            gated[p, start] = part
-    inverse_rms = [lax.rsqrt(total * (1.0 / inner) + EPSILON) for total in squares]
-    for start in range(0, inner, block):
-        lanes = slice(start, start + block)
-        piece = jnp.concatenate(
-            [(gated[p, start] * inverse_rms[p] * gain[:, lanes]).astype(BF16) for p in range(parts)],
-            axis=0,
-        )
-        piece = dot(turn, piece).astype(BF16)
-        normed[:, lanes] = piece
-
-    @pl.when(step_index == 0)
-    def _():
-        for fetch in fetches:
-            fetch.wait()
-
+        inside = slice(start % half, start % half + block)
+        pair = (other, mine) if start < half else (mine, other)
+        full = jnp.where(upper, pair[0][:, inside], pair[1][:, inside])
+        tail = partner[state:, lanes].astype(F32)
+        through = tail[0:1] + tail[1:2]
+        moved = (through * full.astype(F32) + partner[:state, lanes].astype(F32)).astype(BF16)
+        entering[:, lanes] = jnp.where(first, full, moved)
+    tail = dot(reach_all[length:, :], spread[...])
+    index_row = lax.broadcasted_iota(jnp.int32, (HALO, 1), 0)
+    turn = order_matrix(CHUNK, reverse)
+    for i, member in enumerate(members):
+        position = jnp.where(reverse == 1, length // CHUNK - 1 - member, member)
+        here = pl.ds(pl.multiple_of(position * CHUNK, CHUNK), CHUNK)
+        c_rows, reach, local = c_all[here, :], reach_all[here, :], local_all.at[position]
+        before = jnp.sum(jnp.where(index_row == position, tail, 0.0), axis=0, keepdims=True)
+        squares = jnp.zeros((CHUNK, 1), F32)
+        gated = []
+        for start in range(0, inner, block):
+            lanes = slice(start, start + block)
+            full = local[:, lanes].astype(F32) + before[:, lanes] * entering[:, lanes].astype(F32)
+            carried = dot(c_rows, full.astype(BF16)) * dot(reach, spread[:, lanes])
+            part = (y_all[here, lanes] + carried) * silu(gate_all[here, lanes].astype(F32))
+            squares = squares + jnp.sum(part * part, axis=-1, keepdims=True)
+            gated.append(part)
+        inverse_rms = lax.rsqrt(squares * (1.0 / inner) + EPSILON)
+        for index, start in enumerate(range(0, inner, block)):
+            lanes = slice(start, start + block)
+            piece = (gated[index] * inverse_rms * gain[:, lanes]).astype(BF16)
+            normed[i * CHUNK : (i + 1) * CHUNK, lanes] = dot(turn, piece).astype(BF16)
+    for fetch in fetches:
+        fetch.wait()
     total = dot(normed[...], weight[...])
-    base = rows[...].astype(F32) + total
-    if mode[0] == "exchange":
-        earlier = outs[:count]
-        sent = outs[count : 2 * count]
-        outs[2 * count][...] = base
-        for k in range(count):
-
-            @pl.when(step_index == k // parts)
-            def _(k=k):
-                start = k % parts * CHUNK
-                mine_now = total[start : start + CHUNK].astype(BF16)
-                sent[k][...] = jnp.where(info[mode[1]] == 1, earlier[k][...], mine_now)
-
-        return
-    order, skew, place_slot = mode
     place = info[place_slot]
-
-    @pl.when(step_index == 0)
-    def _():
-        for out in outs:
-            out[...] = jnp.zeros_like(out)
-
-    for k, index in enumerate(order):
-        start = index % parts * CHUNK
-        here = slice(start, start + CHUNK)
-
-        @pl.when((step_index == index // parts) & (place == 0))
-        def _(k=k, here=here):
-            outs[k][...] = total[here].astype(outs[k].dtype)
-
-        @pl.when((step_index == index // parts) & (place == 1))
-        def _(k=k, here=here):
-            outs[k + skew][...] = base[here]
+    for i in range(count):
+        term = total[i * CHUNK : (i + 1) * CHUNK]
+        base = rows[members[i] * CHUNK : (members[i] + 1) * CHUNK].astype(F32) + term
+        if last:
+            earlier, sent, base_out = outs[i], outs[count + i], outs[2 * count + i]
+            sent[...] = jnp.where(place == 1, earlier[...], term.astype(BF16))
+            base_out[...] = base
+        else:
+            outs[i][...] = jnp.where(place == 0, term, 0.0).astype(BF16)
+            outs[count + i][...] = jnp.where(place == 1, base, 0.0)
 
 
 def kept(shape, dtype):
@@ -367,6 +309,10 @@
     return tuple(pltpu.with_memory_space_constraint(v, pltpu.VMEM) for v in values)
 
 
+def near_one(value):
+    return near(value)[0]
+
+
 def far(value):
     return pltpu.with_memory_space_constraint(value, pltpu.HBM)
 
@@ -375,7 +321,7 @@
     return pl.BlockSpec(shape, lambda *_: (0,) * len(shape))
 
 
-def prep(info, rows, halo, gain, main, side, conv, bias, decay, spread, inner, state):
+def prep(info, rows, halo, gain, main, side, conv, bias, decay, spread, inner, state, resident=False):
     length, features = rows.shape
     heads = bias.shape[1]
     steps = inner // WIDTH
@@ -439,10 +385,10 @@
             flops=2 * length * features * inner, bytes_accessed=12 * 2**20, transcendentals=0
         ),
         name="prep",
-    )(info, rows, halo, far(gain), far(main), far(side), far(conv), far(conv), far(bias), far(decay), far(spread))
-
-
-def mid(normed, main, x, b, c_rows, cumulative, shifted, skip, spread, inner):
+    )(info, far(rows), halo, far(gain), (far, near_one)[resident](main), far(side), far(conv), far(conv), far(bias), far(decay), far(spread))
+
+
+def mid(normed, main, x, b, c_rows, cumulative, shifted, skip, spread, inner, resident=False):
     length, features = normed.shape
     state = b.shape[1]
     steps = inner // WIDTH
@@ -477,81 +423,103 @@
             flops=2 * length * features * inner, bytes_accessed=12 * 2**20, transcendentals=0
         ),
         name="mid",
-    )(*near(normed), far(main), *near(x, b, c_rows, cumulative, shifted), far(skip), far(spread))
-
-
-def finish(mode, info, rows, y, gate, c_rows, reach, local, state_parts, gain, spread, pieces, earlier):
+    )(*near(normed), (far, near_one)[resident](main), *near(x, b, c_rows, cumulative, shifted), far(skip), far(spread))
+
+
+def finish(
+    members, place_slot, last, info, rows, y, gate, c_rows, reach, local, state_parts,
+    gain, spread, pieces, earlier,
+):
     features = rows.shape[1]
     length, inner = y.shape
     state = c_rows.shape[1]
     mine, other, partner = state_parts
-    plan = [ranges for _, ranges in pieces]
+    resident = not isinstance(pieces, list)
+    plan = [] if resident else [ranges for _, ranges in pieces]
     shard_rows = inner // lax.axis_size("seq")
-    reach_width = reach.shape[1]
-    tail = length // HALO
-    size = 2 * CHUNK
-    steps = length // size
-    chunks = length // CHUNK
-
-    if mode[0] == "exchange":
-        out_specs = [whole_block((CHUNK, features))] * chunks
-        out_specs = out_specs + [pl.BlockSpec((size, features), lambda j, s: (j, 0))]
-        out_shape = [jax.ShapeDtypeStruct((CHUNK, features), BF16)] * chunks
-        out_shape = out_shape + [kept((length, features), F32)]
-    else:
-        skew = mode[1]
-        out_specs = [whole_block((CHUNK, features))] * (chunks + skew)
-        out_shape = [jax.ShapeDtypeStruct((CHUNK, features), BF16)] * skew
-        out_shape = out_shape + [kept((CHUNK, features), F32)] * chunks
-
-    def turned_block(shape):
-        def place(j, s):
-            return (jnp.where(s[0] == 1, steps - 1 - j, j),) + (0,) * (len(shape) - 1)
-
-        return pl.BlockSpec(shape, place)
-
-    grid_spec = pltpu.PrefetchScalarGridSpec(
-        num_scalar_prefetch=1,
-        grid=(steps,),
-        in_specs=[
-            pl.BlockSpec((size, features), lambda j, s: (j, 0)),
-            turned_block((size, inner)),
-            turned_block((size, inner)),
-            turned_block((size, state)),
-            turned_block((size, reach_width)),
-            pl.BlockSpec((HALO, reach_width), lambda j, s: (tail, 0)),
-            turned_block((size // CHUNK, state, inner)),
-            whole_block(mine.shape),
-            whole_block(other.shape),
-            whole_block(partner.shape),
-            whole_block((1, inner)),
-            whole_block(spread.shape),
-        ]
-        + [pl.BlockSpec(memory_space=pl.ANY)] * len(pieces)
-        + [whole_block(value.shape) for value in earlier],
-        out_specs=out_specs,
-        scratch_shapes=[
-            pltpu.VMEM((size, inner), BF16),
-            pltpu.VMEM((state, inner), BF16),
-            pltpu.VMEM((inner, features), BF16),
-            pltpu.SemaphoreType.DMA((sum(len(ranges) for ranges in plan),)),
-        ],
-    )
+    count = len(members)
+    whole = pl.BlockSpec(memory_space=pltpu.VMEM)
+    in_specs = [pl.BlockSpec(memory_space=pltpu.SMEM)]
+    in_specs += [whole] * 11
+    operands = [rows, *near(y, gate, c_rows, reach, local)]
+    in_specs += [whole] if resident else [pl.BlockSpec(memory_space=pl.ANY)] * len(pieces)
+    in_specs += [whole] * len(earlier)
+    operands += [mine, other, partner, far(gain), far(spread)]
+    operands += [*near(pieces)] if resident else [far(piece) for piece, _ in pieces]
+    operands += list(earlier)
+    scratch = [pltpu.VMEM((count * CHUNK, inner), BF16), pltpu.VMEM((state, inner), BF16)]
+    if not resident:
+        scratch.append(pltpu.VMEM((inner, features), BF16))
+        scratch.append(pltpu.SemaphoreType.DMA((sum(len(ranges) for ranges in plan),)))
+    shape = (CHUNK, features)
     return pl.pallas_call(
-        functools.partial(finish_kernel, chunks, plan, shard_rows, mode),
-        grid_spec=grid_spec,
-        out_shape=out_shape,
+        functools.partial(finish_kernel, plan, shard_rows, members, place_slot, last),
+        in_specs=in_specs,
+        out_specs=[whole] * (2 * count),
+        scratch_shapes=scratch,
+        out_shape=[jax.ShapeDtypeStruct(shape, BF16)] * count + [kept(shape, F32)] * count,
         compiler_params=pltpu.CompilerParams(
-            vmem_limit_bytes=LIMIT, dimension_semantics=("arbitrary",)
+            vmem_limit_bytes=LIMIT
         ),
         cost_estimate=pl.CostEstimate(
-            flops=2 * length * features * inner, bytes_accessed=16 * 2**20, transcendentals=0
+            flops=2 * count * CHUNK * features * inner, bytes_accessed=8 * 2**20, transcendentals=0
         ),
         name="finish",
-    )(
-        info, rows, *near(y, gate, c_rows, reach, reach, local), mine, other, partner,
-        far(gain), far(spread), *[far(piece) for piece, _ in pieces], *earlier,
-    )
+    )(info, *operands)
+
+
+def hold_kernel(plan, shard_rows, info, *refs):
+    main = refs[1]
+    far_pieces = refs[2 : 2 + len(plan)]
+    main_out, weight_out, arrived = refs[2 + len(plan) :]
+    parts = 4
+    rows = main.shape[1] // parts
+    copies = []
+    for i in range(parts):
+        here = pl.ds(i * rows, rows)
+        copies.append(
+            pltpu.make_async_copy(main.at[0, here], main_out.at[0, here], arrived.at[len(copies)])
+        )
+    copies += piece_copies(plan, shard_rows, info, far_pieces, weight_out, arrived, len(copies))
+    for copy in copies:
+        copy.start()
+    for copy in copies:
+        copy.wait()
+
+
+def hold(info, trigger, main, pieces, inner):
+    plan = [ranges for _, ranges in pieces]
+    features = main.shape[1]
+    anywhere = pl.BlockSpec(memory_space=pl.ANY)
+    whole = pl.BlockSpec(memory_space=pltpu.VMEM)
+    count = 4 + sum(len(ranges) for ranges in plan)
+    return pl.pallas_call(
+        functools.partial(hold_kernel, plan, inner // lax.axis_size("seq")),
+        in_specs=[pl.BlockSpec(memory_space=pltpu.SMEM)] + [anywhere] * (2 + len(pieces)),
+        out_specs=[whole, whole],
+        out_shape=[kept(main.shape, BF16), kept((inner, features), BF16)],
+        scratch_shapes=[pltpu.SemaphoreType.DMA((count,))],
+        compiler_params=pltpu.CompilerParams(vmem_limit_bytes=SMALL),
+        cost_estimate=pl.CostEstimate(flops=10**6, bytes_accessed=24 * 2**20, transcendentals=0),
+        name="hold",
+    )(info, far(trigger), far(main), *[far(piece) for piece, _ in pieces])
+
+
+def piece_copies(plan, shard_rows, info, far_pieces, weight, arrived, base):
+    copies = []
+    for piece, ranges in zip(far_pieces, plan):
+        for mask, source, offset, extent in ranges:
+            place = 0
+            if mask is not None:
+                place = pl.multiple_of((info[SEQ] ^ mask) * shard_rows + offset, 16)
+            copies.append(
+                pltpu.make_async_copy(
+                    piece.at[source : source + extent],
+                    weight.at[pl.ds(place, extent)],
+                    arrived.at[base + len(copies)],
+                )
+            )
+    return copies
 
 
 def stack_kernel(counts, *refs):
@@ -675,16 +643,16 @@
     rest[-1][...] = jnp.where(section == 0, other[...], rows)
 
 
-def settle(index, place, info, base, sent, other, finished):
-    length, features = base.shape
-    block = pl.BlockSpec((CHUNK, features), lambda j: (index, 0))
+def settle(index, chunks, place, info, base, sent, other, finished):
+    features = base.shape[1]
+    length = chunks * CHUNK
     out_block = pl.BlockSpec((None, CHUNK, features), lambda j: (0, index, 0))
     passed = [] if finished is None else [finished]
     return pl.pallas_call(
         functools.partial(settle_kernel, place),
         grid=(1,),
-        in_specs=[pl.BlockSpec(memory_space=pltpu.SMEM), block]
-        + [whole_block((CHUNK, features))] * 2
+        in_specs=[pl.BlockSpec(memory_space=pltpu.SMEM)]
+        + [whole_block((CHUNK, features))] * 3
         + [pl.BlockSpec(memory_space=pl.ANY)] * len(passed),
         out_specs=out_block,
         out_shape=jax.ShapeDtypeStruct((1, length, features), BF16),
@@ -787,18 +755,18 @@
     info = jnp.stack([fact.astype(jnp.int32) for fact in facts])
     order = [chunks - 1, 0] + list(range(1, chunks - 1))
 
-    def edges(first_rows, last_rows, sections):
+    def edges(first_rows, last_rows, first_wanted, sources, targets):
         pairs = []
-        for s in sections:
+        for source, target in zip(sources, targets):
             for i in range(seq_count):
-                target = i + 1 if s % 2 == 0 else i - 1
-                if 0 <= target < seq_count:
-                    pairs.append((i * section_count + s, target * section_count + s))
-        value = jnp.where(reverse == 1, first_rows, last_rows)
+                beside = i + 1 if target % 2 == 0 else i - 1
+                if 0 <= beside < seq_count:
+                    pairs.append((i * section_count + source, beside * section_count + target))
+        value = jnp.where(first_wanted, first_rows, last_rows)
         return lax.ppermute(value, ("seq", "section"), pairs)
 
     current = tokens
-    halo = edges(tokens[:HALO], tokens[length - HALO :], (0, 1))
+    halo = edges(tokens[:HALO], tokens[length - HALO :], reverse == 1, (0, 1), (0, 1))
     previous = None
     shards = None
     if seq_count == 8:
@@ -808,6 +776,7 @@
     else:
         whole = lax.all_gather(shard, "seq", axis=0, tiled=True)
         pieces = [(whole, [(None, 0, 0, inner)])]
+    main = main_weight
     for round_index in range(rounds):
         active = (2 * round_index, 2 * round_index + 1)
         normed, x, b, c_rows, cumulative, shifted, reach, local, packed = prep(
@@ -815,7 +784,7 @@
             current,
             halo,
             input_gain,
-            main_weight,
+            main,
             jnp.swapaxes(side_weight, 1, 2),
             conv_kernel,
             step_bias,
@@ -823,6 +792,7 @@
             spread,
             inner,
             state,
+            round_index > 0,
         )
         early = round_index == 0 and shards
         if early:
@@ -843,7 +813,10 @@
                 halves = [seq_swap(up, 2), seq_swap(down, 4)]
                 swapped = seq_swap(three, 1)
             ready, _ = lax.optimization_barrier((normed, total))
-            y, gate = mid(ready, main_weight, x, b, c_rows, cumulative, shifted, skip_gain, spread, inner)
+            y, gate = mid(
+                ready, main, x, b, c_rows, cumulative, shifted, skip_gain, spread, inner,
+                round_index > 0,
+            )
             if early:
                 *halves, _ = lax.optimization_barrier((*halves, y))
                 rows = halves[0].shape[0]
@@ -859,43 +832,54 @@
         last_round = round_index + 1 == rounds
         low, high = active
         place = section_index - low
-        mode = ("exchange", places) if last_round else (tuple(order), SKEW, places + round_index)
-        outs = finish(
-            mode, info, current, y, gate, c_rows, reach, local, state_parts,
-            output_gain, spread, pieces, previous if last_round else [],
-        )
+        terms = {}
+        bases = {}
+        for members in (order[: chunks // 2], order[chunks // 2 :]):
+            outs = finish(
+                tuple(members), places if last_round else places + round_index, last_round, info,
+                current, y, gate, c_rows, reach, local, state_parts, output_gain, spread, pieces,
+                [previous[member] for member in members] if last_round else [],
+            )
+            for i, member in enumerate(members):
+                terms[member] = outs[i]
+                bases[member] = outs[len(members) + i]
         if last_round:
-            *sent, base = outs
             break
-        hops = 3
         received = []
         values = []
-        for step in range(chunks + (hops - 1) * SKEW):
-            pairs = [
-                (low + hop, low + hop + 1) for hop in range(hops) if 0 <= step - hop * SKEW < chunks
-            ]
-            if step < SKEW:
-                value = outs[step]
-            elif step < len(outs):
-                value = (outs[step] + received[step - SKEW].astype(F32)).astype(BF16)
-            else:
-                value = received[step - SKEW]
+        direct = None
+        for step in range(chunks + 2 * SKEW - 1):
+            pairs = [(low + hop, low + hop + 1) for hop in range(3) if 0 <= step - hop * SKEW < chunks]
+            value = terms[order[step]] if step < chunks else None
+            if step >= SKEW:
+                passed = received[step - SKEW]
+                if step - SKEW < chunks:
+                    total = bases[order[step - SKEW]] + passed.astype(F32)
+                    total = total if value is None else total + value.astype(F32)
+                    passed = total.astype(BF16)
+                value = passed
             values.append(value)
             received.append(lax.ppermute(value, "section", pairs))
+            if step == chunks + SKEW - 1:
+                direct = lax.ppermute(value, "section", [(low + 1, low + 3)])
+        received.append(direct)
+        trigger, _ = lax.optimization_barrier((values[chunks + SKEW - 1], received[2 * SKEW]))
+        main, pieces = hold(info, trigger, main_weight, pieces, inner)
+        last_rows = jnp.where(place == 3, received[2 * SKEW], received[SKEW])[CHUNK - HALO :]
+        first_rows = jnp.where(place == 3, received[2 * SKEW + 1], received[SKEW + 1])[:HALO]
+        halo = edges(first_rows, last_rows, reverse == 1, (low + 2, high + 2), (low + 2, high + 2))
+        received[-1], received[-2], halo = lax.optimization_barrier((received[-1], received[-2], halo))
         layer_rows = [None] * chunks
         next_rows = [None] * chunks
         for step, index in enumerate(order):
             layer_rows[index] = values[step + SKEW]
             next_rows[index] = jnp.where(place == 3, received[step + 2 * SKEW], received[step + SKEW])
         previous = layer_rows
-        halo = edges(
-            next_rows[0][:HALO], next_rows[chunks - 1][CHUNK - HALO :], (low + 2, high + 2)
-        )
         current = jnp.concatenate(next_rows, axis=0)
     finished = None
-    for index in range(chunks):
-        other = lax.ppermute(sent[index], "section", [(low, high), (high, low), (1, 0)])
-        finished = settle(index, places, info, base, sent[index], other, finished)
+    for index in order:
+        other = lax.ppermute(terms[index], "section", [(low, high), (high, low), (1, 0)])
+        finished = settle(index, chunks, places, info, bases[index], terms[index], other, finished)
     return finished
 
 

time: 193 us -> 183 us (0.948)
  waiting for transfers between devices: 76.5 us -> 55.2 us
  Pallas kernels: 69.4 us -> 79 us
    ppermute x8 -> x7, waiting for transfers between devices: 43.9 us -> 32.1 us  [per_device(): received.append(lax.ppermute(value, 'section', pairs))]
    pallas_call x2 -> x5, Pallas kernels: 16.6 us -> 25.6 us  [the longest x4 20.4 us: finish(): pl.pallas_call(functools.partial(finish_kernel, plan, shard_rows, members...]
    ppermute x4 -> x5, waiting for transfers between devices: 11.4 us -> 7.3 us  [the longest x4 7.3 us: per_device(): lax.ppermute(terms[index], 'section', [(low, high), (high, low), (1, 0)])]
    ppermute x2, waiting for transfers between devices: 3.95 us -> 0.01 us  [edges(): return lax.ppermute(value, ('seq', 'section'), pairs)]
    ppermute x4, starting transfers between devices: 5.22 us -> 7.4 us  [swap(): return lax.ppermute(value, ('seq', 'section'), pairs)]
    ppermute x8 -> x7, starting transfers between devices: 10.4 us -> 9.25 us  [per_device(): received.append(lax.ppermute(value, 'section', pairs))]
    ppermute x4 -> x5, starting transfers between devices: 11.7 us -> 12.4 us  [the longest x4 11.7 us: per_device(): lax.ppermute(terms[index], 'section', [(low, high), (high, low), (1, 0)])]
  transfers between devices with their start and end apart: 30 -> 30, of which waited for: 14 -> 13; matrix products, arithmetic and copies ran while one was open for 0% -> 0% of each run, Pallas kernels for 17% -> 27%
where the time goes in v4:
time: 183 us; the launch traced here: 182 us
  Pallas kernels  79 us (43%)
  waiting for transfers between devices  55.2 us (30%)
  starting transfers between devices  42.5 us (23%)
  other arithmetic  2.27 us (1%)
  local copies, waits for them, and re-layouts  2.15 us (1%)
    ppermute x7, waiting for transfers between devices, per_device(): received.append(lax.ppermute(value, 'section', pairs))  32.1 us
    pallas_call x2, Pallas kernels, prep(): pl.pallas_call(prep_kernel, grid_spec=grid_spec, out_shape=[kept((length,...  26.9 us
    pallas_call x4, Pallas kernels, finish(): pl.pallas_call(functools.partial(finish_kernel, plan, shard_rows, members...  20.4 us
    pallas_call x2, Pallas kernels, mid(): pl.pallas_call(mid_kernel, grid=(steps,), in_specs=[whole_block((length,...  13.3 us
    ppermute x4, starting transfers between devices, per_device(): lax.ppermute(terms[index], 'section', [(low, high), (high, low), (1, 0)])  11.7 us
    ppermute x7, starting transfers between devices, per_device(): received.append(lax.ppermute(value, 'section', pairs))  9.25 us
    ppermute x4, starting transfers between devices, swap(): return lax.ppermute(value, ('seq', 'section'), pairs)  7.4 us
    ppermute x4, waiting for transfers between devices, per_device(): lax.ppermute(terms[index], 'section', [(low, high), (high, low), (1, 0)])  7.3 us
  transfers between devices with their start and end apart: 30, of which 13 were waited for; matrix products, arithmetic and copies ran while one was open for 0% of the time, Pallas kernels for 27%

profile of v4, /device:TPU:20, one launch (start us, length us, event | category | flops | bytes accessed | tf_op | source)
XLA Modules:
  0.0 181.7 jit_solution(8000262428598371804)
XLA Ops:
  2.0 1.5 collective-permute-start.1
  3.6 13.5 %prep.2 = (bf16[512,1024]{1,0:T(8,128)(2,1)S(1)}, bf16[512,2048]{1,0:T(8,128)(2,1)S(1)}, bf16[512,128]{1,0:T(8,128)(2,1)S(1)}, bf16[512,128]{1,0:T(8,128)(2,1)S(...) custom-call(s32[7]{0:T(128)S(1)} %stack.37.info, ...), custom_call_target="tpu_custom_call" | custom-call | flops 2147483648 | bytes 12582912 | tf_op jit(solution)/shard_map/prep/pallas_call | solution.py:367
  18.6 2.9 %stack.39 = (bf16[128,1024]{1,0:T(8,128)(2,1)}, bf16[128,1024]{1,0:T(8,128)(2,1)}, bf16[768,1024]{1,0:T(8,128)(2,1)}) custom-call(bf16[256,1024]{1,0:T(8,128)(2,1)} %copy-done.5, bf16[256,1024]{1,0:T(8,128)(2,1)} %copy-done.6, bf16[256,1024]{1,0:T(8,128)(2,1)} %bitcast.11, bf16[256,1024]{1,0:T(8,128)(2,1)} %copy-done.6, bf16[256,1024]{1,0:T(8,128)(2,1)} %copy-done.5), custom_call_target="tpu_custom_call" | custom-call | flops 1000000 | bytes 1000000 | tf_op jit(solution)/shard_map/stack/pallas_call | solution.py:547
  22.0 1.5 collective-permute-start.9
  24.9 5.5 %collective-permute-done.8.refs_0_.refs_14_.refs_5_ = bf16[128,1024]{1,0:T(8,128)(2,1)S(1)} collective-permute-done((bf16[128,1024]{1,0:T(8,128)(2,1)}, bf16[128,1024]{1,0:T(8,128)(2,1)S(1)}, u32[]{:S(2)}, u32[]{:S(2)}) %collective-permute-start.8) | collective-permute-done | bytes 262176 | tf_op jit(solution)/shard_map/ppermute | solution.py:561
  31.1 6.7 %mid.2 = (f32[512,2048]{1,0:T(8,128)S(1)}, bf16[512,2048]{1,0:T(8,128)(2,1)S(1)}) custom-call(bf16[512,1024]{1,0:T(8,128)(2,1)S(1)} %get-tuple-element.71.normed, bf16[1,1024,4096]{2,1,0:T(8,128)(2,1)} %refs_1_.1, bf16[512,2048]{1,0:T(8,128)(2,1)S(1)} %get-tuple-element.72.x, bf16[512,128]{1,0:T(8,128)(2,1)S(1)} %get-tuple-element.73.b, ...), custom_call_target="tpu_custom_call" | custom-call | flops 2147483648 | bytes 12582912 | tf_op jit(solution)/shard_map/mid/pallas_call | solution.py:396
  38.5 1.9 %stack.40 = bf16[256,1024]{1,0:T(8,128)(2,1)} custom-call(bf16[128,1024]{1,0:T(8,128)(2,1)} %copy-done.8, bf16[128,1024]{1,0:T(8,128)(2,1)} %copy-done.9), custom_call_target="tpu_custom_call" | custom-call | flops 1000000 | bytes 1000000 | tf_op jit(solution)/shard_map/stack/pallas_call | solution.py:547
  40.4 0.9 merge.2.refs_6_
  42.5 0.8 copy-done.7
  43.8 6.0 %finish.5 = (bf16[128,1024]{1,0:T(8,128)(2,1)S(1)}, bf16[128,1024]{1,0:T(8,128)(2,1)S(1)}, f32[128,1024]{1,0:T(8,128)S(1)}, f32[128,1024]{1,0:T(8,128)S(1)}) custom-call(s32[7]{0:T(128)S(1)} %stack.37.info, bf16[512,1024]{1,0:T(8,128)(2,1)S(1)} %copy-done.1, f32[512,2048]{1,0:T(8,128)S(1)} %get-tuple-element.77.refs_1_, ...), custom_call_target="tpu_custom_call" | custom-call | flops 1073741824 | bytes 8388608 | tf_op jit(solution)/shard_map/finish/pallas_call | solution.py:455
  50.5 0.9 collective-permute-start.12
  51.4 6.0 %finish.4 = (bf16[128,1024]{1,0:T(8,128)(2,1)S(1)}, bf16[128,1024]{1,0:T(8,128)(2,1)S(1)}, f32[128,1024]{1,0:T(8,128)S(1)}, f32[128,1024]{1,0:T(8,128)S(1)}) custom-call(s32[7]{0:T(128)S(1)} %stack.37.info, bf16[512,1024]{1,0:T(8,128)(2,1)S(1)} %copy-done.1, f32[512,2048]{1,0:T(8,128)S(1)} %get-tuple-element.77.refs_1_, ...), custom_call_target="tpu_custom_call" | custom-call | flops 1073741824 | bytes 8388608 | tf_op jit(solution)/shard_map/finish/pallas_call | solution.py:455
  57.6 1.3 collective-permute-start.17
  59.0 1.3 collective-permute-start.13
  60.3 20.5 %collective-permute-done.17 = bf16[128,1024]{1,0:T(8,128)(2,1)S(1)} collective-permute-done((bf16[128,1024]{1,0:T(8,128)(2,1)S(1)}, bf16[128,1024]{1,0:T(8,128)(2,1)S(1)}, u32[]{:S(2)}, u32[]{:S(2)}) %collective-permute-start.17) | collective-permute-done | bytes 262176 | tf_op jit(solution)/shard_map/ppermute | solution.py:862
  80.8 1.9 %collective-permute-start.18 = (bf16[128,1024]{1,0:T(8,128)(2,1)S(1)}, bf16[128,1024]{1,0:T(8,128)(2,1)S(1)}, u32[]{:S(2)}, u32[]{:S(2)}) collective-permute-start(bf16[128,1024]{1,0:T(8,128)(2,1)S(1)} %add_convert_fusion.refs_12_), channel_id=1, source_target_pairs={{1,2},{2,3},{5,6},{6,7},{9,10},{10,11},{13,14},{14,15},{17,18},{18... | collective-permute-start | bytes 786440 | tf_op jit(solution)/shard_map/ppermute | solution.py:862
  82.7 4.2 %collective-permute-done.13 = bf16[128,1024]{1,0:T(8,128)(2,1)S(1)} collective-permute-done((bf16[128,1024]{1,0:T(8,128)(2,1)S(1)}, bf16[128,1024]{1,0:T(8,128)(2,1)S(1)}, u32[]{:S(2)}, u32[]{:S(2)}) %collective-permute-start.13) | collective-permute-done | bytes 262176 | tf_op jit(solution)/shard_map/ppermute | solution.py:862
  87.0 1.9 %collective-permute-start.14 = (bf16[128,1024]{1,0:T(8,128)(2,1)S(1)}, bf16[128,1024]{1,0:T(8,128)(2,1)S(1)}, u32[]{:S(2)}, u32[]{:S(2)}) collective-permute-start(bf16[128,1024]{1,0:T(8,128)(2,1)S(1)} %add_convert_fusion.2.refs_0_.refs_13_), channel_id=1, source_target_pairs={{1,2},{2,3},{5,6},{6,7},{9,10},{10,11},{13,14},{14,15},{17,18},{18... | collective-permute-start | bytes 786440 | tf_op jit(solution)/shard_map/ppermute | solution.py:862
  89.7 2.9 %collective-permute-done.18 = bf16[128,1024]{1,0:T(8,128)(2,1)S(1)} collective-permute-done((bf16[128,1024]{1,0:T(8,128)(2,1)S(1)}, bf16[128,1024]{1,0:T(8,128)(2,1)S(1)}, u32[]{:S(2)}, u32[]{:S(2)}) %collective-permute-start.18) | collective-permute-done | bytes 262176 | tf_op jit(solution)/shard_map/ppermute | solution.py:862
  92.6 1.3 collective-permute-start.19
  93.9 4.5 %collective-permute-done.14 = bf16[128,1024]{1,0:T(8,128)(2,1)S(1)} collective-permute-done((bf16[128,1024]{1,0:T(8,128)(2,1)S(1)}, bf16[128,1024]{1,0:T(8,128)(2,1)S(1)}, u32[]{:S(2)}, u32[]{:S(2)}) %collective-permute-start.14) | collective-permute-done | bytes 262176 | tf_op jit(solution)/shard_map/ppermute | solution.py:862
  98.4 1.9 %collective-permute-start.20 = (bf16[16,1024]{1,0:T(8,128)(2,1)S(1)}, bf16[16,1024]{1,0:T(8,128)(2,1)S(1)}, u32[]{:S(2)}, u32[]{:S(2)}) collective-permute-start(bf16[16,1024]{1,0:T(8,128)(2,1)S(1)} %slice_select_fusion), channel_id=1, source_target_pairs={{2,6},{6,10},{10,14},{14,18},{18,22},{22,26},{26,30},{7,3},{11,7},... | collective-permute-start | bytes 98312 | tf_op jit(solution)/shard_map/ppermute | solution.py:766
  100.4 5.2 %hold.1 = (bf16[1,1024,4096]{2,1,0:T(8,128)(2,1)S(1)}, bf16[2048,1024]{1,0:T(8,128)(2,1)S(1)}) custom-call(s32[7]{0:T(128)S(1)} %stack.37.info, bf16[128,1024]{1,0:T(8,128)(2,1)} %copy-done.2, bf16[1,1024,4096]{2,1,0:T(8,128)(2,1)} %refs_1_.1, bf16[256,1024]{1,0:T(8,128)(2,1)} %bitcast.14, bf16[256,1024]{1,0:T(8,128)(2,1)} %copy-done.6, ...), custom_call_target="tpu_custom_call" | custom-call | flops 1000000 | bytes 25165824 | tf_op jit(solution)/shard_map/hold/pallas_call | solution.py:496
  105.7 1.0 pad_maximum_fusion.rows.refs_0_
  106.7 13.4 %prep.3 = (bf16[512,1024]{1,0:T(8,128)(2,1)S(1)}, bf16[512,2048]{1,0:T(8,128)(2,1)S(1)}, bf16[512,128]{1,0:T(8,128)(2,1)S(1)}, bf16[512,128]{1,0:T(8,128)(2,1)S(...) custom-call(s32[7]{0:T(128)S(1)} %stack.37.info, ...), custom_call_target="tpu_custom_call" | custom-call | flops 2147483648 | bytes 12582912 | tf_op jit(solution)/shard_map/prep/pallas_call | solution.py:367
  120.2 3.8 %collective-permute-start.21 = (bf16[144,2048]{1,0:T(8,128)(2,1)S(1)}, bf16[144,2048]{1,0:T(8,128)(2,1)S(1)}, u32[]{:S(2)}, u32[]{:S(2)}) collective-permute-start(bf16[144,2048]{1,0:T(8,128)(2,1)S(1)} %get-tuple-element.106.mine), channel_id=1, source_target_pairs={{2,6},{6,2},{10,14},{14,10},{18,22},{22,18},{26,30},{30,26},{3,7},... | collective-permute-start | bytes 1769480 | tf_op jit(solution)/shard_map/ppermute | solution.py:687
  124.0 1.6 collective-permute-done.21.partner.refs_8_
  126.3 1.3 collective-permute-start.24
  127.6 1.3 collective-permute-start.23
  128.9 2.2 %collective-permute-start.22 = (bf16[144,1024]{1,0:T(8,128)(2,1)S(1)}, bf16[144,1024]{1,0:T(8,128)(2,1)S(1)}, u32[]{:S(2)}, u32[]{:S(2)}) collective-permute-start(bf16[144,1024]{1,0:T(8,128)(2,1)S(1)} %pair.3.refs_0_), channel_id=1, source_target_pairs={{2,10},{6,14},{18,26},{22,30},{11,3},{15,7},{27,19},{31,23}} | collective-permute-start | bytes 884744 | tf_op jit(solution)/shard_map/ppermute | solution.py:696
  131.1 6.6 %mid.3 = (f32[512,2048]{1,0:T(8,128)S(1)}, bf16[512,2048]{1,0:T(8,128)(2,1)S(1)}) custom-call(bf16[512,1024]{1,0:T(8,128)(2,1)S(1)} %get-tuple-element.107.normed, bf16[1,1024,4096]{2,1,0:T(8,128)(2,1)S(1)} %get-tuple-element.104.wide.gate_weight, bf16[512,2048]{1,0:T(8,128)(2,1)S(1)} %get-tuple-element.108.x, bf16[512,128]{1,0:T(8,128)(2,1)S(1)} %get-tuple-element.109.b, ...), custom_call_target="tpu_custom_call" | custom-call | flops 2147483648 | bytes 12582912 | tf_op jit(solution)/shard_map/mid/pallas_call | solution.py:396
  137.7 0.8 collective-permute-done.24.refs_3_
  138.5 6.2 %collective-permute-done.23.refs_2_ = bf16[144,1024]{1,0:T(8,128)(2,1)S(1)} collective-permute-done((bf16[144,1024]{1,0:T(8,128)(2,1)S(1)}, bf16[144,1024]{1,0:T(8,128)(2,1)S(1)}, u32[]{:S(2)}, u32[]{:S(2)}) %collective-permute-start.23) | collective-permute-done | bytes 294944 | tf_op jit(solution)/shard_map/ppermute | solution.py:696
  144.7 0.9 merge.3.refs_6_
  145.7 2.2 %collective-permute-start.25 = (bf16[128,1024]{1,0:T(8,128)(2,1)S(1)}, bf16[128,1024]{1,0:T(8,128)(2,1)S(1)}, u32[]{:S(2)}, u32[]{:S(2)}) collective-permute-start(bf16[128,1024]{1,0:T(8,128)(2,1)S(1)} %merge.3.refs_6_), channel_id=1, source_target_pairs={{2,6},{6,2},{10,14},{14,10},{18,22},{22,18},{26,30},{30,26},{3,7},... | collective-permute-start | bytes 786440 | tf_op jit(solution)/shard_map/ppermute | solution.py:687
  147.9 1.2 collective-permute-done.25.refs_7_
  149.1 4.2 %finish.7 = (bf16[128,1024]{1,0:T(8,128)(2,1)S(1)}, bf16[128,1024]{1,0:T(8,128)(2,1)S(1)}, f32[128,1024]{1,0:T(8,128)S(1)}, f32[128,1024]{1,0:T(8,128)S(1)}) custom-call(s32[7]{0:T(128)S(1)} %stack.37.info, bf16[512,1024]{1,0:T(8,128)(2,1)S(1)} %copy-done, f32[512,2048]{1,0:T(8,128)S(1)} %get-tuple-element.113.refs_1_, ...), custom_call_target="tpu_custom_call" | custom-call | flops 1073741824 | bytes 8388608 | tf_op jit(solution)/shard_map/finish/pallas_call | solution.py:455
  153.3 1.9 %collective-permute-start.28 = (bf16[128,1024]{1,0:T(8,128)(2,1)S(1)}, bf16[128,1024]{1,0:T(8,128)(2,1)S(1)}, u32[]{:S(2)}, u32[]{:S(2)}) collective-permute-start(bf16[128,1024]{1,0:T(8,128)(2,1)S(1)} %get-tuple-element.124.sent), channel_id=1, source_target_pairs={{2,3},{3,2},{1,0},{6,7},{7,6},{5,4},{10,11},{11,10},{9,8},{14,15},... | collective-permute-start | bytes 786440 | tf_op jit(solution)/shard_map/ppermute | solution.py:881
  155.2 3.9 %collective-permute-start.29 = (bf16[128,1024]{1,0:T(8,128)(2,1)S(1)}, bf16[128,1024]{1,0:T(8,128)(2,1)S(1)}, u32[]{:S(2)}, u32[]{:S(2)}) collective-permute-start(bf16[128,1024]{1,0:T(8,128)(2,1)S(1)} %get-tuple-element.126.sent), channel_id=1, source_target_pairs={{2,3},{3,2},{1,0},{6,7},{7,6},{5,4},{10,11},{11,10},{9,8},{14,15},... | collective-permute-start | bytes 786440 | tf_op jit(solution)/shard_map/ppermute | solution.py:881
  159.2 4.1 %finish.6 = (bf16[128,1024]{1,0:T(8,128)(2,1)S(1)}, bf16[128,1024]{1,0:T(8,128)(2,1)S(1)}, f32[128,1024]{1,0:T(8,128)S(1)}, f32[128,1024]{1,0:T(8,128)S(1)}) custom-call(s32[7]{0:T(128)S(1)} %stack.37.info, bf16[512,1024]{1,0:T(8,128)(2,1)S(1)} %copy-done, f32[512,2048]{1,0:T(8,128)S(1)} %get-tuple-element.113.refs_1_, ...), custom_call_target="tpu_custom_call" | custom-call | flops 1073741824 | bytes 8388608 | tf_op jit(solution)/shard_map/finish/pallas_call | solution.py:455
  163.3 1.9 %collective-permute-start.27 = (bf16[128,1024]{1,0:T(8,128)(2,1)S(1)}, bf16[128,1024]{1,0:T(8,128)(2,1)S(1)}, u32[]{:S(2)}, u32[]{:S(2)}) collective-permute-start(bf16[128,1024]{1,0:T(8,128)(2,1)S(1)} %get-tuple-element.122.sent), channel_id=1, source_target_pairs={{2,3},{3,2},{1,0},{6,7},{7,6},{5,4},{10,11},{11,10},{9,8},{14,15},... | collective-permute-start | bytes 786440 | tf_op jit(solution)/shard_map/ppermute | solution.py:881
  165.2 3.9 %collective-permute-start.26 = (bf16[128,1024]{1,0:T(8,128)(2,1)S(1)}, bf16[128,1024]{1,0:T(8,128)(2,1)S(1)}, u32[]{:S(2)}, u32[]{:S(2)}) collective-permute-start(bf16[128,1024]{1,0:T(8,128)(2,1)S(1)} %get-tuple-element.120.sent), channel_id=1, source_target_pairs={{2,3},{3,2},{1,0},{6,7},{7,6},{5,4},{10,11},{11,10},{9,8},{14,15},... | collective-permute-start | bytes 786440 | tf_op jit(solution)/shard_map/ppermute | solution.py:881
  169.9 1.3 settle.4.rest_0_
  171.3 1.3 settle.5.rest_0_
  172.6 3.0 %collective-permute-done.27.other = bf16[128,1024]{1,0:T(8,128)(2,1)S(1)} collective-permute-done((bf16[128,1024]{1,0:T(8,128)(2,1)S(1)}, bf16[128,1024]{1,0:T(8,128)(2,1)S(1)}, u32[]{:S(2)}, u32[]{:S(2)}) %collective-permute-start.27) | collective-permute-done | bytes 262176 | tf_op jit(solution)/shard_map/ppermute | solution.py:881
  175.6 1.3 settle.6.rest_0_
  176.9 3.5 %collective-permute-done.26.other = bf16[128,1024]{1,0:T(8,128)(2,1)S(1)} collective-permute-done((bf16[128,1024]{1,0:T(8,128)(2,1)S(1)}, bf16[128,1024]{1,0:T(8,128)(2,1)S(1)}, u32[]{:S(2)}, u32[]{:S(2)}) %collective-permute-start.26) | collective-permute-done | bytes 262176 | tf_op jit(solution)/shard_map/ppermute | solution.py:881
  180.4 1.3 settle.7
  (62 shorter events, 11.7 us)
Async XLA Ops:
  0.8 0.7 collective-permute-start
  1.5 15.7 %collective-permute-start.2 = (bf16[256,1024]{1,0:T(8,128)(2,1)}, bf16[256,1024]{1,0:T(8,128)(2,1)S(1)}, u32[]{:S(2)}, u32[]{:S(2)}) collective-permute-start(bf16[256,1024]{1,0:T(8,128)(2,1)} %bitcast.9), channel_id=1, source_target_pairs={{0,16},{4,20},{8,24},{12,28},{16,0},{20,4},{24,8},{28,12},{1,17},{... | collective-permute-start | bytes 1572872 | tf_op jit(solution)/shard_map/ppermute | solution.py:561
  2.0 15.1 %collective-permute-start.1 = (bf16[256,1024]{1,0:T(8,128)(2,1)}, bf16[256,1024]{1,0:T(8,128)(2,1)S(1)}, u32[]{:S(2)}, u32[]{:S(2)}) collective-permute-start(bf16[256,1024]{1,0:T(8,128)(2,1)} %bitcast.10), channel_id=1, source_target_pairs={{0,8},{4,12},{8,0},{12,4},{16,24},{20,28},{24,16},{28,20},{1,9},{5... | collective-permute-start | bytes 1572872 | tf_op jit(solution)/shard_map/ppermute | solution.py:561
  17.1 1.4 copy-start.5
  17.1 1.4 copy-start.6
  17.1 0.7 collective-permute-start.3
  21.5 21.0 %collective-permute-start.10 = (bf16[768,1024]{1,0:T(8,128)(2,1)}, bf16[768,1024]{1,0:T(8,128)(2,1)S(1)}, u32[]{:S(2)}, u32[]{:S(2)}) collective-permute-start(bf16[768,1024]{1,0:T(8,128)(2,1)} %get-tuple-element.91), channel_id=1, source_target_pairs={{0,4},{4,0},{8,12},{12,8},{16,20},{20,16},{24,28},{28,24},{1,5},{5... | collective-permute-start | bytes 4718600 | tf_op jit(solution)/shard_map/ppermute | solution.py:561
  21.5 8.9 %collective-permute-start.8 = (bf16[128,1024]{1,0:T(8,128)(2,1)}, bf16[128,1024]{1,0:T(8,128)(2,1)S(1)}, u32[]{:S(2)}, u32[]{:S(2)}) collective-permute-start(bf16[128,1024]{1,0:T(8,128)(2,1)} %get-tuple-element.87), channel_id=1, source_target_pairs={{0,8},{4,12},{8,0},{12,4},{16,24},{20,28},{24,16},{28,20},{1,9},{5... | collective-permute-start | bytes 786440 | tf_op jit(solution)/shard_map/ppermute | solution.py:561
  22.0 15.8 %collective-permute-start.9 = (bf16[128,1024]{1,0:T(8,128)(2,1)}, bf16[128,1024]{1,0:T(8,128)(2,1)S(1)}, u32[]{:S(2)}, u32[]{:S(2)}) collective-permute-start(bf16[128,1024]{1,0:T(8,128)(2,1)} %get-tuple-element.88), channel_id=1, source_target_pairs={{0,16},{4,20},{8,24},{12,28},{16,0},{20,4},{24,8},{28,12},{1,17},{... | collective-permute-start | bytes 786440 | tf_op jit(solution)/shard_map/ppermute | solution.py:561
  23.5 16.9 %collective-permute-start.6 = (bf16[144,1024]{1,0:T(8,128)(2,1)S(1)}, bf16[144,1024]{1,0:T(8,128)(2,1)S(1)}, u32[]{:S(2)}, u32[]{:S(2)}) collective-permute-start(bf16[144,1024]{1,0:T(8,128)(2,1)S(1)} %pair.2.refs_0_), channel_id=1, source_target_pairs={{0,24},{4,28},{8,16},{12,20},{17,9},{21,13},{25,1},{29,5}} | collective-permute-start | bytes 884744 | tf_op jit(solution)/shard_map/ppermute | solution.py:696
  24.2 16.2 %collective-permute-start.5 = (bf16[144,1024]{1,0:T(8,128)(2,1)S(1)}, bf16[144,1024]{1,0:T(8,128)(2,1)S(1)}, u32[]{:S(2)}, u32[]{:S(2)}) collective-permute-start(bf16[144,1024]{1,0:T(8,128)(2,1)S(1)} %pair.2.refs_0_), channel_id=1, source_target_pairs={{0,16},{4,20},{8,24},{12,28},{17,1},{21,5},{25,9},{29,13}} | collective-permute-start | bytes 884744 | tf_op jit(solution)/shard_map/ppermute | solution.py:696
  30.4 7.4 %copy-start.8 = (bf16[128,1024]{1,0:T(8,128)(2,1)}, bf16[128,1024]{1,0:T(8,128)(2,1)S(1)}, u32[]{:S(2)}) copy-start(bf16[128,1024]{1,0:T(8,128)(2,1)S(1)} %collective-permute-done.8.refs_0_.refs_14_.refs_5_) | copy-start | bytes 786436
  30.4 10.0 %collective-permute-start.4 = (bf16[144,1024]{1,0:T(8,128)(2,1)S(1)}, bf16[144,1024]{1,0:T(8,128)(2,1)S(1)}, u32[]{:S(2)}, u32[]{:S(2)}) collective-permute-start(bf16[144,1024]{1,0:T(8,128)(2,1)S(1)} %pair.2.refs_0_), channel_id=1, source_target_pairs={{0,8},{4,12},{16,24},{20,28},{9,1},{13,5},{25,17},{29,21}} | collective-permute-start | bytes 884744 | tf_op jit(solution)/shard_map/ppermute | solution.py:696
  37.8 6.0 %copy-start.1 = (bf16[512,1024]{1,0:T(8,128)(2,1)S(1)}, bf16[512,1024]{1,0:T(8,128)(2,1)}, u32[]{:S(2)}) copy-start(bf16[512,1024]{1,0:T(8,128)(2,1)} %refs_0_.3) | copy-start | bytes 3145732
  37.8 0.7 copy-start.9
  40.4 2.1 %collective-permute-start.11 = (bf16[256,1024]{1,0:T(8,128)(2,1)}, bf16[256,1024]{1,0:T(8,128)(2,1)S(1)}, u32[]{:S(2)}, u32[]{:S(2)}) collective-permute-start(bf16[256,1024]{1,0:T(8,128)(2,1)} %stack.40), channel_id=1, source_target_pairs={{0,4},{4,0},{8,12},{12,8},{16,20},{20,16},{24,28},{28,24},{1,5},{5... | collective-permute-start | bytes 1572872 | tf_op jit(solution)/shard_map/ppermute | solution.py:561
  41.3 0.7 collective-permute-start.7
  42.5 0.8 copy-start.7
  42.5 1.3 copy-start.4
  49.9 7.6 %collective-permute-start.16 = (bf16[128,1024]{1,0:T(8,128)(2,1)S(1)}, bf16[128,1024]{1,0:T(8,128)(2,1)S(1)}, u32[]{:S(2)}, u32[]{:S(2)}) collective-permute-start(bf16[128,1024]{1,0:T(8,128)(2,1)S(1)} %get-tuple-element.98), channel_id=1, source_target_pairs={{0,1},{4,5},{8,9},{12,13},{16,17},{20,21},{24,25},{28,29}} | collective-permute-start | bytes 786440 | tf_op jit(solution)/shard_map/ppermute | solution.py:862
  50.5 8.3 %collective-permute-start.12 = (bf16[128,1024]{1,0:T(8,128)(2,1)S(1)}, bf16[128,1024]{1,0:T(8,128)(2,1)S(1)}, u32[]{:S(2)}, u32[]{:S(2)}) collective-permute-start(bf16[128,1024]{1,0:T(8,128)(2,1)S(1)} %get-tuple-element.94), channel_id=1, source_target_pairs={{0,1},{4,5},{8,9},{12,13},{16,17},{20,21},{24,25},{28,29}} | collective-permute-start | bytes 786440 | tf_op jit(solution)/shard_map/ppermute | solution.py:862
  57.6 23.2 %collective-permute-start.17 = (bf16[128,1024]{1,0:T(8,128)(2,1)S(1)}, bf16[128,1024]{1,0:T(8,128)(2,1)S(1)}, u32[]{:S(2)}, u32[]{:S(2)}) collective-permute-start(bf16[128,1024]{1,0:T(8,128)(2,1)S(1)} %add_convert_fusion.1.refs_12_), channel_id=1, source_target_pairs={{0,1},{1,2},{4,5},{5,6},{8,9},{9,10},{12,13},{13,14},{16,17},{17,1... | collective-permute-start | bytes 786440 | tf_op jit(solution)/shard_map/ppermute | solution.py:862
  59.0 28.0 %collective-permute-start.13 = (bf16[128,1024]{1,0:T(8,128)(2,1)S(1)}, bf16[128,1024]{1,0:T(8,128)(2,1)S(1)}, u32[]{:S(2)}, u32[]{:S(2)}) collective-permute-start(bf16[128,1024]{1,0:T(8,128)(2,1)S(1)} %add_convert_fusion.3.refs_13_), channel_id=1, source_target_pairs={{0,1},{1,2},{4,5},{5,6},{8,9},{9,10},{12,13},{13,14},{16,17},{17,1... | collective-permute-start | bytes 786440 | tf_op jit(solution)/shard_map/ppermute | solution.py:862
  80.8 11.8 %collective-permute-start.18 = (bf16[128,1024]{1,0:T(8,128)(2,1)S(1)}, bf16[128,1024]{1,0:T(8,128)(2,1)S(1)}, u32[]{:S(2)}, u32[]{:S(2)}) collective-permute-start(bf16[128,1024]{1,0:T(8,128)(2,1)S(1)} %add_convert_fusion.refs_12_), channel_id=1, source_target_pairs={{1,2},{2,3},{5,6},{6,7},{9,10},{10,11},{13,14},{14,15},{17,18},{18... | collective-permute-start | bytes 786440 | tf_op jit(solution)/shard_map/ppermute | solution.py:862
  87.0 13.3 %copy-start.2 = (bf16[128,1024]{1,0:T(8,128)(2,1)}, bf16[128,1024]{1,0:T(8,128)(2,1)S(1)}, u32[]{:S(2)}) copy-start(bf16[128,1024]{1,0:T(8,128)(2,1)S(1)} %add_convert_fusion.2.refs_0_.refs_13_) | copy-start | bytes 786436
  87.0 11.3 %collective-permute-start.14 = (bf16[128,1024]{1,0:T(8,128)(2,1)S(1)}, bf16[128,1024]{1,0:T(8,128)(2,1)S(1)}, u32[]{:S(2)}, u32[]{:S(2)}) collective-permute-start(bf16[128,1024]{1,0:T(8,128)(2,1)S(1)} %add_convert_fusion.2.refs_0_.refs_13_), channel_id=1, source_target_pairs={{1,2},{2,3},{5,6},{6,7},{9,10},{10,11},{13,14},{14,15},{17,18},{18... | collective-permute-start | bytes 786440 | tf_op jit(solution)/shard_map/ppermute | solution.py:862
  89.0 16.6 %collective-permute-start.15 = (bf16[128,1024]{1,0:T(8,128)(2,1)S(1)}, bf16[128,1024]{1,0:T(8,128)(2,1)S(1)}, u32[]{:S(2)}, u32[]{:S(2)}) collective-permute-start(bf16[128,1024]{1,0:T(8,128)(2,1)S(1)} %add_convert_fusion.2.refs_0_.refs_13_), channel_id=1, source_target_pairs={{1,3},{5,7},{9,11},{13,15},{17,19},{21,23},{25,27},{29,31}} | collective-permute-start | bytes 786440 | tf_op jit(solution)/shard_map/ppermute | solution.py:864
  92.6 13.0 %collective-permute-start.19 = (bf16[128,1024]{1,0:T(8,128)(2,1)S(1)}, bf16[128,1024]{1,0:T(8,128)(2,1)S(1)}, u32[]{:S(2)}, u32[]{:S(2)}) collective-permute-start(bf16[128,1024]{1,0:T(8,128)(2,1)S(1)} %collective-permute-done.18), channel_id=1, source_target_pairs={{2,3},{6,7},{10,11},{14,15},{18,19},{22,23},{26,27},{30,31}} | collective-permute-start | bytes 786440 | tf_op jit(solution)/shard_map/ppermute | solution.py:862
  98.4 7.2 %collective-permute-start.20 = (bf16[16,1024]{1,0:T(8,128)(2,1)S(1)}, bf16[16,1024]{1,0:T(8,128)(2,1)S(1)}, u32[]{:S(2)}, u32[]{:S(2)}) collective-permute-start(bf16[16,1024]{1,0:T(8,128)(2,1)S(1)} %slice_select_fusion), channel_id=1, source_target_pairs={{2,6},{6,10},{10,14},{14,18},{18,22},{22,26},{26,30},{7,3},{11,7},... | collective-permute-start | bytes 98312 | tf_op jit(solution)/shard_map/ppermute | solution.py:766
  120.2 5.5 %collective-permute-start.21 = (bf16[144,2048]{1,0:T(8,128)(2,1)S(1)}, bf16[144,2048]{1,0:T(8,128)(2,1)S(1)}, u32[]{:S(2)}, u32[]{:S(2)}) collective-permute-start(bf16[144,2048]{1,0:T(8,128)(2,1)S(1)} %get-tuple-element.106.mine), channel_id=1, source_target_pairs={{2,6},{6,2},{10,14},{14,10},{18,22},{22,18},{26,30},{30,26},{3,7},... | collective-permute-start | bytes 1769480 | tf_op jit(solution)/shard_map/ppermute | solution.py:687
  126.3 12.2 %collective-permute-start.24 = (bf16[144,1024]{1,0:T(8,128)(2,1)S(1)}, bf16[144,1024]{1,0:T(8,128)(2,1)S(1)}, u32[]{:S(2)}, u32[]{:S(2)}) collective-permute-start(bf16[144,1024]{1,0:T(8,128)(2,1)S(1)} %pair.3.refs_0_), channel_id=1, source_target_pairs={{2,26},{6,30},{10,18},{14,22},{19,11},{23,15},{27,3},{31,7}} | collective-permute-start | bytes 884744 | tf_op jit(solution)/shard_map/ppermute | solution.py:696
  127.6 17.1 %collective-permute-start.23 = (bf16[144,1024]{1,0:T(8,128)(2,1)S(1)}, bf16[144,1024]{1,0:T(8,128)(2,1)S(1)}, u32[]{:S(2)}, u32[]{:S(2)}) collective-permute-start(bf16[144,1024]{1,0:T(8,128)(2,1)S(1)} %pair.3.refs_0_), channel_id=1, source_target_pairs={{2,18},{6,22},{10,26},{14,30},{19,3},{23,7},{27,11},{31,15}} | collective-permute-start | bytes 884744 | tf_op jit(solution)/shard_map/ppermute | solution.py:696
  128.9 15.8 %collective-permute-start.22 = (bf16[144,1024]{1,0:T(8,128)(2,1)S(1)}, bf16[144,1024]{1,0:T(8,128)(2,1)S(1)}, u32[]{:S(2)}, u32[]{:S(2)}) collective-permute-start(bf16[144,1024]{1,0:T(8,128)(2,1)S(1)} %pair.3.refs_0_), channel_id=1, source_target_pairs={{2,10},{6,14},{18,26},{22,30},{11,3},{15,7},{27,19},{31,23}} | collective-permute-start | bytes 884744 | tf_op jit(solution)/shard_map/ppermute | solution.py:696
  137.7 11.4 %copy-start = (bf16[512,1024]{1,0:T(8,128)(2,1)S(1)}, bf16[512,1024]{1,0:T(8,128)(2,1)}, u32[]{:S(2)}) copy-start(bf16[512,1024]{1,0:T(8,128)(2,1)} %pad_maximum_fusion.rows.refs_0_) | copy-start | bytes 3145732
  145.7 3.4 %collective-permute-start.25 = (bf16[128,1024]{1,0:T(8,128)(2,1)S(1)}, bf16[128,1024]{1,0:T(8,128)(2,1)S(1)}, u32[]{:S(2)}, u32[]{:S(2)}) collective-permute-start(bf16[128,1024]{1,0:T(8,128)(2,1)S(1)} %merge.3.refs_6_), channel_id=1, source_target_pairs={{2,6},{6,2},{10,14},{14,10},{18,22},{22,18},{26,30},{30,26},{3,7},... | collective-permute-start | bytes 786440 | tf_op jit(solution)/shard_map/ppermute | solution.py:687
  149.1 10.0 %copy-start.3 = (bf16[128,1024]{1,0:T(8,128)(2,1)S(1)}, bf16[128,1024]{1,0:T(8,128)(2,1)}, u32[]{:S(2)}) copy-start(bf16[128,1024]{1,0:T(8,128)(2,1)} %copy-done.2) | copy-start | bytes 786436
  153.3 18.0 %collective-permute-start.28 = (bf16[128,1024]{1,0:T(8,128)(2,1)S(1)}, bf16[128,1024]{1,0:T(8,128)(2,1)S(1)}, u32[]{:S(2)}, u32[]{:S(2)}) collective-permute-start(bf16[128,1024]{1,0:T(8,128)(2,1)S(1)} %get-tuple-element.124.sent), channel_id=1, source_target_pairs={{2,3},{3,2},{1,0},{6,7},{7,6},{5,4},{10,11},{11,10},{9,8},{14,15},... | collective-permute-start | bytes 786440 | tf_op jit(solution)/shard_map/ppermute | solution.py:881
  155.2 14.7 %collective-permute-start.29 = (bf16[128,1024]{1,0:T(8,128)(2,1)S(1)}, bf16[128,1024]{1,0:T(8,128)(2,1)S(1)}, u32[]{:S(2)}, u32[]{:S(2)}) collective-permute-start(bf16[128,1024]{1,0:T(8,128)(2,1)S(1)} %get-tuple-element.126.sent), channel_id=1, source_target_pairs={{2,3},{3,2},{1,0},{6,7},{7,6},{5,4},{10,11},{11,10},{9,8},{14,15},... | collective-permute-start | bytes 786440 | tf_op jit(solution)/shard_map/ppermute | solution.py:881
  163.3 12.3 %collective-permute-start.27 = (bf16[128,1024]{1,0:T(8,128)(2,1)S(1)}, bf16[128,1024]{1,0:T(8,128)(2,1)S(1)}, u32[]{:S(2)}, u32[]{:S(2)}) collective-permute-start(bf16[128,1024]{1,0:T(8,128)(2,1)S(1)} %get-tuple-element.122.sent), channel_id=1, source_target_pairs={{2,3},{3,2},{1,0},{6,7},{7,6},{5,4},{10,11},{11,10},{9,8},{14,15},... | collective-permute-start | bytes 786440 | tf_op jit(solution)/shard_map/ppermute | solution.py:881
  165.2 15.1 %collective-permute-start.26 = (bf16[128,1024]{1,0:T(8,128)(2,1)S(1)}, bf16[128,1024]{1,0:T(8,128)(2,1)S(1)}, u32[]{:S(2)}, u32[]{:S(2)}) collective-permute-start(bf16[128,1024]{1,0:T(8,128)(2,1)S(1)} %get-tuple-element.120.sent), channel_id=1, source_target_pairs={{2,3},{3,2},{1,0},{6,7},{7,6},{5,4},{10,11},{11,10},{9,8},{14,15},... | collective-permute-start | bytes 786440 | tf_op jit(solution)/shard_map/ppermute | solution.py:881
